TPU v7x, 32 devices: a whole 2x2x4 slice. The times are simulated.
32 devices in a mesh: seq: 2 (over y), fsdp: 16 (over z, x, core).
Axes of the slice: x: 2, y: 2, z: 4, core: 2. Of those that a mesh axis runs over, the one named last changes fastest.
Arguments:
- tokens: bfloat16 [16, 512, 2048], P('fsdp', 'seq'), may hold values from -6 to 6
- bounds: int32 [4], replicated, may hold values from 1 to 2047, as said below
- norm_attn: bfloat16 [2048], P('fsdp'), may hold values from 0.099609375 to 1.8984375
- weight_qkv: bfloat16 [2048, 6144], P('fsdp'), may hold values from -0.125 to 0.125
- weight_out: bfloat16 [2048, 2048], P('fsdp'), may hold values from -2 to 2
- norm_ffn: bfloat16 [2048], P('fsdp'), may hold values from 0.099609375 to 1.8984375
- weight_gate: bfloat16 [2048, 5504], P('fsdp'), may hold values from -0.125 to 0.125
- weight_up: bfloat16 [2048, 5504], P('fsdp'), may hold values from -0.125 to 0.125
- weight_down: bfloat16 [5504, 2048], P('fsdp'), may hold values from -0.078125 to 0.078125
- cotangent: bfloat16 [16, 512, 2048], P('fsdp', 'seq'), may hold values from -6 to 6
Outputs:
- block_out: bfloat16 [16, 512, 2048], P('fsdp', 'seq')
- grad_tokens: float32 [16, 512, 2048], P('fsdp', 'seq')
- grad_norm_attn: float32 [2048], P('fsdp')
- grad_qkv: float32 [2048, 6144], P('fsdp')
- grad_out: float32 [2048, 2048], P('fsdp')
- grad_norm_ffn: float32 [2048], P('fsdp')
- grad_gate: float32 [2048, 5504], P('fsdp')
- grad_up: float32 [2048, 5504], P('fsdp')
- grad_down: float32 [5504, 2048], P('fsdp')
Inputs may be any that keep to these rules, and one draw needn't show every extreme that they name: Sequence i holds two documents, its tokens before position bounds[i] and those from it on; both ends of the range occur in every draw.
All inputs are finite; a program needn't handle non-finite values.
Results may differ from a plain program's by a relative error of at most 0.02.
Values may be sent and summed in bfloat16 or wider, within the bound.
No kernel may reach another device: no remote copies, remote signals or barrier semaphores. Data moves between devices by JAX's collectives and lax.ppermute only.
A program may use at most 576 MiB of HBM per device.

v0:
```python
import jax
import jax.numpy as jnp
from jax import lax
from jax.sharding import PartitionSpec as P

H = 16
HD = 128
WINDOW = 1024
MIN_LEN = 2048


EPS = 1e-05
NEG = -1e30
THETA = 10000.0
CONTRACT_LAST = (((1,), (1,)), ((), ()))
CONTRACT_FIRST = (((0,), (0,)), ((), ()))


def shifted(block, axis, distance):
    devices = range(lax.axis_size(axis))
    route = [(i - distance, i) for i in devices if i - distance in devices]
    return lax.ppermute(block, axis, route)


def rope_tables(positions, head_size):
    frequency = THETA ** (-jnp.arange(head_size // 2, dtype=jnp.float32) * 2.0 / head_size)
    angles = positions.astype(jnp.float32)[:, None] * frequency[None, :]
    return (jnp.cos(angles)[:, None, :], jnp.sin(angles)[:, None, :])


def rotate(vector, cosine, sine_table):
    half_size = vector.shape[-1] // 2
    front_half = vector[..., :half_size]
    back_half = vector[..., half_size:]
    return jnp.concatenate(
        [
            front_half * cosine - back_half * sine_table,
            back_half * cosine + front_half * sine_table,
        ],
        axis=-1,
    )


def unrotate(vector, cosine, sine_table):
    half_size = vector.shape[-1] // 2
    front_half = vector[..., :half_size]
    back_half = vector[..., half_size:]
    return jnp.concatenate(
        [
            front_half * cosine + back_half * sine_table,
            back_half * cosine - front_half * sine_table,
        ],
        axis=-1,
    )


def masked_scores(query_block, key_block, query_pos, key_pos, boundary):
    scale_factor = query_block.shape[-1] ** (-0.5)
    scores = (
        jnp.einsum("qhd,khd->hqk", query_block, key_block, preferred_element_type=jnp.float32)
        * scale_factor
    )
    behind = query_pos[:, None] - key_pos[None, :]
    same_doc = (query_pos[:, None] >= boundary) == (key_pos[None, :] >= boundary)
    allowed = (key_pos[None, :] >= 0) & (behind >= 0) & (behind < WINDOW) & same_doc
    return jnp.where(allowed[None], scores, NEG)


def attend(query_block, key_block, value_block, query_pos, key_pos, boundary):
    scores = masked_scores(query_block, key_block, query_pos, key_pos, boundary)
    top_score = jnp.max(scores, axis=-1, keepdims=True)
    powered = jnp.exp(scores - top_score)
    row_total = jnp.sum(powered, axis=-1, keepdims=True)
    prob_low = (powered / row_total).astype(jnp.bfloat16)
    result = jnp.einsum("hqk,khd->qhd", prob_low, value_block, preferred_element_type=jnp.float32)
    log_total = (top_score + jnp.log(row_total))[..., 0]
    return (result, log_total)


def attend_back(
    query_block, key_block, value_block, grad_heads, log_total, query_pos, key_pos, boundary
):
    scale_factor = query_block.shape[-1] ** (-0.5)
    scores = masked_scores(query_block, key_block, query_pos, key_pos, boundary)
    prob_full = jnp.exp(scores - log_total[..., None])
    prob_low = prob_full.astype(jnp.bfloat16)
    grad_prob = jnp.einsum(
        "qhd,khd->hqk", grad_heads, value_block, preferred_element_type=jnp.float32
    )
    centred = grad_prob - jnp.sum(prob_full * grad_prob, axis=-1, keepdims=True)
    grad_scores = (prob_full * centred).astype(jnp.bfloat16)
    grad_query = (
        jnp.einsum("hqk,khd->qhd", grad_scores, key_block, preferred_element_type=jnp.float32)
        * scale_factor
    )
    grad_key = (
        jnp.einsum("hqk,qhd->khd", grad_scores, query_block, preferred_element_type=jnp.float32)
        * scale_factor
    )
    grad_value = jnp.einsum(
        "hqk,qhd->khd", prob_low, grad_heads, preferred_element_type=jnp.float32
    )
    return (grad_query, grad_key, grad_value)


def attend_blocks(query_heads, key_all, value_all, query_pos, key_pos, boundary):
    run_rows, head_count, head_size = query_heads.shape
    block_rows = min(run_rows, 512)
    block_count = run_rows // block_rows
    query_blocks = query_heads.reshape(block_count, block_rows, head_count, head_size)
    place_blocks = query_pos.reshape(block_count, block_rows)

    def one_block(block_item):
        return attend(block_item[0], key_all, value_all, block_item[1], key_pos, boundary)

    results, log_totals = lax.map(one_block, (query_blocks, place_blocks))
    return (results.reshape(run_rows, head_count, head_size), log_totals)


def attend_blocks_back(
    query_heads, key_all, value_all, grad_heads, log_totals, query_pos, key_pos, boundary
):
    run_rows, head_count, head_size = query_heads.shape
    block_rows = min(run_rows, 512)
    block_count = run_rows // block_rows
    query_blocks = query_heads.reshape(block_count, block_rows, head_count, head_size)
    grad_blocks = grad_heads.reshape(block_count, block_rows, head_count, head_size)
    place_blocks = query_pos.reshape(block_count, block_rows)

    def one_block(running, block_item):
        grad_query, grad_key, grad_value = attend_back(
            block_item[0],
            key_all,
            value_all,
            block_item[1],
            block_item[2],
            block_item[3],
            key_pos,
            boundary,
        )
        return ((running[0] + grad_key, running[1] + grad_value), grad_query)

    zero_keys = jnp.zeros(key_all.shape, jnp.float32)
    (grad_key, grad_value), grad_query = lax.scan(
        one_block, (zero_keys, zero_keys), (query_blocks, grad_blocks, log_totals, place_blocks)
    )
    return (grad_query.reshape(run_rows, head_count, head_size), grad_key, grad_value)


def reduce_grads(first_grad, second_grad, third_grad):
    halves = (
        lax.psum_scatter(
            first_grad.astype(jnp.bfloat16), "seq", scatter_dimension=1, tiled=True
        ).astype(jnp.float32),
        lax.psum_scatter(
            second_grad.astype(jnp.bfloat16), "seq", scatter_dimension=1, tiled=True
        ).astype(jnp.float32),
        lax.psum_scatter(
            third_grad.astype(jnp.bfloat16), "seq", scatter_dimension=1, tiled=True
        ).astype(jnp.float32),
    )
    pieces = (
        lax.psum_scatter(halves[0], "fsdp", scatter_dimension=0, tiled=True),
        lax.psum_scatter(halves[1], "fsdp", scatter_dimension=0, tiled=True),
        lax.psum_scatter(halves[2], "fsdp", scatter_dimension=0, tiled=True),
    )
    return (
        lax.all_gather(pieces[0].astype(jnp.bfloat16), "seq", axis=1, tiled=True).astype(
            jnp.float32
        ),
        lax.all_gather(pieces[1].astype(jnp.bfloat16), "seq", axis=1, tiled=True).astype(
            jnp.float32
        ),
        lax.all_gather(pieces[2].astype(jnp.bfloat16), "seq", axis=1, tiled=True).astype(
            jnp.float32
        ),
    )


def on_device(
    tokens,
    bounds,
    norm_attn,
    weight_qkv,
    weight_out,
    norm_ffn,
    weight_gate,
    weight_up,
    weight_down,
    cotangent,
):
    row_count = tokens.shape[1]
    run_rows = row_count * lax.axis_size("seq")
    span_runs = max(MIN_LEN // run_rows, 1)
    hops = min(span_runs - 1, (WINDOW + run_rows - 2) // run_rows)
    seq_place = lax.axis_index("seq")
    shard_place = lax.axis_index("fsdp")
    slot = shard_place % span_runs
    sequence_id = shard_place // span_runs
    boundary = jnp.sum(
        jnp.where(jnp.arange(bounds.shape[0], dtype=jnp.int32) == sequence_id, bounds, 0)
    )
    inputs = tokens[0].astype(jnp.float32)
    gain_attn, full_qkv, full_out, gain_ffn, full_gate, full_up, full_down = (
        lax.all_gather(norm_attn, "fsdp", axis=0, tiled=True),
        lax.all_gather(weight_qkv, "fsdp", axis=0, tiled=True),
        lax.all_gather(weight_out, "fsdp", axis=0, tiled=True),
        lax.all_gather(norm_ffn, "fsdp", axis=0, tiled=True),
        lax.all_gather(weight_gate, "fsdp", axis=0, tiled=True),
        lax.all_gather(weight_up, "fsdp", axis=0, tiled=True),
        lax.all_gather(weight_down, "fsdp", axis=0, tiled=True),
    )
    inv_attn = lax.rsqrt(jnp.mean(inputs * inputs, axis=-1, keepdims=True) + EPS)
    base_attn = inputs * inv_attn
    act_attn = (base_attn * gain_attn).astype(jnp.bfloat16)
    proj_qkv = jnp.dot(act_attn, full_qkv, preferred_element_type=jnp.float32).reshape(
        row_count, 3, H, HD
    )
    own_pos = slot * run_rows + seq_place * row_count + jnp.arange(row_count, dtype=jnp.int32)
    cosine, sine_table = rope_tables(own_pos, HD)
    query_own = rotate(proj_qkv[:, 0], cosine, sine_table).astype(jnp.bfloat16)
    key_own = rotate(proj_qkv[:, 1], cosine, sine_table).astype(jnp.bfloat16)
    value_own = proj_qkv[:, 2].astype(jnp.bfloat16)
    query_heads, key_heads, value_heads = (
        lax.all_to_all(query_own, "seq", split_axis=1, concat_axis=0, tiled=True),
        lax.all_to_all(key_own, "seq", split_axis=1, concat_axis=0, tiled=True),
        lax.all_to_all(value_own, "seq", split_axis=1, concat_axis=0, tiled=True),
    )
    run_pos = slot * run_rows + jnp.arange(run_rows, dtype=jnp.int32)
    key_list = [key_heads]
    value_list = [value_heads]
    moving_key, moving_value = (key_heads, value_heads)
    for hop_step in range(hops):
        moving_key, moving_value = shifted((moving_key, moving_value), "fsdp", 1)
        key_list.insert(0, moving_key)
        value_list.insert(0, moving_value)
    key_all = jnp.concatenate(key_list, axis=0)
    value_all = jnp.concatenate(value_list, axis=0)
    key_pos = (slot - hops) * run_rows + jnp.arange((hops + 1) * run_rows, dtype=jnp.int32)
    result, log_totals = attend_blocks(query_heads, key_all, value_all, run_pos, key_pos, boundary)
    attn_tokens = lax.all_to_all(
        result.astype(jnp.bfloat16), "seq", split_axis=0, concat_axis=1, tiled=True
    )
    attn_rows = attn_tokens.reshape(row_count, H * HD)
    middle = inputs + jnp.dot(attn_rows, full_out, preferred_element_type=jnp.float32)
    inv_ffn = lax.rsqrt(jnp.mean(middle * middle, axis=-1, keepdims=True) + EPS)
    base_ffn = middle * inv_ffn
    act_ffn = (base_ffn * gain_ffn).astype(jnp.bfloat16)
    gate_proj = jnp.dot(act_ffn, full_gate, preferred_element_type=jnp.float32)
    up_proj = jnp.dot(act_ffn, full_up, preferred_element_type=jnp.float32)
    hidden = (jax.nn.silu(gate_proj) * up_proj).astype(jnp.bfloat16)
    block_out = middle + jnp.dot(hidden, full_down, preferred_element_type=jnp.float32)
    grad_top = cotangent[0]
    grad_output = grad_top.astype(jnp.float32)
    gain_ffn_back, gate_back, up_back, down_back = (
        lax.all_gather(norm_ffn, "fsdp", axis=0, tiled=True),
        lax.all_gather(weight_gate, "fsdp", axis=0, tiled=True),
        lax.all_gather(weight_up, "fsdp", axis=0, tiled=True),
        lax.all_gather(weight_down, "fsdp", axis=0, tiled=True),
    )
    grad_hidden = lax.dot_general(
        grad_top, down_back, CONTRACT_LAST, preferred_element_type=jnp.float32
    )
    sigmoid_gate = jax.nn.sigmoid(gate_proj)
    silu_gate = gate_proj * sigmoid_gate
    grad_gate_act = (
        grad_hidden * up_proj * sigmoid_gate * (1.0 + gate_proj * (1.0 - sigmoid_gate))
    ).astype(jnp.bfloat16)
    grad_up_act = (grad_hidden * silu_gate).astype(jnp.bfloat16)
    grad_act_ffn = lax.dot_general(
        grad_gate_act, gate_back, CONTRACT_LAST, preferred_element_type=jnp.float32
    )
    grad_act_ffn = grad_act_ffn + lax.dot_general(
        grad_up_act, up_back, CONTRACT_LAST, preferred_element_type=jnp.float32
    )
    grad_down = lax.dot_general(
        hidden, grad_top, CONTRACT_FIRST, preferred_element_type=jnp.float32
    )
    grad_gate = lax.dot_general(
        act_ffn, grad_gate_act, CONTRACT_FIRST, preferred_element_type=jnp.float32
    )
    grad_up = lax.dot_general(
        act_ffn, grad_up_act, CONTRACT_FIRST, preferred_element_type=jnp.float32
    )
    grad_gain_ffn = jnp.sum(grad_act_ffn * base_ffn, axis=0)
    scaled_ffn = grad_act_ffn * gain_ffn_back
    grad_middle = (
        grad_output
        + inv_ffn * scaled_ffn
        - middle * inv_ffn**3 * jnp.mean(scaled_ffn * middle, axis=-1, keepdims=True)
    )
    sum_down, sum_gate, sum_up = reduce_grads(grad_down, grad_gate, grad_up)
    gain_attn_back, qkv_back, out_back = (
        lax.all_gather(norm_attn, "fsdp", axis=0, tiled=True),
        lax.all_gather(weight_qkv, "fsdp", axis=0, tiled=True),
        lax.all_gather(weight_out, "fsdp", axis=0, tiled=True),
    )
    grad_branch = grad_middle.astype(jnp.bfloat16)
    grad_out_proj = lax.dot_general(
        attn_rows, grad_branch, CONTRACT_FIRST, preferred_element_type=jnp.float32
    )
    grad_attn = lax.dot_general(
        grad_branch, out_back, CONTRACT_LAST, preferred_element_type=jnp.float32
    )
    grad_attn = grad_attn.astype(jnp.bfloat16).reshape(row_count, H, HD)
    grad_heads = lax.all_to_all(grad_attn, "seq", split_axis=1, concat_axis=0, tiled=True)
    grad_query, grad_key_all, grad_value_all = attend_blocks_back(
        query_heads, key_all, value_all, grad_heads, log_totals, run_pos, key_pos, boundary
    )
    carry_key = grad_key_all[:run_rows]
    carry_value = grad_value_all[:run_rows]
    for hop_step in range(hops):
        carry_key, carry_value = (
            shifted(carry_key.astype(jnp.bfloat16), "fsdp", -1).astype(carry_key.dtype),
            shifted(carry_value.astype(jnp.bfloat16), "fsdp", -1).astype(carry_value.dtype),
        )
        start_row = (hop_step + 1) * run_rows
        carry_key = carry_key + grad_key_all[start_row : start_row + run_rows]
        carry_value = carry_value + grad_value_all[start_row : start_row + run_rows]
    back_query, back_key, back_value = (
        lax.all_to_all(
            grad_query.astype(jnp.bfloat16), "seq", split_axis=0, concat_axis=1, tiled=True
        ),
        lax.all_to_all(
            carry_key.astype(jnp.bfloat16), "seq", split_axis=0, concat_axis=1, tiled=True
        ),
        lax.all_to_all(
            carry_value.astype(jnp.bfloat16), "seq", split_axis=0, concat_axis=1, tiled=True
        ),
    )
    grad_qkv_rows = jnp.stack(
        [
            unrotate(back_query.astype(jnp.float32), cosine, sine_table),
            unrotate(back_key.astype(jnp.float32), cosine, sine_table),
            back_value.astype(jnp.float32),
        ],
        axis=1,
    )
    grad_qkv_rows = grad_qkv_rows.astype(jnp.bfloat16).reshape(row_count, 3 * H * HD)
    grad_qkv = lax.dot_general(
        act_attn, grad_qkv_rows, CONTRACT_FIRST, preferred_element_type=jnp.float32
    )
    grad_act_attn = lax.dot_general(
        grad_qkv_rows, qkv_back, CONTRACT_LAST, preferred_element_type=jnp.float32
    )
    grad_gain_attn = jnp.sum(grad_act_attn * base_attn, axis=0)
    scaled_attn = grad_act_attn * gain_attn_back
    grad_tokens = (
        grad_middle
        + inv_attn * scaled_attn
        - inputs * inv_attn**3 * jnp.mean(scaled_attn * inputs, axis=-1, keepdims=True)
    )
    both_gains = jnp.stack([grad_gain_attn, grad_gain_ffn], axis=1)
    sum_out, sum_qkv, sum_gains = reduce_grads(grad_out_proj, grad_qkv, both_gains)
    return (
        block_out.astype(jnp.bfloat16)[None],
        grad_tokens[None],
        sum_gains[:, 0],
        sum_qkv,
        sum_out,
        sum_gains[:, 1],
        sum_gate,
        sum_up,
        sum_down,
    )


def solution(mesh):
    return jax.shard_map(
        on_device,
        mesh=mesh,
        in_specs=(
            P("fsdp", "seq", None),
            P(),
            P("fsdp"),
            P("fsdp", None),
            P("fsdp", None),
            P("fsdp"),
            P("fsdp", None),
            P("fsdp", None),
            P("fsdp", None),
            P("fsdp", "seq", None),
        ),
        out_specs=(
            P("fsdp", "seq", None),
            P("fsdp", "seq", None),
            P("fsdp"),
            P("fsdp", None),
            P("fsdp", None),
            P("fsdp"),
            P("fsdp", None),
            P("fsdp", None),
            P("fsdp", None),
        ),
        check_vma=False,
    )
```

profile of v0, /device:TPU:0, one launch (start us, length us, event | category | flops | bytes accessed | tf_op | source)
XLA Modules:
  0.0 2606.4 jit_solution(3403402786494533702)
XLA Ops:
  10.6 23.0 all-gather
  34.9 106.1 %all-gather.13.cloned.1.call-done = bf16[2048,6144]{1,0:T(8,128)(2,1)} async-done(((bf16[128,6144]{1,0:T(8,128)(2,1)}), bf16[2048,6144]{1,0:T(8,128)(2,1)}) %all-gather.13.cloned.1.call-update) | async-done | bytes 25165840 | tf_op jit(solution)/shard_map/all_gather | solution.py:206
  141.0 30.8 %copy.67 = bf16[6144,2048]{1,0:T(8,128)(2,1)} copy(bf16[6144,2048]{0,1:T(8,128)(2,1)} %bitcast.155) | data formatting | bytes 50331648 | tf_op jit(solution)/shard_map/dot_general | solution.py:216
  237.2 33.0 %collective-permute-start.3 = (bf16[512,8,128]{2,0,1:T(8,128)(2,1)}, bf16[512,8,128]{2,0,1:T(8,128)(2,1)}, u32[]{:S(2)}, u32[]{:S(2)}) collective-permute-start(bf16[512,8,128]{2,0,1:T(8,128)(2,1)} %collective-permute-done.2), channel_id=1, source_target_pairs={{0,1},{1,2},{2,3},{3,4},{4,5},{5,6},{6,7},{7,8},{8,9},{9,10},{10,1... | collective-permute-start | bytes 3145736 | tf_op jit(solution)/shard_map/ppermute | solution.py:22
  338.5 57.2 %all-gather.1 = bf16[16,1,128]{2,1,0:T(2,128)(2,1)S(1)} all-gather(bf16[1,1,128]{2,1,0:T(2,128)(2,1)S(1)} %bitcast.189), channel_id=1, replica_groups=mesh['seq'=2,'fsdp'=16] {'fsdp'}, dimensions={0}, use_global_device_ids=true | all-gather | bytes 4352 | tf_op jit(solution)/shard_map/all_gather | solution.py:208
  403.9 14.0 fusion.54
  417.9 72.1 %all-gather.19.cloned.1.call-done = bf16[2048,5504]{1,0:T(8,128)(2,1)} async-done(((bf16[128,5504]{1,0:T(8,128)(2,1)}), bf16[2048,5504]{1,0:T(8,128)(2,1)}) %all-gather.19.cloned.1.call-update) | async-done | bytes 22544400 | tf_op jit(solution)/shard_map/all_gather | solution.py:210
  503.0 104.8 %all-gather.21.cloned.1.call-done = bf16[5504,2048]{1,0:T(8,128)(2,1)} async-done(((bf16[344,2048]{1,0:T(8,128)(2,1)}), bf16[5504,2048]{1,0:T(8,128)(2,1)}) %all-gather.21.cloned.1.call-update) | async-done | bytes 22544400 | tf_op jit(solution)/shard_map/all_gather | solution.py:211
  607.7 18.2 multiply_convert_fusion.1
  705.9 26.0 all-to-all-done.4
  732.0 17.1 multiply_reduce_fusion
  749.1 17.4 multiply_convert_fusion
  815.0 18.9 all-to-all-done.5
  841.2 20.3 all-to-all-done.6
  869.5 20.2 all-to-all-done.7
  895.8 14.0 convolution_convert_fusion.1
  918.2 16.7 reduce-scatter.36.cloned.1.call-done
  934.9 253.4 %reduce-scatter.38.cloned.1.call-done = bf16[2048,2752]{0,1:T(8,128)(2,1)} async-done(((bf16[2048,5504]{0,1:T(8,128)(2,1)}), bf16[2048,2752]{0,1:T(8,128)(2,1)}) %reduce-scatter.38.cloned.1.call-update) | async-done | bytes 11272208
  1188.4 253.4 %reduce-scatter.30.cloned.1.call-done = bf16[5504,1024]{1,0:T(8,128)(2,1)} async-done(((bf16[5504,2048]{1,0:T(8,128)(2,1)}), bf16[5504,1024]{1,0:T(8,128)(2,1)}) %reduce-scatter.30.cloned.1.call-update) | async-done | bytes 11272208 | tf_op jit(solution)/shard_map/reduce_scatter | solution.py:152
  1441.9 281.6 %reduce-scatter.18.cloned.1.call-done = bf16[2048,3072]{1,0:T(8,128)(2,1)} async-done(((bf16[2048,6144]{1,0:T(8,128)(2,1)}), bf16[2048,3072]{1,0:T(8,128)(2,1)}) %reduce-scatter.18.cloned.1.call-update) | async-done | bytes 12582928 | tf_op jit(solution)/shard_map/reduce_scatter | solution.py:155
  1724.7 14.6 fusion.26
  1746.5 78.5 %reduce-scatter.22.cloned.1.call-done = bf16[2048,1024]{1,0:T(8,128)(2,1)} async-done(((bf16[2048,2048]{1,0:T(8,128)(2,1)}), bf16[2048,1024]{1,0:T(8,128)(2,1)}) %reduce-scatter.22.cloned.1.call-update) | async-done | bytes 4194320 | tf_op jit(solution)/shard_map/reduce_scatter | solution.py:152
  1825.1 129.2 %reduce-scatter.26.cloned.1.call-done = bf16[128,2752]{0,1:T(8,128)(2,1)} async-done(((bf16[2048,2752]{0,1:T(8,128)(2,1)}), bf16[128,2752]{0,1:T(8,128)(2,1)}) %reduce-scatter.26.cloned.1.call-update) | async-done | bytes 704528 | tf_op jit(solution)/shard_map/reduce_scatter | solution.py:164
  1954.3 128.8 %reduce-scatter.28.cloned.1.call-done = bf16[128,2752]{0,1:T(8,128)(2,1)} async-done(((bf16[2048,2752]{0,1:T(8,128)(2,1)}), bf16[128,2752]{0,1:T(8,128)(2,1)}) %reduce-scatter.28.cloned.1.call-update) | async-done | bytes 704528 | tf_op jit(solution)/shard_map/reduce_scatter | solution.py:165
  2083.2 128.9 %reduce-scatter.32.cloned.1.call-done = bf16[344,1024]{1,0:T(8,128)(2,1)} async-done(((bf16[5504,1024]{1,0:T(8,128)(2,1)}), bf16[344,1024]{1,0:T(8,128)(2,1)}) %reduce-scatter.32.cloned.1.call-update) | async-done | bytes 704528 | tf_op jit(solution)/shard_map/reduce_scatter | solution.py:163
  2212.2 138.8 %reduce-scatter.20.cloned.1.call-done = bf16[128,3072]{1,0:T(8,128)(2,1)} async-done(((bf16[2048,3072]{1,0:T(8,128)(2,1)}), bf16[128,3072]{1,0:T(8,128)(2,1)}) %reduce-scatter.20.cloned.1.call-update) | async-done | bytes 786448 | tf_op jit(solution)/shard_map/reduce_scatter | solution.py:164
  2365.8 46.1 %reduce-scatter.34.cloned.1.call-done = f32[128,1]{1,0:T(8,128)} async-done(((f32[2048,1]{1,0:T(8,128)}), f32[128,1]{1,0:T(8,128)}) %reduce-scatter.34.cloned.1.call-update) | async-done | bytes 528
  2417.6 69.6 %reduce-scatter.24.cloned.1.call-done = bf16[128,1024]{1,0:T(8,128)(2,1)} async-done(((bf16[2048,1024]{1,0:T(8,128)(2,1)}), bf16[128,1024]{1,0:T(8,128)(2,1)}) %reduce-scatter.24.cloned.1.call-update) | async-done | bytes 262160 | tf_op jit(solution)/shard_map/reduce_scatter | solution.py:163
  2495.6 17.5 all-gather.25.cloned.1.call-done
  2516.0 23.9 all-gather.27.cloned.1.call-done
  2542.9 24.1 all-gather.29.cloned.1.call-done
  2570.2 25.5 all-gather.23.cloned.1.call-done
  (221 shorter events, 367.3 us)
Async XLA Ops:
  7.2 133.8 %all-gather.13.cloned.1.call-start = ((), (), s32[]{:S(2)}) async-start(), calls=%async_computation.19 | async-start | bytes 26738688 | tf_op jit(solution)/shard_map/all_gather | solution.py:206
  7.9 389.3 %all-gather.15.cloned.1.call-start = ((), (), s32[]{:S(2)}) async-start(), calls=%async_computation.20 | async-start | bytes 8912896 | tf_op jit(solution)/shard_map/all_gather | solution.py:207
  8.7 395.2 %all-gather.17.cloned.1.call-start = ((), (), s32[]{:S(2)}) async-start(), calls=%async_computation.21 | async-start | bytes 23953408 | tf_op jit(solution)/shard_map/all_gather | solution.py:209
  9.4 480.6 %all-gather.19.cloned.1.call-start = ((), (), s32[]{:S(2)}) async-start(), calls=%async_computation.22 | async-start | bytes 23953408 | tf_op jit(solution)/shard_map/all_gather | solution.py:210
  10.0 597.7 %all-gather.21.cloned.1.call-start = ((), (), s32[]{:S(2)}) async-start(), calls=%async_computation.23 | async-start | bytes 23953408 | tf_op jit(solution)/shard_map/all_gather | solution.py:211
  188.7 19.8 all-to-all-start
  213.0 18.5 collective-permute-start
  231.5 62.4 %collective-permute-start.1 = (bf16[512,8,128]{0,2,1:T(8,128)(2,1)}, bf16[512,8,128]{0,2,1:T(8,128)(2,1)}, u32[]{:S(2)}, u32[]{:S(2)}) collective-permute-start(bf16[512,8,128]{0,2,1:T(8,128)(2,1)} %collective-permute-done), channel_id=1, source_target_pairs={{0,1},{1,2},{2,3},{3,4},{4,5},{5,6},{6,7},{7,8},{8,9},{9,10},{10,1... | collective-permute-start | bytes 3145736 | tf_op jit(solution)/shard_map/ppermute | solution.py:22
  237.2 59.9 %collective-permute-start.3 = (bf16[512,8,128]{2,0,1:T(8,128)(2,1)}, bf16[512,8,128]{2,0,1:T(8,128)(2,1)}, u32[]{:S(2)}, u32[]{:S(2)}) collective-permute-start(bf16[512,8,128]{2,0,1:T(8,128)(2,1)} %collective-permute-done.2), channel_id=1, source_target_pairs={{0,1},{1,2},{2,3},{3,4},{4,5},{5,6},{6,7},{7,8},{8,9},{9,10},{10,1... | collective-permute-start | bytes 3145736 | tf_op jit(solution)/shard_map/ppermute | solution.py:22
  272.5 18.7 all-to-all-start.1
  334.9 60.9 %all-to-all-start.3 = ((bf16[512,8,128]{2,1,0:T(8,128)(2,1)}), bf16[512,8,128]{2,1,0:T(8,128)(2,1)S(1)}, u32[]{:S(2)}, u32[]{:S(2)}) async-start(bf16[512,8,128]{2,1,0:T(8,128)(2,1)} %copy.71), calls=%async_computation.3 | async-start | bytes 2097152 | tf_op jit(solution)/shard_map/all_to_all | solution.py:241
  338.5 596.4 %reduce-scatter.36.cloned.1.call-start = ((), (), s32[]{:S(2)}) async-start(), calls=%async_computation.37 | async-start | bytes 33816576
  638.7 549.7 %reduce-scatter.38.cloned.1.call-start = ((), (), s32[]{:S(2)}) async-start(), calls=%async_computation.38 | async-start | bytes 33816576
  651.7 790.1 %reduce-scatter.30.cloned.1.call-start = ((), (), s32[]{:S(2)}) async-start(), calls=%async_computation.33 | async-start | bytes 33816576 | tf_op jit(solution)/shard_map/reduce_scatter | solution.py:152
  702.3 29.6 %all-to-all-start.4 = ((bf16[256,16,128]{2,0,1:T(8,128)(2,1)}), bf16[256,16,128]{2,0,1:T(8,128)(2,1)S(1)}, u32[]{:S(2)}, u32[]{:S(2)}) async-start(bf16[256,16,128]{2,0,1:T(8,128)(2,1)} %bitcast.154), calls=%async_computation.4 | async-start | bytes 2097152 | tf_op jit(solution)/shard_map/all_to_all | solution.py:306
  792.2 19.1 collective-permute-start.5
  794.9 42.6 %collective-permute-start.7 = (bf16[512,8,128]{0,2,1:T(8,128)(2,1)}, bf16[512,8,128]{0,2,1:T(8,128)(2,1)}, u32[]{:S(2)}, u32[]{:S(2)}) collective-permute-start(bf16[512,8,128]{0,2,1:T(8,128)(2,1)} %fusion.30), channel_id=1, source_target_pairs={{1,0},{2,1},{3,2},{4,3},{5,4},{6,5},{7,6},{8,7},{9,8},{10,9},{11,1... | collective-permute-start | bytes 3145736 | tf_op jit(solution)/shard_map/ppermute | solution.py:22
  807.7 26.2 %all-to-all-start.5 = ((bf16[512,8,128]{2,1,0:T(8,128)(2,1)}), bf16[512,8,128]{2,1,0:T(8,128)(2,1)S(1)}, u32[]{:S(2)}, u32[]{:S(2)}) async-start(bf16[512,8,128]{2,1,0:T(8,128)(2,1)} %copy.77), calls=%async_computation.5 | async-start | bytes 2097152 | tf_op jit(solution)/shard_map/all_to_all | solution.py:321
  833.9 27.6 %all-to-all-start.6 = ((bf16[512,8,128]{2,1,0:T(8,128)(2,1)}), bf16[512,8,128]{2,1,0:T(8,128)(2,1)S(1)}, u32[]{:S(2)}, u32[]{:S(2)}) async-start(bf16[512,8,128]{2,1,0:T(8,128)(2,1)} %copy.80), calls=%async_computation.6 | async-start | bytes 2097152 | tf_op jit(solution)/shard_map/all_to_all | solution.py:324
  861.5 28.2 %all-to-all-start.7 = ((bf16[512,8,128]{2,1,0:T(8,128)(2,1)}), bf16[512,8,128]{2,1,0:T(8,128)(2,1)}, u32[]{:S(2)}, u32[]{:S(2)}) async-start(bf16[512,8,128]{2,1,0:T(8,128)(2,1)} %copy.83), calls=%async_computation.7 | async-start | bytes 2097152 | tf_op jit(solution)/shard_map/all_to_all | solution.py:327
  865.9 857.6 %reduce-scatter.18.cloned.1.call-start = ((), (), s32[]{:S(2)}) async-start(), calls=%async_computation.24 | async-start | bytes 37748736 | tf_op jit(solution)/shard_map/reduce_scatter | solution.py:155
  909.7 915.3 %reduce-scatter.22.cloned.1.call-start = ((), (), s32[]{:S(2)}) async-start(), calls=%async_computation.27 | async-start | bytes 12582912 | tf_op jit(solution)/shard_map/reduce_scatter | solution.py:152
  918.2 1036.1 %reduce-scatter.26.cloned.1.call-start = ((), (), s32[]{:S(2)}) async-start(), calls=%async_computation.29 | async-start | bytes 11976704 | tf_op jit(solution)/shard_map/reduce_scatter | solution.py:164
  934.9 1148.2 %reduce-scatter.28.cloned.1.call-start = ((), (), s32[]{:S(2)}) async-start(), calls=%async_computation.31 | async-start | bytes 11976704 | tf_op jit(solution)/shard_map/reduce_scatter | solution.py:165
  1188.4 1023.7 %reduce-scatter.32.cloned.1.call-start = ((), (), s32[]{:S(2)}) async-start(), calls=%async_computation.34 | async-start | bytes 11976704 | tf_op jit(solution)/shard_map/reduce_scatter | solution.py:163
  1441.8 909.2 %reduce-scatter.20.cloned.1.call-start = ((), (), s32[]{:S(2)}) async-start(), calls=%async_computation.25 | async-start | bytes 13369344 | tf_op jit(solution)/shard_map/reduce_scatter | solution.py:164
  1723.5 688.5 %reduce-scatter.34.cloned.1.call-start = ((), (), s32[]{:S(2)}) async-start(), calls=%async_computation.36 | async-start | bytes 1114112
  1746.5 740.8 %reduce-scatter.24.cloned.1.call-start = ((), (), s32[]{:S(2)}) async-start(), calls=%async_computation.28 | async-start | bytes 4456448 | tf_op jit(solution)/shard_map/reduce_scatter | solution.py:163
  1825.1 688.0 %all-gather.25.cloned.1.call-start = ((), (), s32[]{:S(2)}) async-start(), calls=%async_computation.30 | async-start | bytes 2113536 | tf_op jit(solution)/shard_map/all_gather | solution.py:171
  1954.3 585.7 %all-gather.27.cloned.1.call-start = ((), (), s32[]{:S(2)}) async-start(), calls=%async_computation.32 | async-start | bytes 2113536 | tf_op jit(solution)/shard_map/all_gather | solution.py:174
  2083.1 483.8 %all-gather.29.cloned.1.call-start = ((), (), s32[]{:S(2)}) async-start(), calls=%async_computation.35 | async-start | bytes 2113536 | tf_op jit(solution)/shard_map/all_gather | solution.py:168
  2212.1 383.6 %all-gather.23.cloned.1.call-start = ((), (), s32[]{:S(2)}) async-start(), calls=%async_computation.26 | async-start | bytes 2359296 | tf_op jit(solution)/shard_map/all_gather | solution.py:171
  (37 other events, 1228.8 us)
Sparse Core Ops, SparseCore 0:
  9.6 131.2 all-gather.12
  143.1 75.2 all-gather.14
  220.0 147.4 all-gather.16
  368.9 120.9 all-gather.18
  491.4 116.2 all-gather.20
  638.8 296.0 reduce-scatter.35
  937.2 251.1 reduce-scatter.37
  1190.6 251.1 reduce-scatter.29
  1444.1 279.2 reduce-scatter.17
  1725.6 99.3 reduce-scatter.21
  1829.7 124.5 reduce-scatter.25
  1958.8 124.2 reduce-scatter.27
  2087.8 124.2 reduce-scatter.31
  2216.6 134.4 reduce-scatter.19
  2355.5 56.4 reduce-scatter.33
  2415.7 71.5 reduce-scatter.23
  2488.7 24.3 all-gather.24
  2514.6 25.3 all-gather.26
  2541.6 25.3 all-gather.28
  2568.4 27.2 all-gather.22
where the time goes:
time: 2610 us
  waiting for transfers between devices  2020 us (77%)
  matrix products  249 us (10%)
  blocking collectives  96.8 us (4%)
  starting transfers between devices  81.4 us (3%)
  local copies, waits for them, and re-layouts  76.2 us (3%)
  other arithmetic  67.1 us (3%)
    reduce_scatter x2, waiting for transfers between devices, reduce_grads(): lax.psum_scatter(first_grad.astype(jnp.bfloat16), 'seq', scatter_dimensio...  332 us
    unnamed x23, waiting for transfers between devices  320 us
    reduce_scatter x1, waiting for transfers between devices, reduce_grads(): lax.psum_scatter(second_grad.astype(jnp.bfloat16), 'seq', scatter_dimensi...  282 us
    reduce_scatter x2, waiting for transfers between devices, reduce_grads(): lax.psum_scatter(halves[1], 'fsdp', scatter_dimension=0, tiled=True)  268 us
    reduce_scatter x2, waiting for transfers between devices, reduce_grads(): lax.psum_scatter(halves[0], 'fsdp', scatter_dimension=0, tiled=True)  199 us
    reduce_scatter x1, waiting for transfers between devices, reduce_grads(): lax.psum_scatter(halves[2], 'fsdp', scatter_dimension=0, tiled=True)  129 us
    all_gather x1, waiting for transfers between devices, on_device(): lax.all_gather(weight_qkv, 'fsdp', axis=0, tiled=True)  106 us
    all_gather x1, waiting for transfers between devices, on_device(): lax.all_gather(weight_down, 'fsdp', axis=0, tiled=True)  105 us
  transfers between devices with their start and end apart: 36, of which 25 were waited for; matrix products, arithmetic and copies ran while one was open for 13% of the time, Pallas kernels for 0%

commit v1 on v0

v1 whole, which is shorter than its diff:
```python
import functools

import jax
import jax.numpy as jnp
from jax import lax
from jax.experimental import pallas as pl
from jax.experimental.pallas import tpu as pltpu
from jax.sharding import Mesh, PartitionSpec as P

HD = 128
WINDOW = 1024
EPS = 1e-05
NEG = -1e30
THETA = 10000.0
F32 = jnp.float32
BF16 = jnp.bfloat16
BITS = (("y", 1), ("x", 2), ("c", 4))
NT = (((1,), (1,)), ((), ()))
TN = (((0,), (0,)), ((), ()))


def axes_of(j):
    return tuple(name for name, bit in BITS if j & bit)


def hop(block, j):
    axes = axes_of(j)
    last = 2 ** len(axes) - 1
    return lax.ppermute(block, axes, [(i, last - i) for i in range(last + 1)])


def gather_plane(block):
    parts = {0: block, 1: hop(block, 1), 2: hop(block, 2), 3: hop(block, 3)}
    for j in range(4):
        parts[j + 4] = hop(parts[j], 4)
    return [parts[j] for j in range(8)]


def exchange_plane(blocks):
    return [blocks[0]] + [hop(blocks[j], j) for j in range(1, 8)]


def scatter_plane(near, far):
    rows = near.shape[0] // 4
    total = (near.astype(F32) + hop(far, 4).astype(F32)).reshape(4, rows, -1)
    own = total[0]
    for j in range(1, 4):
        own = own + hop(total[j].astype(BF16), j).astype(F32)
    return own


def ring_of(size):
    odd = [i for i in range(size) if i % 2 == 1]
    even = [i for i in range(size) if i % 2 == 0 and i > 0]
    return [0] + odd + even[::-1]


def ring_place(z, size, back):
    ring = ring_of(size)
    table = [ring[(ring.index(i) - back) % size] for i in range(size)]
    return jnp.asarray(table, jnp.int32)[z]


def ring_hop(block, size):
    ring = ring_of(size)
    return lax.ppermute(block, "z", [(ring[i], ring[(i + 1) % size]) for i in range(size)])


def ring_gather(block, z, size):
    out = jnp.zeros((size,) + block.shape, block.dtype)
    out = lax.dynamic_update_index_in_dim(out, block, z, 0)
    for back in range(1, size):
        block = ring_hop(block, size)
        out = lax.dynamic_update_index_in_dim(out, block, ring_place(z, size, back), 0)
    return out


def ring_scatter(chunks, z, size):
    total = lax.dynamic_index_in_dim(chunks, ring_place(z, size, 1), 0, False)
    for back in range(2, size + 1):
        moved = ring_hop(total.astype(BF16), size).astype(F32)
        total = moved + lax.dynamic_index_in_dim(
            chunks, ring_place(z, size, back), 0, False
        ).astype(F32)
    return total


def absolute(blocks, rank):
    stacked = jnp.stack(blocks)
    return [
        lax.dynamic_index_in_dim(stacked, jnp.bitwise_xor(rank, i), 0, False)
        for i in range(len(blocks))
    ]


def place_of(block):
    return (block & 1) | ((block >> 1) & 1) << 2 | ((block >> 2) & 1) << 1


def lowest_key(block, rows, bound):
    pos = block * rows + lax.broadcasted_iota(jnp.int32, (rows, 1), 0)
    return jnp.maximum(jnp.where(pos >= bound, bound, 0), pos - (WINDOW - 1))


def block_scores(query, key, low, q_block, k_block, rows):
    scores = lax.dot_general(query, key, NT, preferred_element_type=F32) * HD**-0.5
    pos = k_block * rows + lax.broadcasted_iota(jnp.int32, (rows, rows), 1)
    seen = pos >= low
    if q_block == k_block:
        seen = seen & (
            lax.broadcasted_iota(jnp.int32, (rows, rows), 1)
            <= lax.broadcasted_iota(jnp.int32, (rows, rows), 0)
        )
    return jnp.where(seen, scores, NEG)


def key_blocks(q_block, rows):
    return range(max(0, q_block - WINDOW // rows), q_block + 1)


def attend_kernel(rows, info, proj, cosine, sine, qkv, result, lse):
    count = proj.shape[0] // rows
    rank, bound = info[0], info[1]

    @pl.loop(0, count)
    def _(j):
        at = pl.ds(j * rows, rows)
        for part in range(2):
            value = proj[at, part * HD : (part + 1) * HD]
            turned = value * cosine[at, :] + pltpu.roll(value, HD // 2, 1) * sine[at, :]
            qkv[at, part * HD : (part + 1) * HD] = turned.astype(BF16)
        qkv[at, 2 * HD :] = proj[at, 2 * HD :].astype(BF16)

    def start(block):
        return pl.multiple_of(jnp.bitwise_xor(place_of(block), rank) * rows, rows)

    for b in range(count):
        own = pl.ds(start(b), rows)
        query = qkv[own, :HD]
        low = lowest_key(b, rows, bound)
        spots = [(kb, pl.ds(start(kb), rows)) for kb in key_blocks(b, rows)]
        scores = [
            block_scores(query, qkv[at, HD : 2 * HD], low, b, kb, rows) for kb, at in spots
        ]
        top = functools.reduce(jnp.maximum, [jnp.max(s, axis=1, keepdims=True) for s in scores])
        powered = [jnp.exp(s - top) for s in scores]
        total = functools.reduce(jnp.add, [jnp.sum(p, axis=1, keepdims=True) for p in powered])
        inverse = 1.0 / total
        out = functools.reduce(
            jnp.add,
            [
                jnp.dot(
                    (p * inverse).astype(BF16), qkv[at, 2 * HD :], preferred_element_type=F32
                )
                for p, (_, at) in zip(powered, spots)
            ],
        )
        result[own, :] = out.astype(BF16)
        lse[0, own, :] = top + jnp.log(total)


def attend(info, proj, cosine, sine, rows):
    length = proj.shape[0]
    heads = proj.shape[1] // (3 * HD)
    return pl.pallas_call(
        functools.partial(attend_kernel, rows),
        grid_spec=pltpu.PrefetchScalarGridSpec(
            num_scalar_prefetch=1,
            grid=(heads,),
            in_specs=[
                pl.BlockSpec((length, 3 * HD), lambda h, s: (0, h)),
                pl.BlockSpec((length, HD), lambda h, s: (0, 0)),
                pl.BlockSpec((length, HD), lambda h, s: (0, 0)),
            ],
            out_specs=[
                pl.BlockSpec((length, 3 * HD), lambda h, s: (0, h)),
                pl.BlockSpec((length, HD), lambda h, s: (0, h)),
                pl.BlockSpec((1, length, 1), lambda h, s: (h, 0, 0)),
            ],
        ),
        out_shape=[
            jax.ShapeDtypeStruct(proj.shape, BF16),
            jax.ShapeDtypeStruct((length, heads * HD), BF16),
            jax.ShapeDtypeStruct((heads, length, 1), F32),
        ],
        compiler_params=pltpu.CompilerParams(vmem_limit_bytes=48 * 2**20),
        name="attend",
    )(info, proj, cosine, sine)


def attend_back_kernel(rows, info, qkv, grad, lse, cosine, sine, out, sum_key, sum_value):
    count = qkv.shape[0] // rows
    rank, bound = info[0], info[1]
    sum_key[...] = jnp.zeros_like(sum_key)
    sum_value[...] = jnp.zeros_like(sum_value)

    def start(block):
        return pl.multiple_of(jnp.bitwise_xor(place_of(block), rank) * rows, rows)

    def unturn(value, at):
        value = value.astype(BF16).astype(F32)
        turned = value * cosine[at, :] - pltpu.roll(value, HD // 2, 1) * sine[at, :]
        return turned.astype(BF16)

    for b in range(count):
        own = pl.ds(start(b), rows)
        query = qkv[own, :HD]
        top = grad[own, :]
        low = lowest_key(b, rows, bound)
        log_total = lse[0, own, :]
        spots = [(kb, pl.ds(start(kb), rows)) for kb in key_blocks(b, rows)]
        probs = [
            jnp.exp(block_scores(query, qkv[at, HD : 2 * HD], low, b, kb, rows) - log_total)
            for kb, at in spots
        ]
        grads = [
            lax.dot_general(top, qkv[at, 2 * HD :], NT, preferred_element_type=F32)
            for _, at in spots
        ]
        mean = functools.reduce(
            jnp.add,
            [jnp.sum(p * g, axis=1, keepdims=True) for p, g in zip(probs, grads)],
        )
        sum_query = jnp.zeros((rows, HD), F32)
        for p, g, (_, at) in zip(probs, grads, spots):
            low_grad = (p * (g - mean)).astype(BF16)
            sum_query = sum_query + jnp.dot(
                low_grad, qkv[at, HD : 2 * HD], preferred_element_type=F32
            )
            sum_key[at, :] += lax.dot_general(low_grad, query, TN, preferred_element_type=F32)
            sum_value[at, :] += lax.dot_general(
                p.astype(BF16), top, TN, preferred_element_type=F32
            )
        out[own, :HD] = unturn(sum_query * HD**-0.5, own)

    @pl.loop(0, count)
    def _(j):
        at = pl.ds(pl.multiple_of(j * rows, rows), rows)
        out[at, HD : 2 * HD] = unturn(sum_key[at, :] * HD**-0.5, at)
        out[at, 2 * HD :] = sum_value[at, :].astype(BF16)


def attend_back(info, qkv, grad, lse, cosine, sine, rows):
    length = qkv.shape[0]
    heads = qkv.shape[1] // (3 * HD)
    return pl.pallas_call(
        functools.partial(attend_back_kernel, rows),
        grid_spec=pltpu.PrefetchScalarGridSpec(
            num_scalar_prefetch=1,
            grid=(heads,),
            in_specs=[
                pl.BlockSpec((length, 3 * HD), lambda h, s: (0, h)),
                pl.BlockSpec((length, HD), lambda h, s: (0, h)),
                pl.BlockSpec((1, length, 1), lambda h, s: (h, 0, 0)),
                pl.BlockSpec((length, HD), lambda h, s: (0, 0)),
                pl.BlockSpec((length, HD), lambda h, s: (0, 0)),
            ],
            out_specs=pl.BlockSpec((length, 3 * HD), lambda h, s: (0, h)),
            scratch_shapes=[pltpu.VMEM((length, HD), F32), pltpu.VMEM((length, HD), F32)],
        ),
        out_shape=jax.ShapeDtypeStruct(qkv.shape, BF16),
        compiler_params=pltpu.CompilerParams(vmem_limit_bytes=48 * 2**20),
        name="attend_back",
    )(info, qkv, grad, lse, cosine, sine)


def on_device(
    sizes,
    tokens,
    bounds,
    norm_attn,
    weight_qkv,
    weight_out,
    norm_ffn,
    weight_gate,
    weight_up,
    weight_down,
    cotangent,
):
    planes, shards = sizes
    rows, width = tokens.shape[1], tokens.shape[2]
    hidden_width = weight_gate.shape[1]
    own_rows = weight_qkv.shape[0]
    piece = width // 8
    half_down = weight_down.shape[0] // 2
    pad_down = -(-half_down // 16) * 16
    local = planes * pad_down

    y, z, x, c = (lax.axis_index(name) for name in ("y", "z", "x", "c"))
    rank = 4 * c + 2 * x + y
    shard = 2 * x + c
    other = [0, 4, 2, 6]
    boundary = lax.dynamic_index_in_dim(bounds, z, 0, False)
    info = jnp.stack([rank, boundary])

    def to_column_owners(pieces):
        got = [
            hop_if(lax.dynamic_index_in_dim(pieces, jnp.bitwise_xor(rank, j), 0, False), j)
            for j in other
        ]
        stacked = jnp.stack(got)
        return jnp.concatenate(
            [
                lax.dynamic_index_in_dim(stacked, jnp.bitwise_xor(shard, k), 0, False)
                for k in range(4)
            ]
        )

    def hop_if(block, j):
        return hop(block, j) if j else block

    def to_row_owners(total):
        blocks = total.astype(BF16).reshape(4, own_rows, -1)
        got = [
            hop_if(lax.dynamic_index_in_dim(blocks, jnp.bitwise_xor(shard, k), 0, False), j)
            for k, j in enumerate(other)
        ]
        mine = jnp.stack([got[0], got[2], got[1], got[3]])
        theirs = hop(mine, 1)
        relative = [mine[0], theirs[0], mine[1], theirs[1], mine[2], theirs[2], mine[3], theirs[3]]
        return jnp.stack(absolute(relative, rank))

    qkv_pieces = weight_qkv.reshape(own_rows, 3, 8, 2, HD).transpose(2, 0, 3, 1, 4)
    qkv_plane = to_column_owners(qkv_pieces.reshape(8, own_rows, 6 * HD))
    out_pieces = weight_out.reshape(own_rows, 8, piece).transpose(1, 0, 2)
    out_plane = to_column_owners(out_pieces)

    def hidden_pieces(weight):
        split = weight.reshape(own_rows, planes, 2, 2, 2, half_down)
        split = split.transpose(3, 2, 4, 0, 1, 5)
        split = jnp.pad(split, [(0, 0)] * 5 + [(0, pad_down - half_down)])
        return split.reshape(8, own_rows, local)

    pair_plane = to_column_owners(
        jnp.concatenate([hidden_pieces(weight_gate), hidden_pieces(weight_up)], axis=2)
    )
    down_own = lax.dynamic_slice_in_dim(weight_down, y * half_down, half_down, 0)
    down_own = jnp.pad(down_own, [(0, pad_down - half_down), (0, 0)])

    full_qkv = ring_gather(qkv_plane, z, planes).reshape(width, 6 * HD)
    cols_out = ring_gather(out_plane, z, planes).reshape(width, piece)
    full_pair = ring_gather(pair_plane, z, planes).reshape(width, 2 * local)
    full_down = ring_gather(down_own, z, planes).reshape(local, width)
    full_out = jnp.concatenate(absolute(gather_plane(cols_out), rank), axis=1)
    gains = lax.all_gather(
        jnp.stack([norm_attn, norm_ffn]), ("z", "x", "c"), axis=1, tiled=True
    ).astype(F32)
    gain_attn, gain_ffn = gains[0], gains[1]

    inputs = tokens[0].astype(F32)
    all_tokens = jnp.concatenate(gather_plane(tokens[0])).astype(F32)
    top_all = jnp.concatenate(gather_plane(cotangent[0]))
    inv_all = lax.rsqrt(jnp.mean(all_tokens * all_tokens, axis=-1, keepdims=True) + EPS)
    inv_attn = inv_all[:rows]
    act_attn = (all_tokens * inv_all * gain_attn).astype(BF16)

    blocks = jnp.asarray([place_of(i) for i in range(8)], jnp.int32)
    blocks = jnp.take(blocks, jnp.bitwise_xor(jnp.arange(8, dtype=jnp.int32), rank))
    positions = (blocks[:, None] * rows + jnp.arange(rows, dtype=jnp.int32)[None, :]).reshape(-1)
    frequency = THETA ** (-jnp.arange(HD // 2, dtype=F32) * 2.0 / HD)
    angles = positions.astype(F32)[:, None] * frequency[None, :]
    cosine = jnp.cos(angles)
    sine = jnp.sin(angles)
    cosine = jnp.concatenate([cosine, cosine], axis=1)
    sine = jnp.concatenate([-sine, sine], axis=1)

    proj = jnp.dot(act_attn, full_qkv, preferred_element_type=F32)
    qkv, attn, lse = attend(info, proj, cosine, sine, rows)
    attn_rows = exchange_plane([attn[j * rows : (j + 1) * rows] for j in range(8)])
    attn_rows = jnp.concatenate(absolute(attn_rows, rank), axis=1)
    middle = inputs + jnp.dot(attn_rows, full_out, preferred_element_type=F32)
    inv_ffn = lax.rsqrt(jnp.mean(middle * middle, axis=-1, keepdims=True) + EPS)
    base_ffn = middle * inv_ffn
    act_own = (base_ffn * gain_ffn).astype(BF16)
    act_ffn = jnp.concatenate(gather_plane(act_own))
    pair = jnp.dot(act_ffn, full_pair, preferred_element_type=F32)
    gate_proj, up_proj = pair[:, :local], pair[:, local:]
    sigmoid_gate = jax.nn.sigmoid(gate_proj)
    silu_gate = gate_proj * sigmoid_gate
    hidden = (silu_gate * up_proj).astype(BF16)
    half = 4 * rows
    far_out = jnp.dot(hidden[half:], full_down, preferred_element_type=F32).astype(BF16)
    near_out = jnp.dot(hidden[:half], full_down, preferred_element_type=F32).astype(BF16)
    block_out = middle + scatter_plane(near_out, far_out)

    grad_down = lax.dot_general(hidden, top_all, TN, preferred_element_type=F32)
    sum_down = ring_scatter(
        grad_down.astype(BF16).reshape(planes, pad_down, width), z, planes
    )
    sum_down = sum_down[:half_down].astype(BF16)
    down_halves = absolute([sum_down, hop(sum_down, 1)], y)
    sum_down = jnp.concatenate(down_halves).astype(F32)

    grad_hidden = lax.dot_general(top_all, full_down, NT, preferred_element_type=F32)
    grad_gate = grad_hidden * up_proj * sigmoid_gate * (1.0 + gate_proj * (1.0 - sigmoid_gate))
    grad_up = grad_hidden * silu_gate
    grad_pair = jnp.concatenate([grad_gate.astype(BF16), grad_up.astype(BF16)], axis=1)
    far_act = lax.dot_general(grad_pair[half:], full_pair, NT, preferred_element_type=F32)
    near_act = lax.dot_general(grad_pair[:half], full_pair, NT, preferred_element_type=F32)
    grad_act = scatter_plane(near_act.astype(BF16), far_act.astype(BF16))
    grad_both = lax.dot_general(act_ffn, grad_pair, TN, preferred_element_type=F32)
    sum_both = ring_scatter(
        grad_both.astype(BF16).reshape(planes, 4 * own_rows, 2 * local), z, planes
    )
    sum_both = to_row_owners(sum_both)

    def whole_hidden(parts):
        split = parts.reshape(2, 2, 2, own_rows, planes, pad_down)[..., :half_down]
        split = split.transpose(3, 4, 1, 0, 2, 5)
        return split.reshape(own_rows, hidden_width).astype(F32)

    sum_gate = whole_hidden(sum_both[:, :, :local])
    sum_up = whole_hidden(sum_both[:, :, local:])

    grad_gain_ffn = jnp.sum(grad_act * base_ffn, axis=0)
    scaled_ffn = grad_act * gain_ffn
    grad_middle = (
        cotangent[0].astype(F32)
        + inv_ffn * scaled_ffn
        - middle * inv_ffn**3 * jnp.mean(scaled_ffn * middle, axis=-1, keepdims=True)
    )

    grad_branch = grad_middle.astype(BF16)

    def by_rank(value):
        columns = value.reshape(rows, 8, piece).transpose(1, 0, 2)
        return [
            lax.dynamic_index_in_dim(columns, jnp.bitwise_xor(rank, j), 0, False) for j in range(8)
        ]

    grad_attn = lax.dot_general(grad_branch, full_out, NT, preferred_element_type=F32)
    grad_heads = jnp.concatenate(exchange_plane(by_rank(grad_attn.astype(BF16))))
    grad_qkv_rows = attend_back(info, qkv, grad_heads, lse, cosine, sine, rows)

    branch_cols = jnp.concatenate(exchange_plane(by_rank(grad_branch)))
    attn_all = gather_plane(attn)
    attn_all = [
        jnp.concatenate(
            [attn_all[i][(i ^ j) * rows : ((i ^ j) + 1) * rows] for j in range(8)]
        )
        for i in range(8)
    ]
    grad_out = [
        lax.dot_general(attn_all[i], branch_cols, TN, preferred_element_type=F32).astype(BF16)
        for i in range(8)
    ]
    grad_out = jnp.concatenate(absolute(grad_out, rank))
    sum_out = ring_scatter(grad_out.reshape(planes, 4 * own_rows, piece), z, planes)
    sum_out = to_row_owners(sum_out)
    sum_out = sum_out.transpose(1, 0, 2).reshape(own_rows, width).astype(F32)

    grad_qkv = lax.dot_general(act_attn, grad_qkv_rows, TN, preferred_element_type=F32)
    sum_qkv = ring_scatter(
        grad_qkv.astype(BF16).reshape(planes, 4 * own_rows, 6 * HD), z, planes
    )
    sum_qkv = to_row_owners(sum_qkv).reshape(8, own_rows, 2, 3, HD)
    sum_qkv = sum_qkv.transpose(1, 3, 0, 2, 4).reshape(own_rows, 3 * width).astype(F32)

    far_in = lax.dot_general(grad_qkv_rows[half:], full_qkv, NT, preferred_element_type=F32)
    near_in = lax.dot_general(grad_qkv_rows[:half], full_qkv, NT, preferred_element_type=F32)
    grad_act_attn = scatter_plane(near_in.astype(BF16), far_in.astype(BF16))
    grad_gain_attn = jnp.sum(grad_act_attn * (inputs * inv_attn), axis=0)
    scaled_attn = grad_act_attn * gain_attn
    grad_tokens = (
        grad_middle
        + inv_attn * scaled_attn
        - inputs * inv_attn**3 * jnp.mean(scaled_attn * inputs, axis=-1, keepdims=True)
    )
    sum_gains = lax.psum(jnp.stack([grad_gain_attn, grad_gain_ffn]), ("y", "z", "x", "c"))
    sum_gains = lax.dynamic_slice_in_dim(sum_gains, (4 * z + shard) * own_rows, own_rows, 1)
    return (
        block_out.astype(BF16)[None],
        grad_tokens[None],
        sum_gains[0],
        sum_qkv,
        sum_out,
        sum_gains[1],
        sum_gate,
        sum_up,
        sum_down,
    )


def solution(mesh):
    shards = mesh.shape["fsdp"]
    planes = shards // 4
    grid = Mesh(mesh.devices.reshape(2, planes, 2, 2), ("y", "z", "x", "c"))
    fsdp = ("z", "x", "c")
    by_token = P(fsdp, "y", None)
    by_row = P(fsdp, None)
    return jax.shard_map(
        functools.partial(on_device, (planes, shards)),
        mesh=grid,
        in_specs=(
            by_token,
            P(),
            P(fsdp),
            by_row,
            by_row,
            P(fsdp),
            by_row,
            by_row,
            by_row,
            by_token,
        ),
        out_specs=(
            by_token,
            by_token,
            P(fsdp),
            by_row,
            by_row,
            P(fsdp),
            by_row,
            by_row,
            by_row,
        ),
        check_vma=False,
    )
```

time: 2610 us -> 1140 us (0.44)
  waiting for transfers between devices: 2020 us -> 501 us
  local copies, waits for them, and re-layouts: 76.2 us -> 213 us
  matrix products: 249 us -> 143 us
  Pallas kernels: 0 us -> 38.3 us
  blocking collectives: 96.8 us -> 59.8 us
    reduce_scatter x8 -> x0, waiting for transfers between devices: 1210 us -> none  [the longest x2 332 us: reduce_grads(): lax.psum_scatter(first_grad.astype(jnp.bfloat16), 'seq', scatter_dimensio...]
    ppermute x8 -> x114, waiting for transfers between devices: 0.02 us -> 501 us  [the longest x90 302 us: hop(): return lax.ppermute(block, axes, [(i, last - i) for i in range(last + 1)])]
    all_gather x9 -> x0, waiting for transfers between devices: 374 us -> none  [the longest x1 106 us: on_device(): lax.all_gather(weight_qkv, 'fsdp', axis=0, tiled=True)]
    unnamed x23 -> x0, waiting for transfers between devices: 320 us -> none
    all_to_all x8 -> x0, waiting for transfers between devices: 118 us -> none  [the longest x1 26 us: on_device(): lax.all_to_all(grad_attn, 'seq', split_axis=1, concat_axis=0, tiled=True)]
    dot_general x21 -> x22, matrix products: 249 us -> 143 us  [the longest x1 17.7 us: on_device(): pair = jnp.dot(act_ffn, full_pair, preferred_element_type=F32)]
    unnamed x73 -> x325, local copies, waits for them, and re-layouts: 22.3 us -> 117 us
    all_gather x4 -> x1, blocking collectives: 91.7 us -> 21.6 us  [on_device(): lax.all_gather(jnp.stack([norm_attn, norm_ffn]), ('z', 'x', 'c'), axis=1,...]
  transfers between devices with their start and end apart: 36 -> 114, of which waited for: 25 -> 46; matrix products, arithmetic and copies ran while one was open for 13% -> 32% of each run, Pallas kernels for 0% -> 3%
where the time goes in v1:
time: 1140 us; the launch traced here: 1130 us
  waiting for transfers between devices  501 us (44%)
  local copies, waits for them, and re-layouts  213 us (19%)
  matrix products  143 us (13%)
  other arithmetic  83.6 us (7%)
  starting transfers between devices  82 us (7%)
  blocking collectives  59.8 us (5%)
  Pallas kernels  38.3 us (3%)
    ppermute x90, waiting for transfers between devices, hop(): return lax.ppermute(block, axes, [(i, last - i) for i in range(last + 1)])  302 us
    ppermute x24, waiting for transfers between devices, ring_hop(): lax.ppermute(block, 'z', [(ring[i], ring[(i + 1) % size]) for i in range(...  199 us
    unnamed x325, local copies, waits for them, and re-layouts  117 us
    ppermute x90, starting transfers between devices, hop(): return lax.ppermute(block, axes, [(i, last - i) for i in range(last + 1)])  63.9 us
    psum x1, blocking collectives, on_device(): lax.psum(jnp.stack([grad_gain_attn, grad_gain_ffn]), ('y', 'z', 'x', 'c'))  38.1 us
    another operation x4, other arithmetic  27.1 us
  transfers between devices with their start and end apart: 114, of which 46 were waited for; matrix products, arithmetic and copies ran while one was open for 32% of the time, Pallas kernels for 3%

profile of v1, /device:TPU:0, one launch (start us, length us, event | category | flops | bytes accessed | tf_op | source)
XLA Modules:
  0.0 1130.6 jit_solution(14062671912591302500)
XLA Ops:
  24.7 21.6 %all_gather.3 = bf16[2,2048]{1,0:T(2,128)(2,1)S(1)} all-gather(bf16[2,128]{1,0:T(2,128)(2,1)S(1)} %pad_maximum_fusion.14), channel_id=1, replica_groups=mesh['y'=2,'z'=4,'x'=2,'c'=2] {'z','x','c'}, dimensions={1}, use_global_device_ids=true | all-gather | bytes 8704 | tf_op jit(solution)/shard_map/all_gather | solution.py:345
  120.1 10.9 collective-permute-done.24
  135.2 20.6 %collective-permute-done.25 = bf16[512,256]{1,0:T(8,128)(2,1)S(1)} collective-permute-done((bf16[512,256]{1,0:T(8,128)(2,1)S(1)}, bf16[512,256]{1,0:T(8,128)(2,1)S(1)}, u32[]{:S(2)}, u32[]{:S(2)}) %collective-permute-start.25) | collective-permute-done | bytes 262176 | tf_op jit(solution)/shard_map/ppermute | solution.py:66
  166.7 17.8 %collective-permute-done.53 = bf16[256,2048]{1,0:T(8,128)(2,1)} collective-permute-done((bf16[256,2048]{1,0:T(8,128)(2,1)S(1)}, bf16[256,2048]{1,0:T(8,128)(2,1)}, u32[]{:S(2)}, u32[]{:S(2)}) %collective-permute-start.53) | collective-permute-done | bytes 1048608 | tf_op jit(solution)/shard_map/ppermute | solution.py:29
  190.7 17.7 %collective-permute-done.55 = bf16[256,2048]{1,0:T(8,128)(2,1)} collective-permute-done((bf16[256,2048]{1,0:T(8,128)(2,1)S(1)}, bf16[256,2048]{1,0:T(8,128)(2,1)}, u32[]{:S(2)}, u32[]{:S(2)}) %collective-permute-start.55) | collective-permute-done | bytes 1048608 | tf_op jit(solution)/shard_map/ppermute | solution.py:29
  221.3 12.6 %collective-permute-done.11 = bf16[512,768]{1,0:T(8,128)(2,1)} collective-permute-done((bf16[512,768]{1,0:T(8,128)(2,1)S(1)}, bf16[512,768]{1,0:T(8,128)(2,1)}, u32[]{:S(2)}, u32[]{:S(2)}) %collective-permute-start.11) | collective-permute-done | bytes 786464 | tf_op jit(solution)/shard_map/ppermute | solution.py:66
  241.3 17.8 %collective-permute-done.28 = bf16[2048,256]{1,0:T(8,128)(2,1)} collective-permute-done((bf16[2048,256]{1,0:T(8,128)(2,1)}, bf16[2048,256]{1,0:T(8,128)(2,1)}, u32[]{:S(2)}, u32[]{:S(2)}) %collective-permute-start.28) | collective-permute-done | bytes 1048608 | tf_op jit(solution)/shard_map/ppermute | solution.py:29
  285.3 14.8 %collective-permute-done.12 = bf16[512,768]{1,0:T(8,128)(2,1)} collective-permute-done((bf16[512,768]{1,0:T(8,128)(2,1)}, bf16[512,768]{1,0:T(8,128)(2,1)}, u32[]{:S(2)}, u32[]{:S(2)}) %collective-permute-start.12) | collective-permute-done | bytes 786464 | tf_op jit(solution)/shard_map/ppermute | solution.py:66
  311.7 16.3 %attend.1 = (bf16[2048,768]{1,0:T(8,128)(2,1)}, bf16[2048,256]{1,0:T(8,128)(2,1)S(1)}, f32[2,2048,1]{2,1,0:T(8,128)S(1)}) custom-call(s32[2]{0:T(128)S(1)} %pad_add_fusion.info, f32[2048,768]{1,0:T(8,128)} %fusion.13.proj, f32[2048,128]{1,0:T(8,128)S(1)} %pad_maximum_fusion.5.cosine, f32[2048,128]{1,0:T(8,128)S(1)} %pad_maximum_fusion.6.sine), custom_call_target="tpu_custom_call" | custom-call | tf_op jit(solution)/shard_map/attend/pallas_call | solution.py:165
  391.7 21.6 %collective-permute-done.91 = bf16[2048,256]{1,0:T(8,128)(2,1)S(1)} collective-permute-done((bf16[2048,256]{1,0:T(8,128)(2,1)S(1)}, bf16[2048,256]{1,0:T(8,128)(2,1)S(1)}, u32[]{:S(2)}, u32[]{:S(2)}) %collective-permute-start.91) | collective-permute-done | bytes 1048608 | tf_op jit(solution)/shard_map/ppermute | solution.py:29
  416.6 19.1 %collective-permute-done.33 = bf16[256,2048]{1,0:T(8,128)(2,1)S(1)} collective-permute-done((bf16[256,2048]{1,0:T(8,128)(2,1)S(1)}, bf16[256,2048]{1,0:T(8,128)(2,1)S(1)}, u32[]{:S(2)}, u32[]{:S(2)}) %collective-permute-start.33) | collective-permute-done | bytes 1048608 | tf_op jit(solution)/shard_map/ppermute | solution.py:29
  435.9 21.2 %collective-permute-done.35 = bf16[256,2048]{1,0:T(8,128)(2,1)S(1)} collective-permute-done((bf16[256,2048]{1,0:T(8,128)(2,1)S(1)}, bf16[256,2048]{1,0:T(8,128)(2,1)S(1)}, u32[]{:S(2)}, u32[]{:S(2)}) %collective-permute-start.35) | collective-permute-done | bytes 1048608 | tf_op jit(solution)/shard_map/ppermute | solution.py:29
  475.7 17.7 %fusion.113 = f32[2048,1408]{0,1:T(8,128)} fusion(bf16[2048,2048]{1,0:T(8,128)(2,1)} %copy-done.58, bf16[2048,1408]{1,0:T(8,128)(2,1)S(1)} %bitcast.445), kind=kOutput, calls=%fused_computation.454 | convolution fusion | flops 11811160064 | bytes 25690112 | tf_op jit(solution)/shard_map/dot_general | solution.py:376
  493.4 16.8 %multiply_convert_fusion = (bf16[2048,704]{0,1:T(8,128)(2,1)}, bf16[2048,704]{0,1:T(8,128)(2,1)}, bf16[2048,704]{0,1:T(8,128)(2,1)S(1)}) fusion(f32[2048,1408]{0,1:T(8,128)} %fusion.113, bf16[2048,2048]{1,0:T(8,128)(2,1)} %constant_dynamic-update-slice_fusion.32, bf16[704,2048]{1,0:T(8,128)(2,1)} %bitcast.100), kind=kOutput, calls=%fused_computation.15 | convolution fusion | flops 5927206912 | bytes 31457280 | tf_op jit(solution)/shard_map/dot_general | solution.py:394
  520.0 17.2 %convolution_convert_fusion = bf16[2048,1408]{1,0:T(8,128)(2,1)S(1)} fusion(bf16[2048,2048]{1,0:T(8,128)(2,1)} %copy-done.58, bf16[2048,704]{0,1:T(8,128)(2,1)} %get-tuple-element.64, bf16[2048,704]{0,1:T(8,128)(2,1)} %get-tuple-element.65), kind=kOutput, calls=%fused_computation.9 | convolution fusion | flops 11825577984 | bytes 19922944 | tf_op jit(solution)/shard_map/dot_general | solution.py:401
  537.3 12.1 %convolution_convert_fusion.1 = bf16[1024,2048]{1,0:T(8,128)(2,1)S(1)} fusion(bf16[2048,1408]{1,0:T(8,128)(2,1)} %bitcast.446, bf16[2048,704]{0,1:T(8,128)(2,1)} %get-tuple-element.65, bf16[2048,704]{0,1:T(8,128)(2,1)} %get-tuple-element.64), kind=kOutput, calls=%fused_computation.28 | convolution fusion | flops 5913444352 | bytes 15728640 | tf_op jit(solution)/shard_map/dot_general | solution.py:398
  552.8 11.6 %fusion.5 = bf16[1024,2048]{1,0:T(8,128)(2,1)} fusion(bf16[2048,1408]{1,0:T(8,128)(2,1)} %bitcast.447, bf16[2048,704]{0,1:T(8,128)(2,1)} %get-tuple-element.65, bf16[2048,704]{0,1:T(8,128)(2,1)} %get-tuple-element.64), kind=kOutput, calls=%fused_computation.38 | convolution fusion | flops 5911347200 | bytes 15728640 | tf_op jit(solution)/shard_map/dot_general | solution.py:399
  564.4 35.9 %collective-permute-done.111 = bf16[176,2048]{1,0:T(8,128)(2,1)S(1)} collective-permute-done((bf16[176,2048]{1,0:T(8,128)(2,1)S(1)}, bf16[176,2048]{1,0:T(8,128)(2,1)S(1)}, u32[]{:S(2)}, u32[]{:S(2)}) %collective-permute-start.111) | collective-permute-done | bytes 720928 | tf_op jit(solution)/shard_map/ppermute | solution.py:66
  638.1 12.2 %collective-permute-done.104 = bf16[512,1408]{1,0:T(8,128)(2,1)S(1)} collective-permute-done((bf16[512,1408]{1,0:T(8,128)(2,1)S(1)}, bf16[512,1408]{1,0:T(8,128)(2,1)S(1)}, u32[]{:S(2)}, u32[]{:S(2)}) %collective-permute-start.104) | collective-permute-done | bytes 1441824 | tf_op jit(solution)/shard_map/ppermute | solution.py:66
  665.4 19.2 %collective-permute-done.105 = bf16[512,1408]{1,0:T(8,128)(2,1)S(1)} collective-permute-done((bf16[512,1408]{1,0:T(8,128)(2,1)S(1)}, bf16[512,1408]{1,0:T(8,128)(2,1)S(1)}, u32[]{:S(2)}, u32[]{:S(2)}) %collective-permute-start.105) | collective-permute-done | bytes 1441824 | tf_op jit(solution)/shard_map/ppermute | solution.py:66
  697.1 17.2 %collective-permute-done.108 = bf16[128,1408]{1,0:T(8,128)(2,1)S(1)} collective-permute-done((bf16[128,1408]{1,0:T(8,128)(2,1)S(1)}, bf16[128,1408]{1,0:T(8,128)(2,1)S(1)}, u32[]{:S(2)}, u32[]{:S(2)}) %collective-permute-start.108) | collective-permute-done | bytes 360480 | tf_op jit(solution)/shard_map/ppermute | solution.py:29
  734.9 14.3 %collective-permute-done.52 = bf16[256,2048]{1,0:T(8,128)(2,1)S(1)} collective-permute-done((bf16[256,2048]{1,0:T(8,128)(2,1)S(1)}, bf16[256,2048]{1,0:T(8,128)(2,1)S(1)}, u32[]{:S(2)}, u32[]{:S(2)}) %collective-permute-start.52) | collective-permute-done | bytes 1048608 | tf_op jit(solution)/shard_map/ppermute | solution.py:29
  749.2 21.3 %collective-permute-done.51 = bf16[256,2048]{1,0:T(8,128)(2,1)S(1)} collective-permute-done((bf16[256,2048]{1,0:T(8,128)(2,1)S(1)}, bf16[256,2048]{1,0:T(8,128)(2,1)S(1)}, u32[]{:S(2)}, u32[]{:S(2)}) %collective-permute-start.51) | collective-permute-done | bytes 1048608 | tf_op jit(solution)/shard_map/ppermute | solution.py:29
  793.2 15.4 %collective-permute-done.64 = bf16[256,256]{1,0:T(8,128)(2,1)S(1)} collective-permute-done((bf16[256,256]{1,0:T(8,128)(2,1)S(1)}, bf16[256,256]{1,0:T(8,128)(2,1)S(1)}, u32[]{:S(2)}, u32[]{:S(2)}) %collective-permute-start.64) | collective-permute-done | bytes 131104 | tf_op jit(solution)/shard_map/ppermute | solution.py:29
  818.9 22.1 %attend_back.1 = bf16[2048,768]{1,0:T(8,128)(2,1)} custom-call(s32[2]{0:T(128)S(1)} %pad_add_fusion.info, bf16[2048,768]{1,0:T(8,128)(2,1)} %get-tuple-element.13.qkv, bf16[2048,256]{1,0:T(8,128)(2,1)S(1)} %constant_dynamic-update-slice_fusion.40.grad, f32[2,2048,1]{2,1,0:T(8,128)S(1)} %get-tuple-element.14.lse, f32[2048,128]{1,0:T(8,128)S(1)} %pad_maximum_fusion.5.cosine, ...), custom_call_target="tpu_custom_call" | custom-call | tf_op jit(solution)/shard_map/attend_back/pallas_call | solution.py:246
  841.0 11.3 convolution_convert_fusion.4
  898.2 13.6 %collective-permute-done.98 = bf16[512,256]{1,0:T(8,128)(2,1)S(1)} collective-permute-done((bf16[512,256]{1,0:T(8,128)(2,1)S(1)}, bf16[512,256]{1,0:T(8,128)(2,1)S(1)}, u32[]{:S(2)}, u32[]{:S(2)}) %collective-permute-start.98) | collective-permute-done | bytes 262176 | tf_op jit(solution)/shard_map/ppermute | solution.py:66
  951.4 14.0 %collective-permute-done.76 = bf16[512,768]{1,0:T(8,128)(2,1)S(1)} collective-permute-done((bf16[512,768]{1,0:T(8,128)(2,1)S(1)}, bf16[512,768]{1,0:T(8,128)(2,1)S(1)}, u32[]{:S(2)}, u32[]{:S(2)}) %collective-permute-start.76) | collective-permute-done | bytes 786464 | tf_op jit(solution)/shard_map/ppermute | solution.py:66
  965.7 18.7 %collective-permute-done.77 = bf16[512,768]{1,0:T(8,128)(2,1)S(1)} collective-permute-done((bf16[512,768]{1,0:T(8,128)(2,1)S(1)}, bf16[512,768]{1,0:T(8,128)(2,1)S(1)}, u32[]{:S(2)}, u32[]{:S(2)}) %collective-permute-start.77) | collective-permute-done | bytes 786464 | tf_op jit(solution)/shard_map/ppermute | solution.py:66
  1000.7 16.4 %collective-permute-done.81 = bf16[4,128,768]{2,1,0:T(8,128)(2,1)} collective-permute-done((bf16[4,128,768]{2,1,0:T(8,128)(2,1)}, bf16[4,128,768]{2,1,0:T(8,128)(2,1)}, u32[]{:S(2)}, u32[]{:S(2)}) %collective-permute-start.81) | collective-permute-done | bytes 786464 | tf_op jit(solution)/shard_map/ppermute | solution.py:29
  1062.0 21.0 %collective-permute-done.73 = bf16[256,2048]{1,0:T(8,128)(2,1)} collective-permute-done((bf16[256,2048]{1,0:T(8,128)(2,1)}, bf16[256,2048]{1,0:T(8,128)(2,1)}, u32[]{:S(2)}, u32[]{:S(2)}) %collective-permute-start.73) | collective-permute-done | bytes 1048608 | tf_op jit(solution)/shard_map/ppermute | solution.py:29
  1087.5 38.1 %psum.7 = f32[2,2048]{1,0:T(2,128)S(1)} all-reduce(f32[2,2048]{1,0:T(2,128)S(1)} %pad_maximum_fusion.13), channel_id=1, replica_groups=mesh['y'=2,'z'=4,'x'=2,'c'=2] {'y','z','x','c'}, use_global_device_ids=true, to_apply=%region_6.7 | all-reduce | flops 4096 | bytes 32768 | tf_op jit(solution)/shard_map/psum | solution.py:469
  (694 shorter events, 543.5 us)
Async XLA Ops:
  8.4 81.8 %collective-permute-start.9 = (bf16[128,768]{0,1:T(8,128)(2,1)}, bf16[128,768]{0,1:T(8,128)(2,1)}, u32[]{:S(2)}, u32[]{:S(2)}) collective-permute-start(bf16[128,768]{0,1:T(8,128)(2,1)} %get-tuple-element.86), channel_id=1, source_target_pairs={{0,3},{1,2},{2,1},{3,0},{4,7},{5,6},{6,5},{7,4},{8,11},{9,10},{10,... | collective-permute-start | bytes 589832 | tf_op jit(solution)/shard_map/ppermute | solution.py:29
  10.7 81.0 %collective-permute-start.8 = (bf16[128,768]{0,1:T(8,128)(2,1)}, bf16[128,768]{0,1:T(8,128)(2,1)}, u32[]{:S(2)}, u32[]{:S(2)}) collective-permute-start(bf16[128,768]{0,1:T(8,128)(2,1)} %get-tuple-element.87), channel_id=1, source_target_pairs={{0,2},{2,0},{1,3},{3,1},{4,6},{6,4},{5,7},{7,5},{8,10},{10,8},{9,1... | collective-permute-start | bytes 589832 | tf_op jit(solution)/shard_map/ppermute | solution.py:29
  14.1 70.8 %collective-permute-start.22 = (bf16[128,256]{1,0:T(8,128)(2,1)}, bf16[128,256]{1,0:T(8,128)(2,1)}, u32[]{:S(2)}, u32[]{:S(2)}) collective-permute-start(bf16[128,256]{1,0:T(8,128)(2,1)} %bitcast.49), channel_id=1, source_target_pairs={{0,3},{1,2},{2,1},{3,0},{4,7},{5,6},{6,5},{7,4},{8,11},{9,10},{10,... | collective-permute-start | bytes 196616 | tf_op jit(solution)/shard_map/ppermute | solution.py:29
  16.3 68.9 %collective-permute-start.21 = (bf16[128,256]{1,0:T(8,128)(2,1)}, bf16[128,256]{1,0:T(8,128)(2,1)}, u32[]{:S(2)}, u32[]{:S(2)}) collective-permute-start(bf16[128,256]{1,0:T(8,128)(2,1)} %bitcast.47), channel_id=1, source_target_pairs={{0,2},{2,0},{1,3},{3,1},{4,6},{6,4},{5,7},{7,5},{8,10},{10,8},{9,1... | collective-permute-start | bytes 196616 | tf_op jit(solution)/shard_map/ppermute | solution.py:29
  17.2 69.5 %collective-permute-start.20 = (bf16[128,256]{1,0:T(8,128)(2,1)}, bf16[128,256]{1,0:T(8,128)(2,1)}, u32[]{:S(2)}, u32[]{:S(2)}) collective-permute-start(bf16[128,256]{1,0:T(8,128)(2,1)} %bitcast.45), channel_id=1, source_target_pairs={{0,1},{1,0},{2,3},{3,2},{4,5},{5,4},{6,7},{7,6},{8,9},{9,8},{10,11... | collective-permute-start | bytes 196616 | tf_op jit(solution)/shard_map/ppermute | solution.py:29
  85.2 75.3 %collective-permute-start = (bf16[256,2048]{1,0:T(8,128)(2,1)S(1)}, bf16[256,2048]{1,0:T(8,128)(2,1)}, u32[]{:S(2)}, u32[]{:S(2)}) collective-permute-start(bf16[256,2048]{1,0:T(8,128)(2,1)S(1)} %bitcast.434), channel_id=1, source_target_pairs={{0,16},{16,0},{1,17},{17,1},{2,18},{18,2},{3,19},{19,3},{4,20},{20... | collective-permute-start | bytes 3145736 | tf_op jit(solution)/shard_map/ppermute | solution.py:29
  102.9 59.8 %collective-permute-start.1 = (bf16[256,2048]{1,0:T(8,128)(2,1)S(1)}, bf16[256,2048]{1,0:T(8,128)(2,1)}, u32[]{:S(2)}, u32[]{:S(2)}) collective-permute-start(bf16[256,2048]{1,0:T(8,128)(2,1)S(1)} %bitcast.435), channel_id=1, source_target_pairs={{0,2},{2,0},{1,3},{3,1},{4,6},{6,4},{5,7},{7,5},{8,10},{10,8},{9,1... | collective-permute-start | bytes 3145736 | tf_op jit(solution)/shard_map/ppermute | solution.py:29
  105.2 60.0 %collective-permute-start.2 = (bf16[256,2048]{1,0:T(8,128)(2,1)S(1)}, bf16[256,2048]{1,0:T(8,128)(2,1)}, u32[]{:S(2)}, u32[]{:S(2)}) collective-permute-start(bf16[256,2048]{1,0:T(8,128)(2,1)S(1)} %bitcast.436), channel_id=1, source_target_pairs={{0,18},{2,16},{16,2},{18,0},{1,19},{3,17},{17,3},{19,1},{4,22},{6,... | collective-permute-start | bytes 3145736 | tf_op jit(solution)/shard_map/ppermute | solution.py:29
  162.7 45.8 %collective-permute-start.55 = (bf16[256,2048]{1,0:T(8,128)(2,1)S(1)}, bf16[256,2048]{1,0:T(8,128)(2,1)}, u32[]{:S(2)}, u32[]{:S(2)}) collective-permute-start(bf16[256,2048]{1,0:T(8,128)(2,1)S(1)} %bitcast.457), channel_id=1, source_target_pairs={{0,18},{2,16},{16,2},{18,0},{1,19},{3,17},{17,3},{19,1},{4,22},{6,... | collective-permute-start | bytes 3145736 | tf_op jit(solution)/shard_map/ppermute | solution.py:29
  165.2 45.7 %collective-permute-start.56 = (bf16[256,2048]{1,0:T(8,128)(2,1)S(1)}, bf16[256,2048]{1,0:T(8,128)(2,1)S(1)}, u32[]{:S(2)}, u32[]{:S(2)}) collective-permute-start(bf16[256,2048]{1,0:T(8,128)(2,1)S(1)} %bitcast.458), channel_id=1, source_target_pairs={{0,1},{1,0},{2,3},{3,2},{4,5},{5,4},{6,7},{7,6},{8,9},{9,8},{10,11... | collective-permute-start | bytes 3145736 | tf_op jit(solution)/shard_map/ppermute | solution.py:29
  166.6 68.5 %collective-permute-start.43 = (bf16[512,1408]{1,0:T(8,128)(2,1)S(1)}, bf16[512,1408]{1,0:T(8,128)(2,1)}, u32[]{:S(2)}, u32[]{:S(2)}) collective-permute-start(bf16[512,1408]{1,0:T(8,128)(2,1)S(1)} %pad_maximum_fusion.3), channel_id=1, source_target_pairs={{0,4},{4,12},{12,8},{8,0},{1,5},{5,13},{13,9},{9,1},{2,6},{6,14},{... | collective-permute-start | bytes 4325384 | tf_op jit(solution)/shard_map/ppermute | solution.py:66
  186.9 50.4 %collective-permute-start.26 = (bf16[2048,256]{1,0:T(8,128)(2,1)}, bf16[2048,256]{1,0:T(8,128)(2,1)S(1)}, u32[]{:S(2)}, u32[]{:S(2)}) collective-permute-start(bf16[2048,256]{1,0:T(8,128)(2,1)} %bitcast.60), channel_id=1, source_target_pairs={{0,16},{16,0},{1,17},{17,1},{2,18},{18,2},{3,19},{19,3},{4,20},{20... | collective-permute-start | bytes 3145736 | tf_op jit(solution)/shard_map/ppermute | solution.py:29
  267.3 121.6 %collective-permute-start.44 = (bf16[512,1408]{1,0:T(8,128)(2,1)}, bf16[512,1408]{1,0:T(8,128)(2,1)}, u32[]{:S(2)}, u32[]{:S(2)}) collective-permute-start(bf16[512,1408]{1,0:T(8,128)(2,1)} %collective-permute-done.43), channel_id=1, source_target_pairs={{0,4},{4,12},{12,8},{8,0},{1,5},{5,13},{13,9},{9,1},{2,6},{6,14},{... | collective-permute-start | bytes 4325384 | tf_op jit(solution)/shard_map/ppermute | solution.py:66
  272.2 91.0 %collective-permute-start.30 = (bf16[2048,256]{1,0:T(8,128)(2,1)S(1)}, bf16[2048,256]{1,0:T(8,128)(2,1)}, u32[]{:S(2)}, u32[]{:S(2)}) collective-permute-start(bf16[2048,256]{1,0:T(8,128)(2,1)S(1)} %copy-done.43), channel_id=1, source_target_pairs={{0,1},{1,0},{2,3},{3,2},{4,5},{5,4},{6,7},{7,6},{8,9},{9,8},{10,11... | collective-permute-start | bytes 3145736 | tf_op jit(solution)/shard_map/ppermute | solution.py:29
  275.1 91.4 %collective-permute-start.31 = (bf16[2048,256]{1,0:T(8,128)(2,1)}, bf16[2048,256]{1,0:T(8,128)(2,1)}, u32[]{:S(2)}, u32[]{:S(2)}) collective-permute-start(bf16[2048,256]{1,0:T(8,128)(2,1)} %collective-permute-done.27), channel_id=1, source_target_pairs={{0,1},{1,0},{2,3},{3,2},{4,5},{5,4},{6,7},{7,6},{8,9},{9,8},{10,11... | collective-permute-start | bytes 3145736 | tf_op jit(solution)/shard_map/ppermute | solution.py:29
  283.2 88.2 %collective-permute-start.32 = (bf16[2048,256]{1,0:T(8,128)(2,1)}, bf16[2048,256]{1,0:T(8,128)(2,1)}, u32[]{:S(2)}, u32[]{:S(2)}) collective-permute-start(bf16[2048,256]{1,0:T(8,128)(2,1)} %collective-permute-done.28), channel_id=1, source_target_pairs={{0,1},{1,0},{2,3},{3,2},{4,5},{5,4},{6,7},{7,6},{8,9},{9,8},{10,11... | collective-permute-start | bytes 3145736 | tf_op jit(solution)/shard_map/ppermute | solution.py:29
  363.2 50.5 %collective-permute-start.90 = (bf16[2048,256]{1,0:T(8,128)(2,1)S(1)}, bf16[2048,256]{1,0:T(8,128)(2,1)S(1)}, u32[]{:S(2)}, u32[]{:S(2)}) collective-permute-start(bf16[2048,256]{1,0:T(8,128)(2,1)S(1)} %get-tuple-element.12), channel_id=1, source_target_pairs={{0,2},{2,0},{1,3},{3,1},{4,6},{6,4},{5,7},{7,5},{8,10},{10,8},{9,1... | collective-permute-start | bytes 3145736 | tf_op jit(solution)/shard_map/ppermute | solution.py:29
  366.5 46.8 %collective-permute-start.91 = (bf16[2048,256]{1,0:T(8,128)(2,1)S(1)}, bf16[2048,256]{1,0:T(8,128)(2,1)S(1)}, u32[]{:S(2)}, u32[]{:S(2)}) collective-permute-start(bf16[2048,256]{1,0:T(8,128)(2,1)S(1)} %get-tuple-element.12), channel_id=1, source_target_pairs={{0,18},{2,16},{16,2},{18,0},{1,19},{3,17},{17,3},{19,1},{4,22},{6,... | collective-permute-start | bytes 3145736 | tf_op jit(solution)/shard_map/ppermute | solution.py:29
  388.9 46.8 %collective-permute-start.33 = (bf16[256,2048]{1,0:T(8,128)(2,1)S(1)}, bf16[256,2048]{1,0:T(8,128)(2,1)S(1)}, u32[]{:S(2)}, u32[]{:S(2)}) collective-permute-start(bf16[256,2048]{1,0:T(8,128)(2,1)S(1)} %get-tuple-element.63), channel_id=1, source_target_pairs={{0,16},{16,0},{1,17},{17,1},{2,18},{18,2},{3,19},{19,3},{4,20},{20... | collective-permute-start | bytes 3145736 | tf_op jit(solution)/shard_map/ppermute | solution.py:29
  390.6 45.2 %collective-permute-start.34 = (bf16[256,2048]{1,0:T(8,128)(2,1)S(1)}, bf16[256,2048]{1,0:T(8,128)(2,1)S(1)}, u32[]{:S(2)}, u32[]{:S(2)}) collective-permute-start(bf16[256,2048]{1,0:T(8,128)(2,1)S(1)} %get-tuple-element.63), channel_id=1, source_target_pairs={{0,2},{2,0},{1,3},{3,1},{4,6},{6,4},{5,7},{7,5},{8,10},{10,8},{9,1... | collective-permute-start | bytes 3145736 | tf_op jit(solution)/shard_map/ppermute | solution.py:29
  549.5 101.7 %collective-permute-start.60 = (bf16[1024,2048]{1,0:T(8,128)(2,1)S(1)}, bf16[1024,2048]{1,0:T(8,128)(2,1)}, u32[]{:S(2)}, u32[]{:S(2)}) collective-permute-start(bf16[1024,2048]{1,0:T(8,128)(2,1)S(1)} %convolution_convert_fusion.1), channel_id=1, source_target_pairs={{0,1},{1,0},{2,3},{3,2},{4,5},{5,4},{6,7},{7,6},{8,9},{9,8},{10,11... | collective-permute-start | bytes 12582920 | tf_op jit(solution)/shard_map/ppermute | solution.py:29
  549.7 59.6 %collective-permute-start.103 = (bf16[512,1408]{1,0:T(8,128)(2,1)S(1)}, bf16[512,1408]{1,0:T(8,128)(2,1)S(1)}, u32[]{:S(2)}, u32[]{:S(2)}) collective-permute-start(bf16[512,1408]{1,0:T(8,128)(2,1)S(1)} %dynamic-slice_bitcast_fusion), channel_id=1, source_target_pairs={{0,4},{4,12},{12,8},{8,0},{1,5},{5,13},{13,9},{9,1},{2,6},{6,14},{... | collective-permute-start | bytes 4325384 | tf_op jit(solution)/shard_map/ppermute | solution.py:66
  552.0 48.3 %collective-permute-start.111 = (bf16[176,2048]{1,0:T(8,128)(2,1)S(1)}, bf16[176,2048]{1,0:T(8,128)(2,1)S(1)}, u32[]{:S(2)}, u32[]{:S(2)}) collective-permute-start(bf16[176,2048]{1,0:T(8,128)(2,1)S(1)} %fusion.40), channel_id=1, source_target_pairs={{0,4},{4,12},{12,8},{8,0},{1,5},{5,13},{13,9},{9,1},{2,6},{6,14},{... | collective-permute-start | bytes 2162696 | tf_op jit(solution)/shard_map/ppermute | solution.py:66
  609.3 78.1 %collective-permute-start.49 = (bf16[1024,2048]{1,0:T(8,128)(2,1)}, bf16[1024,2048]{1,0:T(8,128)(2,1)}, u32[]{:S(2)}, u32[]{:S(2)}) collective-permute-start(bf16[1024,2048]{1,0:T(8,128)(2,1)} %convolution_convert_fusion.2), channel_id=1, source_target_pairs={{0,1},{1,0},{2,3},{3,2},{4,5},{5,4},{6,7},{7,6},{8,9},{9,8},{10,11... | collective-permute-start | bytes 12582920 | tf_op jit(solution)/shard_map/ppermute | solution.py:29
  661.9 64.8 %collective-permute-start.63 = (bf16[256,2048]{1,0:T(8,128)(2,1)}, bf16[256,2048]{1,0:T(8,128)(2,1)}, u32[]{:S(2)}, u32[]{:S(2)}) collective-permute-start(bf16[256,2048]{1,0:T(8,128)(2,1)} %get-tuple-element.71), channel_id=1, source_target_pairs={{0,18},{2,16},{16,2},{18,0},{1,19},{3,17},{17,3},{19,1},{4,22},{6,... | collective-permute-start | bytes 3145736 | tf_op jit(solution)/shard_map/ppermute | solution.py:29
  662.3 68.6 %collective-permute-start.62 = (bf16[256,2048]{1,0:T(8,128)(2,1)}, bf16[256,2048]{1,0:T(8,128)(2,1)}, u32[]{:S(2)}, u32[]{:S(2)}) collective-permute-start(bf16[256,2048]{1,0:T(8,128)(2,1)} %get-tuple-element.72), channel_id=1, source_target_pairs={{0,2},{2,0},{1,3},{3,1},{4,6},{6,4},{5,7},{7,5},{8,10},{10,8},{9,1... | collective-permute-start | bytes 3145736 | tf_op jit(solution)/shard_map/ppermute | solution.py:29
  663.4 67.6 %collective-permute-start.61 = (bf16[256,2048]{1,0:T(8,128)(2,1)}, bf16[256,2048]{1,0:T(8,128)(2,1)}, u32[]{:S(2)}, u32[]{:S(2)}) collective-permute-start(bf16[256,2048]{1,0:T(8,128)(2,1)} %get-tuple-element.70), channel_id=1, source_target_pairs={{0,16},{16,0},{1,17},{17,1},{2,18},{18,2},{3,19},{19,3},{4,20},{20... | collective-permute-start | bytes 3145736 | tf_op jit(solution)/shard_map/ppermute | solution.py:29
  726.7 45.4 %collective-permute-start.50 = (bf16[256,2048]{1,0:T(8,128)(2,1)S(1)}, bf16[256,2048]{1,0:T(8,128)(2,1)S(1)}, u32[]{:S(2)}, u32[]{:S(2)}) collective-permute-start(bf16[256,2048]{1,0:T(8,128)(2,1)S(1)} %get-tuple-element.73), channel_id=1, source_target_pairs={{0,16},{16,0},{1,17},{17,1},{2,18},{18,2},{3,19},{19,3},{4,20},{20... | collective-permute-start | bytes 3145736 | tf_op jit(solution)/shard_map/ppermute | solution.py:29
  730.9 157.1 %collective-permute-start.109 = (bf16[4,128,1408]{2,1,0:T(8,128)(2,1)S(1)}, bf16[4,128,1408]{2,1,0:T(8,128)(2,1)S(1)}, u32[]{:S(2)}, u32[]{:S(2)}) collective-permute-start(bf16[4,128,1408]{2,1,0:T(8,128)(2,1)S(1)} %pad_maximum_fusion.4), channel_id=1, source_target_pairs={{0,16},{16,0},{1,17},{17,1},{2,18},{18,2},{3,19},{19,3},{4,20},{20... | collective-permute-start | bytes 4325384 | tf_op jit(solution)/shard_map/ppermute | solution.py:29
  884.2 139.8 %collective-permute-start.71 = (bf16[1024,2048]{1,0:T(8,128)(2,1)}, bf16[1024,2048]{1,0:T(8,128)(2,1)}, u32[]{:S(2)}, u32[]{:S(2)}) collective-permute-start(bf16[1024,2048]{1,0:T(8,128)(2,1)} %convolution_convert_fusion.3), channel_id=1, source_target_pairs={{0,1},{1,0},{2,3},{3,2},{4,5},{5,4},{6,7},{7,6},{8,9},{9,8},{10,11... | collective-permute-start | bytes 12582920 | tf_op jit(solution)/shard_map/ppermute | solution.py:29
  885.2 58.7 %collective-permute-start.75 = (bf16[512,768]{1,0:T(8,128)(2,1)}, bf16[512,768]{1,0:T(8,128)(2,1)}, u32[]{:S(2)}, u32[]{:S(2)}) collective-permute-start(bf16[512,768]{1,0:T(8,128)(2,1)} %dynamic-slice_bitcast_fusion.1), channel_id=1, source_target_pairs={{0,4},{4,12},{12,8},{8,0},{1,5},{5,13},{13,9},{9,1},{2,6},{6,14},{... | collective-permute-start | bytes 2359304 | tf_op jit(solution)/shard_map/ppermute | solution.py:66
  1036.6 46.4 %collective-permute-start.73 = (bf16[256,2048]{1,0:T(8,128)(2,1)}, bf16[256,2048]{1,0:T(8,128)(2,1)}, u32[]{:S(2)}, u32[]{:S(2)}) collective-permute-start(bf16[256,2048]{1,0:T(8,128)(2,1)} %get-tuple-element.69), channel_id=1, source_target_pairs={{0,2},{2,0},{1,3},{3,1},{4,6},{6,4},{5,7},{7,5},{8,10},{10,8},{9,1... | collective-permute-start | bytes 3145736 | tf_op jit(solution)/shard_map/ppermute | solution.py:29
  (162 other events, 3613.6 us)

commit v2 on v1

v2 whole, which is shorter than its diff:
```python
import functools

import jax
import jax.numpy as jnp
from jax import lax
from jax.experimental import pallas as pl
from jax.experimental.pallas import tpu as pltpu
from jax.sharding import Mesh, PartitionSpec as P

HD = 128
WINDOW = 1024
EPS = 1e-05
NEG = -1e30
THETA = 10000.0
F32 = jnp.float32
BF16 = jnp.bfloat16
BITS = (("y", 1), ("x", 2), ("c", 4))
SHARD_TO_RANK = (0, 4, 2, 6)
NT = (((1,), (1,)), ((), ()))
TN = (((0,), (0,)), ((), ()))
VMEM_LIMIT = 56 * 2**20
RANK, BOUND, SHARD, PLANES = 0, 1, 2, 3


def shape(dims, dtype):
    return jax.ShapeDtypeStruct(tuple(dims), dtype)


def after(value, *earlier):
    return lax.optimization_barrier((value, *earlier))[0]


def call(kernel, info, grid, in_specs, out_specs, out_shape, operands, name, flops, scratch=()):
    traffic = sum(a.size * a.dtype.itemsize for a in operands)
    traffic += sum(s.size * s.dtype.itemsize for s in jax.tree.leaves(out_shape))
    cost = int(1.2e9 + 230 * traffic)
    return pl.pallas_call(
        kernel,
        grid_spec=pltpu.PrefetchScalarGridSpec(
            num_scalar_prefetch=1,
            grid=grid,
            in_specs=in_specs,
            out_specs=out_specs,
            scratch_shapes=scratch,
        ),
        out_shape=out_shape,
        compiler_params=pltpu.CompilerParams(vmem_limit_bytes=VMEM_LIMIT),
        cost_estimate=pl.CostEstimate(flops=cost, bytes_accessed=1, transcendentals=0),
        name=name,
    )(info, *operands)


def whole(array):
    dims = array.shape
    return pl.BlockSpec(dims, lambda *_: (0,) * len(dims))


def dot(a, b):
    return jnp.dot(a, b, preferred_element_type=F32)


def dot_nt(a, b):
    return lax.dot_general(a, b, NT, preferred_element_type=F32)


def dot_tn(a, b):
    return lax.dot_general(a, b, TN, preferred_element_type=F32)


def hop(block, j):
    if not j:
        return block
    axes = tuple(name for name, bit in BITS if j & bit)
    last = 2 ** len(axes) - 1
    return lax.ppermute(block, axes, [(i, last - i) for i in range(last + 1)])


def ring_of(size):
    odd = [i for i in range(size) if i % 2 == 1]
    even = [i for i in range(size) if i % 2 == 0 and i > 0]
    return [0] + odd + even[::-1]


class Order:
    def __init__(self):
        self.gate = ()

    def do(self, function, info, *operands, **options):
        result = function(after(info, *self.gate), *operands, **options)
        self.gate = (jax.tree.leaves(result)[0],)
        return result

    def need(self, *moved):
        self.gate = self.gate + moved

    def then(self, value):
        return after(value, *self.gate) if self.gate else value


class Lane:
    def __init__(self, size):
        ring = ring_of(size)
        self.size = size
        self.route = [(ring[i], ring[(i + 1) % size]) for i in range(size)]
        self.last = ()

    def hop(self, block):
        if self.last:
            block = after(block, *self.last)
        moved = lax.ppermute(block, "z", self.route)
        self.last = (moved,)
        return moved

    def gather(self, block, steps=None):
        held = block if isinstance(block, list) else [block]
        for _ in range(steps or self.size - len(held)):
            held.append(self.hop(held[-1]))
        return held


class Sum:
    def __init__(self, order, lane, chunks):
        self.order, self.lane, self.total, self.rest = order, lane, chunks[0], list(chunks[1:])

    def move(self):
        if self.rest:
            moved = self.order.then(self.lane.hop(self.total)).astype(F32)
            self.total = (moved + self.rest.pop(0).astype(F32)).astype(BF16)
            self.order.need(self.total)

    def finish(self):
        while self.rest:
            self.move()


def near_parts(block, before_y=(), before_x=(), before_halves=()):
    half = block.shape[0] // 2
    from_y = hop(after(block, *before_y), 1)
    from_x = hop(after(block, *before_x), 2)
    first, second = after((from_y[:half], from_x[half:]), *before_halves)
    return [block, from_y, from_x, hop(first, 2), hop(second, 1)]


def join_kernel(cuts, info, *refs):
    count = len(cuts)
    out, sems = refs[count], refs[count + 1]
    copies, start = [], 0
    for i, (first, rows) in enumerate(cuts):
        source = refs[i].at[pl.ds(first, rows), :]
        copies.append(pltpu.make_async_copy(source, out.at[pl.ds(start, rows), :], sems.at[i]))
        start += rows
    for copy in copies:
        copy.start()
    for copy in copies:
        copy.wait()


def join(info, *blocks):
    blocks = [b if isinstance(b, tuple) else (b, 0, b.shape[0]) for b in blocks]
    arrays = [b[0] for b in blocks]
    cuts = tuple(b[1:] for b in blocks)
    out = shape((sum(rows for _, rows in cuts), arrays[0].shape[1]), arrays[0].dtype)
    anywhere = pl.BlockSpec(memory_space=pl.ANY)
    return call(
        functools.partial(join_kernel, cuts),
        info, (1,), [anywhere] * len(arrays), whole(out), out, arrays, "join", 0,
        [pltpu.SemaphoreType.DMA((len(arrays),))],
    )


def combine_kernel(info, near, moved, own, *outs):
    own[...] = near[0].astype(F32) + moved[0].astype(F32)
    for j, out in enumerate(outs):
        out[...] = (near[j + 1].astype(F32) + moved[j + 1].astype(F32)).astype(BF16)


def combine(info, near, moved):
    near = near.reshape(4, -1, near.shape[-1])
    moved = moved.reshape(near.shape)
    rows, columns = near.shape[1:]
    part = rows // 4
    outs = [shape((rows, columns), F32)] + [shape((rows, columns), BF16)] * 3
    source = pl.BlockSpec((4, part, columns), lambda i, s: (0, i, 0))
    return call(
        combine_kernel,
        info, (4,), [source, source], [pl.BlockSpec((part, columns), lambda i, s: (i, 0))] * 4,
        outs, (near, moved), "combine", 0,
    )


def near_moves(blocks):
    return [hop(block, j) for j, block in enumerate(blocks)]


def scatter_moves(own, *terms):
    return own, [hop(term, j + 1) for j, term in enumerate(terms)]


def meet_kernel(info, near, moved, *outs):
    rows = outs[0].shape[0] // 2
    for j, out in enumerate(outs):
        out[:rows, :] = near[j * rows : (j + 1) * rows, :]
        out[rows:, :] = moved[j * rows : (j + 1) * rows, :]


def meet(info, near, moved):
    outs = [shape((near.shape[0] // 2, near.shape[1]), near.dtype)] * 4
    return call(
        meet_kernel,
        info, (1,), [whole(near), whole(moved)], [whole(a) for a in outs], outs, (near, moved),
        "meet", 0,
    )


def pack_kernel(piece, width, info, weight_qkv, weight_out, gain, *outs):
    for k, j in enumerate(SHARD_TO_RANK):
        rank = jnp.bitwise_xor(info[RANK], j)
        for head in range(piece // HD):
            for part in range(3):
                start = pl.multiple_of(part * width + rank * piece + head * HD, HD)
                column = (head * 3 + part) * HD
                value = weight_qkv[:, pl.ds(start, HD)].astype(F32) * gain[...]
                outs[k][:, column : column + HD] = value.astype(BF16)
        outs[k][:, 3 * piece :] = weight_out[:, pl.ds(pl.multiple_of(rank * piece, piece), piece)]


def pack(info, weight_qkv, weight_out, gain):
    rows, width = weight_out.shape
    piece = width // 8
    outs = [shape((rows, 4 * piece), BF16)] * 4
    operands = (weight_qkv, weight_out, gain)
    return call(
        functools.partial(pack_kernel, piece, width),
        info, (1,), [whole(a) for a in operands], [whole(a) for a in outs], outs, operands,
        "pack", 0,
    )


def join_two_kernel(count, info, *refs):
    first, second = refs[count:]
    columns = first.shape[1]
    rows = refs[0].shape[0]
    for k in range(count):
        first[k * rows : (k + 1) * rows, :] = refs[k][:, :columns]
        second[k * rows : (k + 1) * rows, :] = refs[k][:, columns:]


def join_two(info, columns, *blocks):
    rows = sum(block.shape[0] for block in blocks)
    outs = [shape((rows, columns), BF16), shape((rows, blocks[0].shape[1] - columns), BF16)]
    return call(
        functools.partial(join_two_kernel, len(blocks)),
        info, (1,), [whole(a) for a in blocks], [whole(a) for a in outs], outs, blocks,
        "join_two", 0,
    )


def place_rows(info, parts, out):
    rows = parts[0].shape[0] // 4
    for s, source in enumerate(parts):
        for k in range(4):
            block = info[PLANES + s] * 4 + jnp.bitwise_xor(info[SHARD], k)
            out[pl.ds(pl.multiple_of(block * rows, rows), rows), :] = source[
                k * rows : (k + 1) * rows, :
            ]


def assemble_kernel(info, *refs):
    place_rows(info, refs[:-1], refs[-1])


def assemble(info, *parts):
    out = shape((len(parts) * parts[0].shape[0], parts[0].shape[1]), BF16)
    return call(
        assemble_kernel,
        info, (1,), [whole(a) for a in parts], whole(out), out, parts, "assemble", 0,
    )


def stack_kernel(count, cut, info, *refs):
    first, second = refs[count:]
    rest = refs[0].shape[0] - cut
    for s in range(count):
        plane = info[PLANES + s]
        first[pl.ds(pl.multiple_of(plane * cut, cut), cut), :] = refs[s][:cut, :]
        second[pl.ds(pl.multiple_of(plane * rest, rest), rest), :] = refs[s][cut:, :]
    for out, rows in ((first, cut), (second, rest)):
        if out.shape[0] > count * rows:
            out[count * rows :, :] = jnp.zeros((out.shape[0] - count * rows, out.shape[1]), BF16)


def stack_planes(info, cut, *parts):
    count, (rows, width) = len(parts), parts[0].shape
    outs = [
        shape((-(-count * size // 128) * 128, width), BF16) for size in (cut, rows - cut)
    ]
    return call(
        functools.partial(stack_kernel, count, cut),
        info, (1,), [whole(a) for a in parts], [whole(a) for a in outs], outs, parts, "stack", 0,
    )


def spread_kernel(count, rows, piece, info, *refs):
    out = refs[-1]
    for j in range(8):
        columns = pl.ds(
            pl.multiple_of(jnp.bitwise_xor(info[RANK], j) * piece, piece), piece
        )
        shift = 2 * ((j >> 1) & 1) + (j >> 2)
        source = refs[j // 4]
        base = (j % 4) * count * 4 * rows
        for s in range(count):
            for k in range(4):
                block = info[PLANES + s] * 4 + jnp.bitwise_xor(info[SHARD], k ^ shift)
                start = base + (s * 4 + k) * rows
                out[pl.ds(pl.multiple_of(block * rows, rows), rows), columns] = source[
                    start : start + rows, :
                ]


def spread(info, near, far, count):
    piece = near.shape[1]
    width = piece * 8
    rows = width // (4 * count)
    out = shape((width, width), BF16)
    return call(
        functools.partial(spread_kernel, count, rows, piece),
        info, (1,), [whole(near), whole(far)], whole(out), out, (near, far), "spread", 0,
    )


def project_kernel(count, info, near, far, *refs):
    parts, tables = refs[:count], refs[count : count + 4]
    weight, out, act_near, act_far = refs[count + 4 :]

    @pl.when(pl.program_id(0) == 0)
    def _():
        place_rows(info, parts, weight)

    for half, (tokens, act) in enumerate(((near, act_near), (far, act_far))):
        values = tokens[...].astype(F32)
        inverse = lax.rsqrt(jnp.mean(values * values, axis=1, keepdims=True) + EPS)
        act[...] = (values * inverse).astype(BF16)
        proj = dot(act[...], weight[...])
        for part in range(proj.shape[1] // HD):
            value = proj[:, part * HD : (part + 1) * HD]
            if part % 3 < 2:
                turned = pltpu.roll(value, HD // 2, 1)
                value = value * tables[half][...] + turned * tables[2 + half][...]
            out[half, :, part * HD : (part + 1) * HD] = value.astype(BF16)


def project(info, near, far, parts, cosine, sine):
    rows, width = near.shape
    tile = rows // 4
    columns = parts[0].shape[1]
    outs = [
        shape((width, columns), BF16),
        shape((2, rows, columns), BF16),
        shape((rows, width), BF16),
        shape((rows, width), BF16),
    ]
    tiles = pl.BlockSpec((tile, width), lambda i, s: (i, 0))
    first = pl.BlockSpec((tile, HD), lambda i, s: (i, 0))
    second = pl.BlockSpec((tile, HD), lambda i, s: (i + 4, 0))
    weight, out, act_near, act_far = call(
        functools.partial(project_kernel, len(parts)),
        info, (4,),
        [tiles, tiles]
        + [whole(a) for a in parts]
        + [first, second, first, second],
        [whole(outs[0]), pl.BlockSpec((2, tile, columns), lambda i, s: (0, i, 0)), tiles, tiles],
        outs, (near, far, *parts, cosine, cosine, sine, sine),
        "project", 4 * rows * width * columns,
    )
    return out.reshape(2 * rows, columns), weight, act_near, act_far


def place_of(block):
    return (block & 1) | ((block >> 1) & 1) << 2 | ((block >> 2) & 1) << 1


def lowest_key(block, rows, bound):
    pos = block * rows + lax.broadcasted_iota(jnp.int32, (rows, 1), 0)
    return jnp.maximum(jnp.where(pos >= bound, bound, 0), pos - (WINDOW - 1))


def block_scores(query, key, low, q_block, k_block, rows):
    scores = dot_nt(query, key) * HD**-0.5
    pos = k_block * rows + lax.broadcasted_iota(jnp.int32, (rows, rows), 1)
    seen = pos >= low
    if q_block == k_block:
        seen = seen & (
            lax.broadcasted_iota(jnp.int32, (rows, rows), 1)
            <= lax.broadcasted_iota(jnp.int32, (rows, rows), 0)
        )
    return jnp.where(seen, scores, NEG)


def key_blocks(q_block, rows):
    return range(max(0, q_block - WINDOW // rows), q_block + 1)


def row_start(block, rank, rows):
    return pl.multiple_of(jnp.bitwise_xor(place_of(block), rank) * rows, rows)


def attend_kernel(info, qkv, *refs):
    near, far, lse, result = refs
    rows = qkv.shape[0] // 8
    rank, bound = info[RANK], info[BOUND]
    for b in range(8):
        own = pl.ds(row_start(b, rank, rows), rows)
        query = qkv[own, :HD]
        low = lowest_key(b, rows, bound)
        spots = [(kb, pl.ds(row_start(kb, rank, rows), rows)) for kb in key_blocks(b, rows)]
        scores = [
            block_scores(query, qkv[at, HD : 2 * HD], low, b, kb, rows) for kb, at in spots
        ]
        top = functools.reduce(jnp.maximum, [jnp.max(s, axis=1, keepdims=True) for s in scores])
        powered = [jnp.exp(s - top) for s in scores]
        total = functools.reduce(jnp.add, [jnp.sum(p, axis=1, keepdims=True) for p in powered])
        inverse = 1.0 / total
        out = functools.reduce(
            jnp.add,
            [
                dot((p * inverse).astype(BF16), qkv[at, 2 * HD :])
                for p, (_, at) in zip(powered, spots)
            ],
        )
        result[own, :] = out.astype(BF16)
        lse[0, own, :] = top + jnp.log(total)
    near[...] = result[: 4 * rows, :]
    far[...] = result[4 * rows :, :]


def attend(info, qkv):
    length = qkv.shape[0]
    rows = length // 8
    heads = qkv.shape[1] // (3 * HD)
    outs = [shape((4 * rows, heads * HD), BF16)] * 2 + [shape((heads, length, 1), F32)]
    return call(
        attend_kernel,
        info, (heads,), [pl.BlockSpec((length, 3 * HD), lambda h, s: (0, h))],
        [pl.BlockSpec((4 * rows, HD), lambda h, s: (0, h))] * 2
        + [pl.BlockSpec((1, length, 1), lambda h, s: (h, 0, 0))],
        outs, (qkv,), "attend", 8 * heads * length * WINDOW * HD,
        [pltpu.VMEM((length, HD), BF16)],
    )


def attend_back_kernel(info, qkv, *refs):
    grads, (lse, cosine, sine, out, top_all, sum_key, sum_value) = refs[:4], refs[4:]
    rows = qkv.shape[0] // 8
    rank, bound = info[RANK], info[BOUND]
    sum_key[...] = jnp.zeros_like(sum_key)
    sum_value[...] = jnp.zeros_like(sum_value)
    for j in range(4):
        top_all[j * rows : (j + 1) * rows, :] = grads[j][:rows, :]
        top_all[(j + 4) * rows : (j + 5) * rows, :] = grads[j][rows:, :]

    def unturn(value, at):
        value = value.astype(BF16).astype(F32)
        turned = value * cosine[at, :] - pltpu.roll(value, HD // 2, 1) * sine[at, :]
        return turned.astype(BF16)

    for b in range(8):
        own = pl.ds(row_start(b, rank, rows), rows)
        query = qkv[own, :HD]
        top = top_all[own, :]
        low = lowest_key(b, rows, bound)
        log_total = lse[0, own, :]
        spots = [(kb, pl.ds(row_start(kb, rank, rows), rows)) for kb in key_blocks(b, rows)]
        probs = [
            jnp.exp(block_scores(query, qkv[at, HD : 2 * HD], low, b, kb, rows) - log_total)
            for kb, at in spots
        ]
        slopes = [dot_nt(top, qkv[at, 2 * HD :]) for _, at in spots]
        mean = functools.reduce(
            jnp.add, [jnp.sum(p * g, axis=1, keepdims=True) for p, g in zip(probs, slopes)]
        )
        sum_query = jnp.zeros((rows, HD), F32)
        for p, g, (_, at) in zip(probs, slopes, spots):
            low_grad = (p * (g - mean)).astype(BF16)
            sum_query = sum_query + dot(low_grad, qkv[at, HD : 2 * HD])
            sum_key[at, :] += dot_tn(low_grad, query)
            sum_value[at, :] += dot_tn(p.astype(BF16), top)
        out[own, :HD] = unturn(sum_query * HD**-0.5, own)

    @pl.loop(0, 8)
    def _(j):
        at = pl.ds(pl.multiple_of(j * rows, rows), rows)
        out[at, HD : 2 * HD] = unturn(sum_key[at, :] * HD**-0.5, at)
        out[at, 2 * HD :] = sum_value[at, :].astype(BF16)


def attend_back(info, qkv, grads, lse, cosine, sine, head):
    length = qkv.shape[0]
    rows = length // 8
    out = shape((length, 3 * HD), BF16)
    return call(
        attend_back_kernel,
        info, (1,),
        [pl.BlockSpec((length, 3 * HD), lambda i, s: (0, head))]
        + [pl.BlockSpec((2 * rows, HD), lambda i, s: (0, head))] * 4
        + [pl.BlockSpec((1, length, 1), lambda i, s: (head, 0, 0))]
        + [whole(cosine), whole(sine)],
        whole(out), out, (qkv, *grads, lse, cosine, sine), "attend_back",
        20 * length * WINDOW * HD,
        [
            pltpu.VMEM((length, HD), BF16),
            pltpu.VMEM((length, HD), F32),
            pltpu.VMEM((length, HD), F32),
        ],
    )


def branch_kernel(piece, info, *refs):
    blocks = refs[:4]
    weight, tokens, attn, middle, scale, act = refs[4:]
    step = pl.program_id(0)
    width = weight.shape[1]

    @pl.when(step == 0)
    def _():
        rows = tokens.shape[0]
        for j in range(8):
            start = pl.multiple_of(jnp.bitwise_xor(info[RANK], j) * piece, piece)
            first = j // 4 * rows
            attn[:, pl.ds(start, piece)] = blocks[j % 4][first : first + rows, :]

    at = pl.ds(pl.multiple_of(step * width, width), width)
    middle[:, at] = tokens[:, at].astype(F32) + dot(attn[...], weight[...])

    @pl.when(step == pl.num_programs(0) - 1)
    def _():
        value = middle[...]
        inverse = lax.rsqrt(jnp.mean(value * value, axis=1, keepdims=True) + EPS)
        scale[...] = inverse
        act[...] = (value * inverse).astype(BF16)


def branch(info, blocks, weight, tokens):
    rows, width = tokens.shape
    outs = [
        shape((rows, width), BF16),
        shape((rows, width), F32),
        shape((rows, 1), F32),
        shape((rows, width), BF16),
    ]
    return call(
        functools.partial(branch_kernel, width // 8),
        info, (4,),
        [whole(a) for a in blocks]
        + [pl.BlockSpec((width, width // 4), lambda i, s: (0, i)), whole(tokens)],
        [whole(a) for a in outs], outs, (*blocks, weight, tokens), "branch",
        2 * rows * width * width,
    )


def slopes_kernel(info, near, far, first, second, out_near, out_far):
    columns = first.shape[0]
    for top, out in ((near, out_near), (far, out_far)):
        out[:, :columns] = dot_nt(top[...], first[...])
        out[:, columns:] = dot_nt(top[...], second[...])


def slopes(info, near, far, first, second):
    rows, width = near.shape
    tile = rows // 4
    columns = first.shape[0] + second.shape[0]
    tiles = pl.BlockSpec((tile, width), lambda i, s: (i, 0))
    return call(
        slopes_kernel,
        info, (4,), [tiles, tiles, whole(first), whole(second)],
        [pl.BlockSpec((tile, columns), lambda i, s: (i, 0))] * 2,
        [shape((rows, columns), F32)] * 2, (near, far, first, second), "slopes",
        4 * rows * width * columns,
    )


def ffn_kernel(tail, more, info, *refs):
    if more:
        act, slope, pair, earlier, earlier_pair, hidden, grads, back = refs
    else:
        act, slope, pair, hidden, grads = refs
    double = pair.shape[1]
    main = double // 2 - tail
    proj = dot(act[...], pair[...])

    def gated(gate, up, grad):
        sigmoid = jax.nn.sigmoid(gate)
        silu = gate * sigmoid
        return (
            silu * up,
            grad * up * sigmoid * (1.0 + gate * (1.0 - sigmoid)),
            grad * silu,
        )

    value, to_gate, to_up = gated(proj[:, :main], proj[:, double - main :], slope[:, :main])
    hidden[:, :main] = value.astype(BF16)
    grads[:, :main] = to_gate.astype(BF16)
    grads[:, double - main :] = to_up.astype(BF16)
    if tail:
        mixed = proj[:, main : main + 2 * tail]
        value, to_gate, to_up = gated(
            mixed, pltpu.roll(mixed, tail, 1), slope[:, main : main + 2 * tail]
        )
        first = lax.broadcasted_iota(jnp.int32, mixed.shape, 1) < tail
        hidden[:, main : main + 2 * tail] = jnp.where(first, value, 0.0).astype(BF16)
        grads[:, main : main + 2 * tail] = jnp.where(
            first, to_gate, pltpu.roll(to_up, tail, 1)
        ).astype(BF16)
    if more:
        total = dot_nt(grads[...], pair[...]) + dot_nt(earlier[...], earlier_pair[...])
        back[...] = total.astype(BF16)


def ffn(info, act, slope, chunk, pair, earlier=None, earlier_pair=None):
    rows, width = act.shape
    tile = rows // 4
    double = pair.shape[1]
    columns = -(-double // 256) * 128
    offset = slope.shape[1] // columns - 1 if chunk else 0
    more = earlier is not None
    tiles = pl.BlockSpec((tile, width), lambda i, s: (i, 0))
    operands = [act, slope, pair]
    in_specs = [tiles, pl.BlockSpec((tile, columns), lambda i, s: (i, offset)), whole(pair)]
    outs = [shape((rows, columns), BF16), shape((rows, double), BF16)]
    out_specs = [
        pl.BlockSpec((tile, columns), lambda i, s: (i, 0)),
        pl.BlockSpec((tile, double), lambda i, s: (i, 0)),
    ]
    flops = 2 * rows * width * double
    if more:
        operands += [earlier, earlier_pair]
        in_specs += [
            pl.BlockSpec((tile, earlier.shape[1]), lambda i, s: (i, 0)),
            whole(earlier_pair),
        ]
        outs += [shape((rows, width), BF16)]
        out_specs += [tiles]
        flops += 2 * rows * width * (double + earlier.shape[1])
    return call(
        functools.partial(ffn_kernel, double // 2 % 128, more),
        info, (4,), in_specs, out_specs, outs, operands, "ffn", flops,
    )


def grad_rows_kernel(own_rows, info, act_near, act_far, near, far, *refs):
    outs, total = refs[:-1], refs[-1]
    total[...] = dot_tn(act_near[...], near[...]) + dot_tn(act_far[...], far[...])
    for i, out in enumerate(outs):

        @pl.when(pl.program_id(0) == i)
        def _():
            for k in range(4):
                start = jnp.bitwise_xor(info[SHARD], k) * own_rows
                value = total[pl.ds(pl.multiple_of(start, own_rows), own_rows), :]
                out[k * own_rows : (k + 1) * own_rows, :] = value.astype(BF16)


def grad_rows(info, act_near, act_far, near, far, count, name, split=False):
    rows, width = act_near.shape
    chunk = width // count
    columns = near.shape[1]

    def spot(i, s):
        return (0, s[PLANES + (i + 1) % count])

    acts = pl.BlockSpec((rows, chunk), spot)
    outs = [shape((chunk, columns), BF16)] * count
    first = pl.BlockSpec((rows, columns), lambda i, s: (0, 0))
    second = pl.BlockSpec((rows, columns), lambda i, s: (1 if split else 0, 0))
    return call(
        functools.partial(grad_rows_kernel, chunk // 4),
        info, (count,), [acts, acts, first, second], [whole(a) for a in outs], outs,
        (act_near, act_far, near, far), name, 4 * rows * width * columns,
        [pltpu.VMEM((chunk, columns), F32)],
    )


def grad_down_kernel(rows, info, first_near, first_far, second_near, second_far, *refs):
    top_near, top_far = refs[:2]
    outs, total = refs[2:-1], refs[-1]
    count = len(outs)
    start = 0
    for near, far, part in ((first_near, first_far, rows[0]), (second_near, second_far, rows[1])):
        units = near.shape[1]
        total[:units, :] = dot_tn(near[...], top_near[...]) + dot_tn(far[...], top_far[...])
        for i in range(count):
            at = pl.multiple_of(info[PLANES + (i + 1) % count] * part, part)
            outs[i][start : start + part, :] = total[pl.ds(at, part), :].astype(BF16)
        start += part


def grad_down(info, first, second, top_near, top_far, count, rows):
    tokens, width = top_near.shape
    part = width // 4
    outs = [shape((sum(rows), width), BF16)] * count
    tops = pl.BlockSpec((tokens, part), lambda i, s: (0, i))
    hidden = (*first, *second)
    units = max(a.shape[1] for a in hidden)
    return call(
        functools.partial(grad_down_kernel, rows),
        info, (4,), [whole(a) for a in hidden] + [tops, tops],
        [pl.BlockSpec((sum(rows), part), lambda i, s: (0, i))] * count, outs,
        (*hidden, top_near, top_far), "grad_down",
        4 * tokens * width * (first[0].shape[1] + second[0].shape[1]),
        [pltpu.VMEM((units, part), F32)],
    )


def matmul_two_kernel(info, a, b, c, d, out):
    out[...] = (dot(a[...], b[...]) + dot(c[...], d[...])).astype(BF16)


def down_product(info, first, second, down_first, down_second):
    rows, width = first.shape[0], down_first.shape[1]
    tile = rows // 4
    out = shape((rows, width), BF16)
    return call(
        matmul_two_kernel,
        info, (4,),
        [
            pl.BlockSpec((tile, first.shape[1]), lambda i, s: (i, 0)), whole(down_first),
            pl.BlockSpec((tile, second.shape[1]), lambda i, s: (i, 0)), whole(down_second),
        ],
        pl.BlockSpec((tile, width), lambda i, s: (i, 0)), out,
        (first, down_first, second, down_second), "down_product",
        2 * rows * width * (first.shape[1] + second.shape[1]),
    )


def grad_attn_kernel(info, *refs):
    own, first, second, third, top, middle, scale, weight = refs[:8]
    grad_middle, branch_ref, near, far = refs[8:]
    step = pl.program_id(0)
    rows = own.shape[0]

    @pl.when(step == 0)
    def _():
        grad = own[...]
        for moved in (first, second, third):
            grad = grad + moved[...].astype(F32)
        value, inverse = middle[...], scale[...]
        mean = jnp.mean(grad * value, axis=1, keepdims=True)
        total = top[...].astype(F32) + inverse * grad - value * (inverse**3 * mean)
        grad_middle[...] = total
        branch_ref[...] = total.astype(BF16)

    value = dot_nt(branch_ref[...], weight[...]).astype(BF16)
    for j in range(8):

        @pl.when(step == j)
        def _():
            out = far if j > 3 else near
            out[j % 4 * rows : (j % 4 + 1) * rows, :] = value


def grad_attn(info, own, parts, top, middle, scale, weight):
    rows, width = middle.shape
    piece = width // 8
    outs = [shape((rows, width), F32), shape((rows, width), BF16)]
    outs += [shape((4 * rows, piece), BF16)] * 2
    operands = (own, *parts, top, middle, scale)

    def spot(i, s):
        return (jnp.bitwise_xor(s[RANK], i), 0)

    return call(
        grad_attn_kernel,
        info, (8,), [whole(a) for a in operands] + [pl.BlockSpec((piece, width), spot)],
        [whole(a) for a in outs], outs, (*operands, weight), "grad_attn",
        2 * rows * width * width,
    )


def grad_out_kernel(info, attn, near_cols, far_cols, near, far):
    near[0] = dot_tn(attn[...], near_cols[...]).astype(BF16)
    far[0] = dot_tn(attn[...], far_cols[...]).astype(BF16)


def grad_out_terms(info, attn, grad):
    rows, width = attn.shape
    piece = width // 8
    outs = [shape((4, width, piece), BF16)] * 2
    return call(
        grad_out_kernel,
        info, (4,),
        [
            whole(attn),
            pl.BlockSpec((rows, piece), lambda i, s: (0, jnp.bitwise_xor(s[RANK], i))),
            pl.BlockSpec((rows, piece), lambda i, s: (0, jnp.bitwise_xor(s[RANK], i + 4))),
        ],
        [pl.BlockSpec((1, width, piece), lambda i, s: (i, 0, 0))] * 2, outs,
        (attn, grad, grad), "grad_out", 2 * rows * width * width,
    )


def order_kernel(own_rows, info, own, first, second, third, *refs):
    outs, total = refs[:-1], refs[-1]
    count = len(outs)
    value = own[...]
    for moved in (first, second, third):
        value = value + moved[...].astype(F32)
    total[...] = value
    for i, out in enumerate(outs):
        for k in range(4):
            block = info[PLANES + (i + 1) % count] * 4 + jnp.bitwise_xor(info[SHARD], k)
            value = total[pl.ds(pl.multiple_of(block * own_rows, own_rows), own_rows), :]
            out[k * own_rows : (k + 1) * own_rows, :] = value.astype(BF16)


def order_out(info, own, parts, count):
    width, columns = own.shape
    outs = [shape((width // count, columns), BF16)] * count
    return call(
        functools.partial(order_kernel, width // count // 4),
        info, (1,), [whole(a) for a in (own, *parts)], [whole(a) for a in outs], outs,
        (own, *parts), "order_out", 0, [pltpu.VMEM((width, columns), F32)],
    )


def back_product_kernel(info, first, second, weight, out):
    columns = first.shape[1]
    total = dot_nt(first[...], weight[:, :columns]) + dot_nt(second[...], weight[:, columns:])
    out[...] = total.astype(BF16)


def back_product(info, first, second, weight, far):
    rows, width = first.shape[0] // 2, weight.shape[0]
    tile = rows // 4
    out = shape((rows, width), BF16)
    tiles = pl.BlockSpec((tile, first.shape[1]), lambda i, s: (i + (4 if far else 0), 0))
    return call(
        back_product_kernel,
        info, (4,), [tiles, tiles, whole(weight)],
        pl.BlockSpec((tile, width), lambda i, s: (i, 0)), out, (first, second, weight),
        "back_product", 2 * rows * width * weight.shape[1],
    )


def rank_block(info, j, mine, theirs):
    rows = mine.shape[0] // 4
    source = theirs if j % 2 else mine
    return source[j // 2 * rows : (j // 2 + 1) * rows, :]


def finish_qkv_kernel(info, *refs):
    pairs = (refs[:2], refs[2:4])
    weight, gain, out, gain_out = refs[4:]
    rows, width = out.shape[0], out.shape[1] // 3
    total = jnp.zeros((rows, HD), F32)
    for j in range(8):
        rank = jnp.bitwise_xor(info[RANK], j)
        for head, pair in enumerate(pairs):
            block = rank_block(info, j, *pair)
            for part in range(3):
                start = pl.multiple_of(part * width + (2 * rank + head) * HD, HD)
                value = block[:, part * HD : (part + 1) * HD].astype(F32)
                out[:, pl.ds(start, HD)] = value * gain[...]
                total = total + value * weight[:, pl.ds(start, HD)].astype(F32)
    gain_out[...] = jnp.sum(total, axis=1, keepdims=True)


def finish_qkv(info, first, second, weight, gain):
    outs = [shape(weight.shape, F32), shape(gain.shape, F32)]
    operands = (*first, *second, weight, gain)
    return call(
        finish_qkv_kernel,
        info, (1,), [whole(a) for a in operands], [whole(a) for a in outs], outs, operands,
        "finish_qkv", 0,
    )


def finish_out_kernel(info, mine, theirs, out):
    piece = mine.shape[1]
    for j in range(8):
        start = pl.multiple_of(jnp.bitwise_xor(info[RANK], j) * piece, piece)
        out[:, pl.ds(start, piece)] = rank_block(info, j, mine, theirs).astype(F32)


def finish_out(info, mine, theirs):
    rows, piece = mine.shape[0] // 4, mine.shape[1]
    out = shape((rows, 8 * piece), F32)
    return call(
        finish_out_kernel,
        info, (1,), [whole(mine), whole(theirs)], whole(out), out, (mine, theirs),
        "finish_out", 0,
    )


def unit_lanes(first, count, local):
    main = local // 128 * 128
    runs = []
    while count:
        size = min(count, main - first) if first < main else count
        up = local + (local - main) + first if first < main else local + first - main
        runs.append((first, up, size))
        first, count = first + size, count - size
    return runs


def finish_pair_kernel(planes, reals, pads, info, *refs):
    chunks = (refs[:2], refs[2:4])
    weights, gain, outs, gain_out = refs[4:6], refs[6], refs[7:9], refs[9]
    held = refs[10:]
    rows, width = outs[0].shape
    half_down = sum(reals)
    for (mine, theirs), by_rank in zip(chunks, held):
        for j in range(8):
            start = jnp.bitwise_xor(info[RANK], j) * rows
            block = rank_block(info, j, mine, theirs)
            by_rank[pl.ds(pl.multiple_of(start, rows), rows), :] = block[...].astype(F32)

    def move(chunk, rank, lane, out, column, size):
        source, target = lane // 128 * 128, column // 128 * 128
        wide = 128 if (lane - source) + size <= 128 and (column - target) + size <= 128 else 256
        at = slice(rank * rows, (rank + 1) * rows)
        if (lane - source) + size <= 128:
            value = held[chunk][at, source : source + 128]
            if wide == 256:
                value = jnp.concatenate([value, value], axis=1)
        else:
            value = held[chunk][at, source : source + 256]
        shift = ((column - target) - (lane - source)) % wide
        if shift:
            value = pltpu.roll(value, shift, 1)
        lanes = lax.broadcasted_iota(jnp.int32, value.shape, 1)
        keep = (lanes >= column - target) & (lanes < column - target + size)
        spot = slice(target, min(target + wide, width))
        if target + wide > width:
            value, keep = value[:, : width - target], keep[:, : width - target]
        out[:, spot] = jnp.where(keep, value, out[:, spot])

    for plane in range(planes):
        for rank in range(8):
            shard = 2 * (rank >> 1 & 1) + (rank >> 2)
            column = ((plane * 4 + shard) * 2 + (rank & 1)) * half_down
            for chunk, (real, pad) in enumerate(zip(reals, pads)):
                start = column
                for gate, up, size in unit_lanes(plane * pad, real, planes * pad):
                    move(chunk, rank, gate, outs[0], start, size)
                    move(chunk, rank, up, outs[1], start, size)
                    start += size
                column += real
    total = jnp.zeros((rows, 128), F32)
    for weight, out in zip(weights, outs):
        for tile in range(width // 128):
            at = slice(tile * 128, (tile + 1) * 128)
            value = out[:, at]
            total = total + value * weight[:, at].astype(F32)
            out[:, at] = value * gain[...]
    gain_out[...] = jnp.sum(total, axis=1, keepdims=True)


def finish_pair(info, first, second, gate, up, gain, planes, reals, pads):
    rows = gate.shape[0]
    outs = [shape(gate.shape, F32)] * 2 + [shape(gain.shape, F32)]
    operands = (*first, *second, gate, up, gain)
    return call(
        functools.partial(finish_pair_kernel, planes, reals, pads),
        info, (1,), [whole(a) for a in operands], [whole(a) for a in outs], outs, operands,
        "finish_pair", 0,
        [pltpu.VMEM((8 * rows, pair[0].shape[1]), F32) for pair in (first, second)],
    )


def on_device(
    planes,
    tokens,
    bounds,
    norm_attn,
    weight_qkv,
    weight_out,
    norm_ffn,
    weight_gate,
    weight_up,
    weight_down,
    cotangent,
):
    rows, width = tokens.shape[1], tokens.shape[2]
    own_rows = weight_qkv.shape[0]
    half_down = weight_down.shape[0] // 2
    cut = -(-half_down // 32) * 16
    pads = (cut, -(-(half_down - cut) // 16) * 16)
    reals = (cut, half_down - cut)
    starts = (0, cut)

    y, z, x, c = (lax.axis_index(name) for name in ("y", "z", "x", "c"))
    rank = 4 * c + 2 * x + y
    shard = 2 * x + c
    ring_list = ring_of(planes)
    table = [
        [ring_list[(ring_list.index(i) - s) % planes] for s in range(planes)]
        for i in range(planes)
    ]
    arrival = jnp.asarray(table, jnp.int32)[z]
    boundary = lax.dynamic_index_in_dim(bounds, z, 0, False)
    info = jnp.concatenate([jnp.stack([rank, boundary, shard]).astype(jnp.int32), arrival])
    order = Order()
    do, need = order.do, order.need
    lane_a, lane_b = Lane(planes), Lane(planes)

    def spread_pieces(pieces):
        return [hop(piece, j) for piece, j in zip(pieces, SHARD_TO_RANK)]

    def owners(total):
        return [
            hop(total[k * own_rows : (k + 1) * own_rows], SHARD_TO_RANK[k]) for k in (2, 1, 3)
        ]

    def rows_of(total, pieces):
        need(*pieces)
        mine = do(join, info, (total, 0, own_rows), *pieces)
        return mine, hop(mine, 1)

    down_own = lax.dynamic_slice_in_dim(weight_down, y * half_down, half_down, 0)
    down_own = jnp.pad(down_own, [(0, sum(pads) - half_down), (0, 0)])
    down_got = lane_a.gather(down_own, 1)
    wide_attn = norm_attn.astype(F32)[:, None]
    wide_ffn = norm_ffn.astype(F32)[:, None]
    pieces = spread_pieces(do(pack, info, weight_qkv, weight_out, wide_attn))
    token_parts = near_parts(tokens[0], (), pieces[1:])

    def split_hidden(weight):
        split = (after(weight, *pieces).astype(F32) * wide_ffn).astype(BF16)
        split = split.reshape(own_rows, planes, 2, 2, 2, half_down)
        return split.transpose(3, 2, 4, 0, 1, 5).reshape(8, own_rows, planes, half_down)

    gate_split, up_split = split_hidden(weight_gate), split_hidden(weight_up)
    pair_pieces = []
    for start, real, pad in zip(starts, reals, pads):
        both = []
        for split in (gate_split, up_split):
            part = split[..., start : start + real]
            part = jnp.pad(part, [(0, 0)] * 3 + [(0, pad - real)])
            both.append(part.reshape(8, own_rows, planes * pad))
        main = planes * pad // 128 * 128
        pair_pieces += [both[0], both[1][..., main:], both[1][..., :main]]
    pair_pieces = jnp.concatenate(pair_pieces, axis=-1)
    pair_pieces = spread_pieces(
        [
            lax.dynamic_index_in_dim(pair_pieces, jnp.bitwise_xor(rank, j), 0, False)
            for j in SHARD_TO_RANK
        ]
    )

    blocks = jnp.asarray([place_of(i) for i in range(8)], jnp.int32)
    blocks = jnp.take(blocks, jnp.bitwise_xor(jnp.arange(8, dtype=jnp.int32), rank))
    positions = (blocks[:, None] * rows + jnp.arange(rows, dtype=jnp.int32)[None, :]).reshape(-1)
    frequency = THETA ** (-jnp.arange(HD // 2, dtype=F32) * 2.0 / HD)
    angles = positions.astype(F32)[:, None] * frequency[None, :]
    cosine = jnp.cos(angles)
    sine = jnp.sin(angles)
    cosine = jnp.concatenate([cosine, cosine], axis=1)
    sine = jnp.concatenate([-sine, sine], axis=1)

    need(down_got[1], *pieces[1:])
    qkv_plane, out_plane = do(join_two, info, 3 * (width // 8), *pieces)
    out_got = lane_a.gather(out_plane)
    qkv_got = lane_b.gather(qkv_plane)
    need(out_got[1], *pair_pieces[1:])
    pair_first, pair_second = do(join_two, info, 2 * planes * pads[0], *pair_pieces)
    need(*out_got, qkv_got[1])
    out_cols = do(join, info, *out_got)
    out_parts = near_parts(out_cols, token_parts[1:2], pair_pieces, token_parts)
    need(*token_parts)
    tokens_near = do(join, info, *token_parts)
    tokens_far = hop(tokens_near, 4)
    lane_a.last = (qkv_got[-1],)
    pair_first_got = lane_b.gather(pair_first)
    down_got = lane_a.gather(down_got)
    pair_second_got = lane_a.gather(pair_second)
    need(tokens_far, *qkv_got)
    qkv, full_qkv, act_near, act_far = do(
        project, info, tokens_near, tokens_far, qkv_got, cosine, sine
    )
    need(*out_parts)
    out_near = do(join, info, *out_parts)
    out_far = hop(out_near, 4)
    top_parts = near_parts(after(cotangent[0], *out_parts))
    attn_near, attn_far, lse = do(attend, info, qkv)
    moved = hop(attn_far, 4)
    need(out_far, down_got[2], pair_first_got[1])
    full_out = do(spread, info, out_near, out_far, planes)
    need(moved)
    attn_moved = near_moves(do(meet, info, attn_near, moved))
    need(*attn_moved)
    attn, middle, scale, act_own = do(branch, info, attn_moved, full_out, tokens[0])
    act_parts = near_parts(act_own)
    need(*top_parts, pair_first_got[2])
    top_near = do(join, info, *top_parts)
    top_far = hop(top_near, 4)
    need(*down_got)
    down_a, down_b = do(stack_planes, info, pads[0], *down_got)
    need(top_far)
    slope_near, slope_far = do(slopes, info, top_near, top_far, down_a, down_b)
    need(*pair_first_got, pair_second_got[1])
    full_first = do(assemble, info, *pair_first_got)
    need(*act_parts)
    ffn_near = do(join, info, *act_parts)
    ffn_far = hop(ffn_near, 4)

    hidden_near, grads_near = do(ffn, info, ffn_near, slope_near, 0, full_first)
    need(ffn_far, pair_second_got[2])
    hidden_far, grads_far = do(ffn, info, ffn_far, slope_far, 0, full_first)
    lane_c = Lane(planes)
    pair_a = Sum(
        order,
        lane_b,
        do(grad_rows, info, ffn_near, ffn_far, grads_near, grads_far, planes, "grad_pair"),
    )
    need(*pair_second_got)
    full_second = do(assemble, info, *pair_second_got)
    second_far, more_far, far_terms = do(
        ffn, info, ffn_far, slope_far, 1, full_second, grads_far, full_first
    )
    moved = hop(far_terms, 4)
    second_near, more_near, near_terms = do(
        ffn, info, ffn_near, slope_near, 1, full_second, grads_near, full_first
    )
    pair_a.move()
    need(moved)
    own, parts = scatter_moves(*do(combine, info, near_terms, moved))
    pair_b = Sum(
        order,
        lane_a,
        do(grad_rows, info, ffn_near, ffn_far, more_near, more_far, planes, "grad_pair"),
    )
    pair_a.move()
    down_sum = Sum(
        order,
        lane_b,
        do(
            grad_down, info, (hidden_near, hidden_far), (second_near, second_far),
            top_near, top_far, planes, pads,
        ),
    )
    block_near = do(down_product, info, hidden_near, second_near, down_a, down_b)
    need(*parts)

    grad_middle, grad_branch, attn_near, attn_far = do(
        grad_attn, info, own, parts, cotangent[0], middle, scale, full_out
    )
    pair_a.move()
    away = hop(attn_far, 4)
    near_out, far_out = do(grad_out_terms, info, attn, grad_branch)
    pair_b.move()
    first_pieces = owners(pair_a.total)
    need(away)
    attn_grads = near_moves(do(meet, info, attn_near, away))
    out_moved = hop(after(far_out, attn_grads[0]), 4)
    need(*first_pieces)
    block_far = do(down_product, info, hidden_far, second_far, down_a, down_b)
    need(*attn_grads)
    grads_first = do(attend_back, info, qkv, attn_grads, lse, cosine, sine, 0)
    pair_b.move()
    sums_first = rows_of(pair_a.total, first_pieces)
    need(out_moved)
    out_own, out_parts = scatter_moves(*do(combine, info, near_out, out_moved))
    down_sum.move()
    qkv_first = Sum(
        order,
        lane_a,
        do(grad_rows, info, act_near, act_far, grads_first, grads_first, planes, "grad_qkv", True),
    )
    block_moved = hop(after(block_far, qkv_first.total), 4)
    pair_b.move()
    grads_second = do(attend_back, info, qkv, attn_grads, lse, cosine, sine, 1)
    second_pieces = owners(pair_b.total)
    down_sum.move()
    need(block_moved)
    block_terms = do(combine, info, block_near, block_moved)
    qkv_first.move()
    need(*second_pieces)
    sums_second = rows_of(pair_b.total, second_pieces)
    qkv_second = Sum(
        order,
        lane_b,
        do(
            grad_rows, info, act_near, act_far, grads_second, grads_second, planes,
            "grad_qkv", True,
        ),
    )
    block_own, block_parts = scatter_moves(block_terms[0], *after(block_terms[1:], *out_parts))
    down_sum.move()

    in_far = do(back_product, info, grads_first, grads_second, full_qkv, True)
    in_moved = hop(in_far, 4)
    qkv_first.move()
    down_mine = down_sum.total[:half_down]
    down_theirs = hop(down_mine, 1)
    in_near = do(back_product, info, grads_first, grads_second, full_qkv, False)
    need(*out_parts)
    out_sum = Sum(order, lane_c, do(order_out, info, out_own, out_parts, planes))
    qkv_second.move()
    need(in_moved, *block_parts)
    in_own, in_parts = scatter_moves(*do(combine, info, in_near, in_moved))
    qkv_first.move()
    out_sum.move()
    need(*sums_first, *sums_second)
    sum_gate, sum_up, gain_sum_ffn = do(
        finish_pair, info, sums_first, sums_second, weight_gate, weight_up, wide_ffn,
        planes, reals, pads,
    )
    first_pieces = owners(qkv_first.total)
    qkv_second.move()
    out_sum.finish()
    first_rows = rows_of(qkv_first.total, first_pieces)
    out_pieces = owners(out_sum.total)
    qkv_second.finish()
    second_pieces = owners(qkv_second.total)
    out_rows = rows_of(out_sum.total, out_pieces)
    second_rows = rows_of(qkv_second.total, second_pieces)

    down_both = jnp.stack([down_mine, down_theirs])
    sum_down = jnp.concatenate(
        [lax.dynamic_index_in_dim(down_both, jnp.bitwise_xor(y, i), 0, False) for i in range(2)]
    ).astype(F32)
    need(out_rows[1])
    sum_out = do(finish_out, info, *out_rows)
    need(first_rows[1], second_rows[1])
    sum_qkv, gain_sum_attn = do(
        finish_qkv, info, first_rows, second_rows, weight_qkv, wide_attn
    )
    block_out = middle + block_own + sum(part.astype(F32) for part in block_parts)
    inputs = tokens[0].astype(F32)
    inv_attn = lax.rsqrt(jnp.mean(inputs * inputs, axis=-1, keepdims=True) + EPS)
    scaled = in_own + sum(part.astype(F32) for part in in_parts)
    grad_tokens = (
        grad_middle
        + inv_attn * scaled
        - inputs * inv_attn**3 * jnp.mean(scaled * inputs, axis=-1, keepdims=True)
    )
    return (
        block_out.astype(BF16)[None],
        grad_tokens[None],
        gain_sum_attn[:, 0],
        sum_qkv,
        sum_out,
        gain_sum_ffn[:, 0],
        sum_gate,
        sum_up,
        sum_down,
    )


def solution(mesh):
    planes = mesh.shape["fsdp"] // 4
    grid = Mesh(mesh.devices.reshape(2, planes, 2, 2), ("y", "z", "x", "c"))
    fsdp = ("z", "x", "c")
    by_token = P(fsdp, "y", None)
    by_row = P(fsdp, None)
    gain = P(fsdp)
    return jax.shard_map(
        functools.partial(on_device, planes),
        mesh=grid,
        in_specs=(
            by_token, P(), gain, by_row, by_row, gain, by_row, by_row, by_row, by_token,
        ),
        out_specs=(
            by_token, by_token, gain, by_row, by_row, gain, by_row, by_row, by_row,
        ),
        check_vma=False,
    )
```

time: 1140 us -> 871 us (0.76)
  Pallas kernels: 38.3 us -> 367 us
  waiting for transfers between devices: 501 us -> 314 us
  local copies, waits for them, and re-layouts: 213 us -> 37.7 us
  matrix products: 143 us -> 0 us
  blocking collectives: 59.8 us -> 0 us
  other arithmetic: 83.6 us -> 29.1 us
  starting transfers between devices: 82 us -> 113 us
    pallas_call x2 -> x48, Pallas kernels: 38.3 us -> 367 us  [call(): pl.pallas_call(kernel, grid_spec=pltpu.PrefetchScalarGridSpec(num_scalar_...]
    dot_general x22 -> x0, matrix products: 143 us -> none  [the longest x1 17.7 us: on_device(): pair = jnp.dot(act_ffn, full_pair, preferred_element_type=F32)]
    ppermute x90 -> x71, waiting for transfers between devices: 302 us -> 186 us  [hop(): return lax.ppermute(block, axes, [(i, last - i) for i in range(last + 1)])]
    unnamed x325 -> x205, local copies, waits for them, and re-layouts: 117 us -> 25.4 us
    ppermute x24 -> x33, waiting for transfers between devices: 199 us -> 128 us  [hop(): moved = lax.ppermute(block, 'z', self.route)]
    psum x1 -> x0, blocking collectives: 38.1 us -> none  [on_device(): lax.psum(jnp.stack([grad_gain_attn, grad_gain_ffn]), ('y', 'z', 'x', 'c'))]
    another operation x13 -> x0, other arithmetic: 32.6 us -> none
    ppermute x24 -> x33, starting transfers between devices: 18.2 us -> 49.8 us  [hop(): moved = lax.ppermute(block, 'z', self.route)]
  transfers between devices with their start and end apart: 114 -> 104, of which waited for: 46 -> 33; matrix products, arithmetic and copies ran while one was open for 32% -> 4% of each run, Pallas kernels for 3% -> 35%
where the time goes in v2:
time: 871 us; the launch traced here: 863 us
  Pallas kernels  367 us (42%)
  waiting for transfers between devices  314 us (36%)
  starting transfers between devices  113 us (13%)
  local copies, waits for them, and re-layouts  37.7 us (4%)
  other arithmetic  29.1 us (3%)
    pallas_call x48, Pallas kernels, call(): pl.pallas_call(kernel, grid_spec=pltpu.PrefetchScalarGridSpec(num_scalar_...  367 us
    ppermute x71, waiting for transfers between devices, hop(): return lax.ppermute(block, axes, [(i, last - i) for i in range(last + 1)])  186 us
    ppermute x33, waiting for transfers between devices, hop(): moved = lax.ppermute(block, 'z', self.route)  128 us
    ppermute x71, starting transfers between devices, hop(): return lax.ppermute(block, axes, [(i, last - i) for i in range(last + 1)])  62.7 us
    ppermute x33, starting transfers between devices, hop(): moved = lax.ppermute(block, 'z', self.route)  49.8 us
    unnamed x205, local copies, waits for them, and re-layouts  25.4 us
  transfers between devices with their start and end apart: 104, of which 33 were waited for; matrix products, arithmetic and copies ran while one was open for 4% of the time, Pallas kernels for 35%

profile of v2, /device:TPU:0, one launch (start us, length us, event | category | flops | bytes accessed | tf_op | source)
XLA Modules:
  0.0 863.0 jit_solution(8123731512128121910)
XLA Ops:
  95.8 15.5 %collective-permute-done.16.refs_2_ = bf16[512,768]{1,0:T(8,128)(2,1)S(1)} collective-permute-done((bf16[512,768]{1,0:T(8,128)(2,1)}, bf16[512,768]{1,0:T(8,128)(2,1)S(1)}, u32[]{:S(2)}, u32[]{:S(2)}) %collective-permute-start.16) | collective-permute-done | bytes 786464 | tf_op jit(solution)/shard_map/ppermute | solution.py:110
  121.4 10.3 %collective-permute-done.17.refs_3_ = bf16[512,768]{1,0:T(8,128)(2,1)S(1)} collective-permute-done((bf16[512,768]{1,0:T(8,128)(2,1)S(1)}, bf16[512,768]{1,0:T(8,128)(2,1)S(1)}, u32[]{:S(2)}, u32[]{:S(2)}) %collective-permute-start.17) | collective-permute-done | bytes 786464 | tf_op jit(solution)/shard_map/ppermute | solution.py:110
  132.6 15.7 %project.1 = (bf16[2048,768]{1,0:T(8,128)(2,1)}, bf16[2,1024,768]{2,1,0:T(8,128)(2,1)}, bf16[1024,2048]{1,0:T(8,128)(2,1)}, bf16[1024,2048]{1,0:T(8,128)(2,1)}) custom-call(s32[7]{0:T(128)} %pad_add_fusion.info, bf16[1024,2048]{1,0:T(8,128)(2,1)} %join.11.near, bf16[1024,2048]{1,0:T(8,128)(2,1)} %collective-permute-done.15.far, ...), custom_call_target="tpu_custom_call" | custom-call | flops 8194001920 | bytes 1 | tf_op jit(solution)/shard_map/project/pallas_call | solution.py:37
  162.0 13.7 %attend.1 = (bf16[1024,256]{1,0:T(8,128)(2,1)}, bf16[1024,256]{1,0:T(8,128)(2,1)}, f32[2,2048,1]{2,1,0:T(8,128)}) custom-call(s32[7]{0:T(128)} %pad_add_fusion.info, bf16[2048,768]{1,0:T(8,128)(2,1)} %bitcast.74), custom_call_target="tpu_custom_call" | custom-call | flops 2168458240 | bytes 1 | tf_op jit(solution)/shard_map/attend/pallas_call | solution.py:37
  175.8 14.9 %collective-permute-done.23.refs_2_ = bf16[176,2048]{1,0:T(8,128)(2,1)} collective-permute-done((bf16[176,2048]{1,0:T(8,128)(2,1)}, bf16[176,2048]{1,0:T(8,128)(2,1)}, u32[]{:S(2)}, u32[]{:S(2)}) %collective-permute-start.23) | collective-permute-done | bytes 720928 | tf_op jit(solution)/shard_map/ppermute | solution.py:110
  223.0 9.2 %branch.1 = (bf16[256,2048]{1,0:T(8,128)(2,1)}, f32[256,2048]{1,0:T(8,128)}, f32[256,1]{1,0:T(8,128)}, bf16[256,2048]{1,0:T(8,128)(2,1)}) custom-call(s32[7]{0:T(128)} %pad_add_fusion.info, bf16[512,256]{1,0:T(8,128)(2,1)} %get-tuple-element.250.refs_0_, bf16[512,256]{1,0:T(8,128)(2,1)} %copy-done.81, bf16[512,256]{1,0:T(8,128)(2,1)} %copy-done.82, ...), custom_call_target="tpu_custom_call" | custom-call | flops 4576650240 | bytes 1 | tf_op jit(solution)/shard_map/branch/pallas_call | solution.py:37
  245.0 16.8 %collective-permute-done.34.refs_3_ = bf16[176,2048]{1,0:T(8,128)(2,1)S(1)} collective-permute-done((bf16[176,2048]{1,0:T(8,128)(2,1)}, bf16[176,2048]{1,0:T(8,128)(2,1)S(1)}, u32[]{:S(2)}, u32[]{:S(2)}) %collective-permute-start.34) | collective-permute-done | bytes 720928 | tf_op jit(solution)/shard_map/ppermute | solution.py:110
  271.6 13.5 %slopes.1 = (f32[1024,768]{1,0:T(8,128)}, f32[1024,768]{1,0:T(8,128)}) custom-call(s32[7]{0:T(128)} %pad_add_fusion.info, bf16[1024,2048]{1,0:T(8,128)(2,1)} %join.13.near.refs_0_, bf16[1024,2048]{1,0:T(8,128)(2,1)} %copy-done.44, bf16[384,2048]{1,0:T(8,128)(2,1)} %get-tuple-element.264.first.b, bf16[384,2048]{1,0:T(8,128)(2,1)} %get-tuple-element.266.second.d), custom_call_target="tpu_custom_call" | custom-call | flops 5299932160 | bytes 1 | tf_op jit(solution)/shard_map/slopes/pallas_call | solution.py:37
  303.5 15.6 %collective-permute-done.43.refs_2_ = bf16[512,640]{1,0:T(8,128)(2,1)S(1)} collective-permute-done((bf16[512,640]{1,0:T(8,128)(2,1)S(1)}, bf16[512,640]{1,0:T(8,128)(2,1)S(1)}, u32[]{:S(2)}, u32[]{:S(2)}) %collective-permute-start.43) | collective-permute-done | bytes 655392 | tf_op jit(solution)/shard_map/ppermute | solution.py:110
  331.4 8.7 %ffn.5 = (bf16[1024,384]{1,0:T(8,128)(2,1)}, bf16[1024,768]{1,0:T(8,128)(2,1)}) custom-call(s32[7]{0:T(128)} %pad_add_fusion.info, bf16[1024,2048]{1,0:T(8,128)(2,1)} %copy-done.47, f32[1024,768]{1,0:T(8,128)} %get-tuple-element.280.refs_1_, bf16[2048,768]{1,0:T(8,128)(2,1)} %assemble.2.refs_2_.refs_4_), custom_call_target="tpu_custom_call" | custom-call | flops 4154362880 | bytes 1 | tf_op jit(solution)/shard_map/ffn/pallas_call | solution.py:37
  340.0 12.7 %grad_pair.2 = (bf16[512,768]{1,0:T(8,128)(2,1)}, bf16[512,768]{1,0:T(8,128)(2,1)}, bf16[512,768]{1,0:T(8,128)(2,1)}, bf16[512,768]{1,0:T(8,128)(2,1)}) custom-call(s32[7]{0:T(128)} %pad_add_fusion.info, bf16[1024,2048]{1,0:T(8,128)(2,1)} %join.14.refs_0_.act_near, bf16[1024,2048]{1,0:T(8,128)(2,1)} %copy-done.47, ...), custom_call_target="tpu_custom_call" | custom-call | flops 4576414720 | bytes 1 | tf_op jit(solution)/shard_map/grad_pair/pallas_call | solution.py:37
  357.6 15.8 %ffn.6 = (bf16[1024,384]{1,0:T(8,128)(2,1)}, bf16[1024,640]{1,0:T(8,128)(2,1)}, bf16[1024,2048]{1,0:T(8,128)(2,1)}) custom-call(s32[7]{0:T(128)} %pad_add_fusion.info, bf16[1024,2048]{1,0:T(8,128)(2,1)} %copy-done.47, f32[1024,768]{1,0:T(8,128)} %get-tuple-element.280.refs_1_, bf16[2048,640]{1,0:T(8,128)(2,1)} %assemble.3.refs_2_, ...), custom_call_target="tpu_custom_call" | custom-call | flops 6023449600 | bytes 1 | tf_op jit(solution)/shard_map/ffn/pallas_call | solution.py:37
  375.6 15.8 %ffn.7 = (bf16[1024,384]{1,0:T(8,128)(2,1)}, bf16[1024,640]{1,0:T(8,128)(2,1)}, bf16[1024,2048]{1,0:T(8,128)(2,1)}) custom-call(s32[7]{0:T(128)} %pad_add_fusion.info, bf16[1024,2048]{1,0:T(8,128)(2,1)} %join.14.refs_0_.act_near, f32[1024,768]{1,0:T(8,128)} %get-tuple-element.267.refs_1_, bf16[2048,640]{1,0:T(8,128)(2,1)} %assemble.3.refs_2_, ...), custom_call_target="tpu_custom_call" | custom-call | flops 6023449600 | bytes 1 | tf_op jit(solution)/shard_map/ffn/pallas_call | solution.py:37
  407.9 12.4 %grad_pair.3 = (bf16[512,640]{1,0:T(8,128)(2,1)}, bf16[512,640]{1,0:T(8,128)(2,1)}, bf16[512,640]{1,0:T(8,128)(2,1)}, bf16[512,640]{1,0:T(8,128)(2,1)}) custom-call(s32[7]{0:T(128)} %pad_add_fusion.info, bf16[1024,2048]{1,0:T(8,128)(2,1)} %join.14.refs_0_.act_near, bf16[1024,2048]{1,0:T(8,128)(2,1)} %copy-done.47, ...), custom_call_target="tpu_custom_call" | custom-call | flops 4335242240 | bytes 1 | tf_op jit(solution)/shard_map/grad_pair/pallas_call | solution.py:37
  422.8 11.6 %grad_down.1 = (bf16[176,2048]{1,0:T(8,128)(2,1)}, bf16[176,2048]{1,0:T(8,128)(2,1)}, bf16[176,2048]{1,0:T(8,128)(2,1)}, bf16[176,2048]{1,0:T(8,128)(2,1)}) custom-call(s32[7]{0:T(128)} %pad_add_fusion.info, bf16[1024,384]{1,0:T(8,128)(2,1)} %get-tuple-element.277.first_near.a, bf16[1024,384]{1,0:T(8,128)(2,1)} %get-tuple-element.281.first_far.a, ...), custom_call_target="tpu_custom_call" | custom-call | flops 4516121600 | bytes 1 | tf_op jit(solution)/shard_map/grad_down/pallas_call | solution.py:37
  434.3 9.0 %down_product.2 = bf16[1024,2048]{1,0:T(8,128)(2,1)} custom-call(s32[7]{0:T(128)} %pad_add_fusion.info, bf16[1024,384]{1,0:T(8,128)(2,1)} %get-tuple-element.277.first_near.a, bf16[384,2048]{1,0:T(8,128)(2,1)} %get-tuple-element.264.first.b, bf16[1024,384]{1,0:T(8,128)(2,1)} %get-tuple-element.291.second_near.c, bf16[384,2048]{1,0:T(8,128)(2,1)} %get-tuple-element.266.second.d), custom_call_target="tpu_custom_call" | custom-call | flops 3249966080 | bytes 1 | tf_op jit(solution)/shard_map/down_product/pallas_call | solution.py:37
  443.3 9.3 %collective-permute-done.50.refs_3_ = bf16[256,2048]{1,0:T(8,128)(2,1)S(1)} collective-permute-done((bf16[256,2048]{1,0:T(8,128)(2,1)}, bf16[256,2048]{1,0:T(8,128)(2,1)S(1)}, u32[]{:S(2)}, u32[]{:S(2)}) %collective-permute-start.50) | collective-permute-done | bytes 1048608 | tf_op jit(solution)/shard_map/ppermute | solution.py:75
  453.7 14.2 %grad_attn.1 = (f32[256,2048]{1,0:T(8,128)}, bf16[256,2048]{1,0:T(8,128)(2,1)}, bf16[1024,256]{1,0:T(8,128)(2,1)}, bf16[1024,256]{1,0:T(8,128)(2,1)}) custom-call(s32[7]{0:T(128)} %pad_add_fusion.info, f32[256,2048]{1,0:T(8,128)} %get-tuple-element.298.refs_0_, bf16[256,2048]{1,0:T(8,128)(2,1)} %copy-done.53, bf16[256,2048]{1,0:T(8,128)(2,1)} %copy-done.54, ...), custom_call_target="tpu_custom_call" | custom-call | flops 6023685120 | bytes 1 | tf_op jit(solution)/shard_map/grad_attn/pallas_call | solution.py:37
  495.1 8.9 %down_product.3 = bf16[1024,2048]{1,0:T(8,128)(2,1)} custom-call(s32[7]{0:T(128)} %pad_add_fusion.info, bf16[1024,384]{1,0:T(8,128)(2,1)} %get-tuple-element.281.first_far.a, bf16[384,2048]{1,0:T(8,128)(2,1)} %get-tuple-element.264.first.b, bf16[1024,384]{1,0:T(8,128)(2,1)} %get-tuple-element.289.second_far.c, bf16[384,2048]{1,0:T(8,128)(2,1)} %get-tuple-element.266.second.d), custom_call_target="tpu_custom_call" | custom-call | flops 3249966080 | bytes 1 | tf_op jit(solution)/shard_map/down_product/pallas_call | solution.py:37
  508.6 14.0 %attend_back.2.near.far.first = bf16[2048,384]{1,0:T(8,128)(2,1)} custom-call(s32[7]{0:T(128)} %pad_add_fusion.info, bf16[2048,768]{1,0:T(8,128)(2,1)} %bitcast.75, bf16[512,256]{1,0:T(8,128)(2,1)} %get-tuple-element.327.refs_0_, bf16[512,256]{1,0:T(8,128)(2,1)} %copy-done.77, bf16[512,256]{1,0:T(8,128)(2,1)} %copy-done.78, bf16[512,256]{1,0:T(8,128)(2,1)} %copy-done.79, ...), custom_call_target="tpu_custom_call" | custom-call | flops 3012561920 | bytes 1 | tf_op jit(solution)/shard_map/attend_back/pallas_call | solution.py:37
  532.7 10.1 %grad_qkv.2 = (bf16[512,384]{1,0:T(8,128)(2,1)}, bf16[512,384]{1,0:T(8,128)(2,1)}, bf16[512,384]{1,0:T(8,128)(2,1)}, bf16[512,384]{1,0:T(8,128)(2,1)}) custom-call(s32[7]{0:T(128)} %pad_add_fusion.info, bf16[1024,2048]{1,0:T(8,128)(2,1)} %get-tuple-element.346.act_near, bf16[1024,2048]{1,0:T(8,128)(2,1)} %get-tuple-element.347.act_far, ...), custom_call_target="tpu_custom_call" | custom-call | flops 4214656000 | bytes 1 | tf_op jit(solution)/shard_map/grad_qkv/pallas_call | solution.py:37
  544.6 16.8 %collective-permute-done.63 = bf16[512,640]{1,0:T(8,128)(2,1)S(1)} collective-permute-done((bf16[512,640]{1,0:T(8,128)(2,1)S(1)}, bf16[512,640]{1,0:T(8,128)(2,1)S(1)}, u32[]{:S(2)}, u32[]{:S(2)}) %collective-permute-start.63) | collective-permute-done | bytes 655392 | tf_op jit(solution)/shard_map/ppermute | solution.py:110
  562.9 14.0 %attend_back.3.near.far.second = bf16[2048,384]{1,0:T(8,128)(2,1)} custom-call(s32[7]{0:T(128)} %pad_add_fusion.info, bf16[2048,768]{1,0:T(8,128)(2,1)} %bitcast.76, bf16[512,256]{1,0:T(8,128)(2,1)} %get-tuple-element.327.refs_0_, bf16[512,256]{1,0:T(8,128)(2,1)} %copy-done.77, bf16[512,256]{1,0:T(8,128)(2,1)} %copy-done.78, bf16[512,256]{1,0:T(8,128)(2,1)} %copy-done.79, ...), custom_call_target="tpu_custom_call" | custom-call | flops 3012561920 | bytes 1 | tf_op jit(solution)/shard_map/attend_back/pallas_call | solution.py:37
  592.0 9.7 %grad_qkv.3 = (bf16[512,384]{1,0:T(8,128)(2,1)}, bf16[512,384]{1,0:T(8,128)(2,1)}, bf16[512,384]{1,0:T(8,128)(2,1)}, bf16[512,384]{1,0:T(8,128)(2,1)}) custom-call(s32[7]{0:T(128)} %pad_add_fusion.info, bf16[1024,2048]{1,0:T(8,128)(2,1)} %get-tuple-element.346.act_near, bf16[1024,2048]{1,0:T(8,128)(2,1)} %get-tuple-element.347.act_far, ...), custom_call_target="tpu_custom_call" | custom-call | flops 4214656000 | bytes 1 | tf_op jit(solution)/shard_map/grad_qkv/pallas_call | solution.py:37
  602.0 9.2 %back_product.2 = bf16[1024,2048]{1,0:T(8,128)(2,1)} custom-call(s32[7]{0:T(128)} %pad_add_fusion.info, bf16[2048,384]{1,0:T(8,128)(2,1)} %attend_back.2.near.far.first, bf16[2048,384]{1,0:T(8,128)(2,1)} %attend_back.3.near.far.second, bf16[2048,768]{1,0:T(8,128)(2,1)} %get-tuple-element.378.weight), custom_call_target="tpu_custom_call" | custom-call | flops 3611724800 | bytes 1 | tf_op jit(solution)/shard_map/back_product/pallas_call | solution.py:37
  616.7 20.4 %collective-permute-done.66.first = bf16[2048,256]{1,0:T(8,128)(2,1)} collective-permute-done((bf16[2048,256]{1,0:T(8,128)(2,1)}, bf16[2048,256]{1,0:T(8,128)(2,1)}, u32[]{:S(2)}, u32[]{:S(2)}) %collective-permute-start.66) | collective-permute-done | bytes 1048608 | tf_op jit(solution)/shard_map/ppermute | solution.py:75
  638.3 22.3 %collective-permute-done.68.third = bf16[2048,256]{1,0:T(8,128)(2,1)} collective-permute-done((bf16[2048,256]{1,0:T(8,128)(2,1)S(1)}, bf16[2048,256]{1,0:T(8,128)(2,1)}, u32[]{:S(2)}, u32[]{:S(2)}) %collective-permute-start.68) | collective-permute-done | bytes 1048608 | tf_op jit(solution)/shard_map/ppermute | solution.py:75
  664.3 9.1 %back_product.3 = bf16[1024,2048]{1,0:T(8,128)(2,1)} custom-call(s32[7]{0:T(128)} %pad_add_fusion.info, bf16[2048,384]{1,0:T(8,128)(2,1)} %attend_back.2.near.far.first, bf16[2048,384]{1,0:T(8,128)(2,1)} %attend_back.3.near.far.second, bf16[2048,768]{1,0:T(8,128)(2,1)} %get-tuple-element.378.weight), custom_call_target="tpu_custom_call" | custom-call | flops 3611724800 | bytes 1 | tf_op jit(solution)/shard_map/back_product/pallas_call | solution.py:37
  679.1 30.2 %collective-permute-done.69 = bf16[256,2048]{1,0:T(8,128)(2,1)S(1)} collective-permute-done((bf16[256,2048]{1,0:T(8,128)(2,1)}, bf16[256,2048]{1,0:T(8,128)(2,1)S(1)}, u32[]{:S(2)}, u32[]{:S(2)}) %collective-permute-start.69) | collective-permute-done | bytes 1048608 | tf_op jit(solution)/shard_map/ppermute | solution.py:75
  727.8 12.5 %collective-permute-done.86.refs_3_ = bf16[512,640]{1,0:T(8,128)(2,1)} collective-permute-done((bf16[512,640]{1,0:T(8,128)(2,1)}, bf16[512,640]{1,0:T(8,128)(2,1)}, u32[]{:S(2)}, u32[]{:S(2)}) %collective-permute-start.86) | collective-permute-done | bytes 655392 | tf_op jit(solution)/shard_map/ppermute | solution.py:75
  741.7 10.8 %finish_pair.1 = (f32[128,5504]{1,0:T(8,128)}, f32[128,5504]{1,0:T(8,128)}, f32[128,1]{1,0:T(8,128)}) custom-call(s32[7]{0:T(128)} %pad_add_fusion.info, bf16[512,768]{1,0:T(8,128)(2,1)} %join.15.refs_0_, bf16[512,768]{1,0:T(8,128)(2,1)} %collective-permute-done.85.refs_1_, bf16[512,640]{1,0:T(8,128)(2,1)} %join.16.refs_2_, ...), custom_call_target="tpu_custom_call" | custom-call | flops 3807912960 | bytes 1 | tf_op jit(solution)/shard_map/finish_pair/pallas_call | solution.py:37
  794.0 45.4 %collective-permute-done.101.refs_1_ = bf16[512,384]{1,0:T(8,128)(2,1)} collective-permute-done((bf16[512,384]{1,0:T(8,128)(2,1)}, bf16[512,384]{1,0:T(8,128)(2,1)}, u32[]{:S(2)}, u32[]{:S(2)}) %collective-permute-start.101) | collective-permute-done | bytes 393248 | tf_op jit(solution)/shard_map/ppermute | solution.py:75
  (506 shorter events, 392.6 us)
Async XLA Ops:
  14.9 34.1 %collective-permute-start.11 = (bf16[256,2048]{1,0:T(8,128)(2,1)}, bf16[256,2048]{1,0:T(8,128)(2,1)}, u32[]{:S(2)}, u32[]{:S(2)}) collective-permute-start(bf16[256,2048]{1,0:T(8,128)(2,1)} %bitcast.16.refs_0_.refs_5_), channel_id=1, source_target_pairs={{0,16},{16,0},{1,17},{17,1},{2,18},{18,2},{3,19},{19,3},{4,20},{20... | collective-permute-start | bytes 3145736 | tf_op jit(solution)/shard_map/ppermute | solution.py:75
  39.3 41.3 %collective-permute-start.10 = (bf16[512,768]{1,0:T(8,128)(2,1)}, bf16[512,768]{1,0:T(8,128)(2,1)}, u32[]{:S(2)}, u32[]{:S(2)}) collective-permute-start(bf16[512,768]{1,0:T(8,128)(2,1)} %get-tuple-element.220.refs_0_), channel_id=1, source_target_pairs={{0,4},{4,12},{12,8},{8,0},{1,5},{5,13},{13,9},{9,1},{2,6},{6,14},{... | collective-permute-start | bytes 2359304 | tf_op jit(solution)/shard_map/ppermute | solution.py:110
  90.0 41.7 %collective-permute-start.15 = (bf16[1024,2048]{1,0:T(8,128)(2,1)}, bf16[1024,2048]{1,0:T(8,128)(2,1)}, u32[]{:S(2)}, u32[]{:S(2)}) collective-permute-start(bf16[1024,2048]{1,0:T(8,128)(2,1)} %join.11.near), channel_id=1, source_target_pairs={{0,1},{1,0},{2,3},{3,2},{4,5},{5,4},{6,7},{7,6},{8,9},{9,8},{10,11... | collective-permute-start | bytes 12582920 | tf_op jit(solution)/shard_map/ppermute | solution.py:75
  154.2 36.5 %collective-permute-start.22 = (bf16[8192,256]{1,0:T(8,128)(2,1)}, bf16[8192,256]{1,0:T(8,128)(2,1)S(1)}, u32[]{:S(2)}, u32[]{:S(2)}) collective-permute-start(bf16[8192,256]{1,0:T(8,128)(2,1)} %join.12.refs_0_), channel_id=1, source_target_pairs={{0,1},{1,0},{2,3},{3,2},{4,5},{5,4},{6,7},{7,6},{8,9},{9,8},{10,11... | collective-permute-start | bytes 12582920 | tf_op jit(solution)/shard_map/ppermute | solution.py:75
  155.1 35.6 %collective-permute-start.23 = (bf16[176,2048]{1,0:T(8,128)(2,1)}, bf16[176,2048]{1,0:T(8,128)(2,1)}, u32[]{:S(2)}, u32[]{:S(2)}) collective-permute-start(bf16[176,2048]{1,0:T(8,128)(2,1)} %collective-permute-done.refs_1_), channel_id=1, source_target_pairs={{0,4},{4,12},{12,8},{8,0},{1,5},{5,13},{13,9},{9,1},{2,6},{6,14},{... | collective-permute-start | bytes 2162696 | tf_op jit(solution)/shard_map/ppermute | solution.py:110
  159.0 49.8 %collective-permute-start.29 = (bf16[256,2048]{1,0:T(8,128)(2,1)}, bf16[256,2048]{1,0:T(8,128)(2,1)S(1)}, u32[]{:S(2)}, u32[]{:S(2)}) collective-permute-start(bf16[256,2048]{1,0:T(8,128)(2,1)} %bitcast.19.refs_0_.refs_4_), channel_id=1, source_target_pairs={{0,16},{16,0},{1,17},{17,1},{2,18},{18,2},{3,19},{19,3},{4,20},{20... | collective-permute-start | bytes 3145736 | tf_op jit(solution)/shard_map/ppermute | solution.py:75
  160.5 48.8 %collective-permute-start.30 = (bf16[256,2048]{1,0:T(8,128)(2,1)}, bf16[256,2048]{1,0:T(8,128)(2,1)S(1)}, u32[]{:S(2)}, u32[]{:S(2)}) collective-permute-start(bf16[256,2048]{1,0:T(8,128)(2,1)} %bitcast.19.refs_0_.refs_4_), channel_id=1, source_target_pairs={{0,2},{2,0},{1,3},{3,1},{4,6},{6,4},{5,7},{7,5},{8,10},{10,8},{9,1... | collective-permute-start | bytes 3145736 | tf_op jit(solution)/shard_map/ppermute | solution.py:75
  238.4 31.3 %collective-permute-start.35 = (bf16[1024,2048]{1,0:T(8,128)(2,1)}, bf16[1024,2048]{1,0:T(8,128)(2,1)S(1)}, u32[]{:S(2)}, u32[]{:S(2)}) collective-permute-start(bf16[1024,2048]{1,0:T(8,128)(2,1)} %join.13.near.refs_0_), channel_id=1, source_target_pairs={{0,1},{1,0},{2,3},{3,2},{4,5},{5,4},{6,7},{7,6},{8,9},{9,8},{10,11... | collective-permute-start | bytes 12582920 | tf_op jit(solution)/shard_map/ppermute | solution.py:75
  244.9 46.7 %collective-permute-start.36 = (bf16[512,768]{1,0:T(8,128)(2,1)}, bf16[512,768]{1,0:T(8,128)(2,1)}, u32[]{:S(2)}, u32[]{:S(2)}) collective-permute-start(bf16[512,768]{1,0:T(8,128)(2,1)} %copy-done.58), channel_id=1, source_target_pairs={{0,4},{4,12},{12,8},{8,0},{1,5},{5,13},{13,9},{9,1},{2,6},{6,14},{... | collective-permute-start | bytes 2359304 | tf_op jit(solution)/shard_map/ppermute | solution.py:110
  319.1 33.6 %collective-permute-start.44 = (bf16[512,640]{1,0:T(8,128)(2,1)S(1)}, bf16[512,640]{1,0:T(8,128)(2,1)S(1)}, u32[]{:S(2)}, u32[]{:S(2)}) collective-permute-start(bf16[512,640]{1,0:T(8,128)(2,1)S(1)} %collective-permute-done.43.refs_2_), channel_id=1, source_target_pairs={{0,4},{4,12},{12,8},{8,0},{1,5},{5,13},{13,9},{9,1},{2,6},{6,14},{... | collective-permute-start | bytes 1966088 | tf_op jit(solution)/shard_map/ppermute | solution.py:110
  404.4 38.9 %collective-permute-start.48 = (bf16[256,2048]{1,0:T(8,128)(2,1)}, bf16[256,2048]{1,0:T(8,128)(2,1)S(1)}, u32[]{:S(2)}, u32[]{:S(2)}) collective-permute-start(bf16[256,2048]{1,0:T(8,128)(2,1)} %get-tuple-element.309), channel_id=1, source_target_pairs={{0,16},{16,0},{1,17},{17,1},{2,18},{18,2},{3,19},{19,3},{4,20},{20... | collective-permute-start | bytes 3145736 | tf_op jit(solution)/shard_map/ppermute | solution.py:75
  404.9 38.5 %collective-permute-start.49 = (bf16[256,2048]{1,0:T(8,128)(2,1)}, bf16[256,2048]{1,0:T(8,128)(2,1)S(1)}, u32[]{:S(2)}, u32[]{:S(2)}) collective-permute-start(bf16[256,2048]{1,0:T(8,128)(2,1)} %get-tuple-element.310), channel_id=1, source_target_pairs={{0,2},{2,0},{1,3},{3,1},{4,6},{6,4},{5,7},{7,5},{8,10},{10,8},{9,1... | collective-permute-start | bytes 3145736 | tf_op jit(solution)/shard_map/ppermute | solution.py:75
  405.4 47.3 %collective-permute-start.50 = (bf16[256,2048]{1,0:T(8,128)(2,1)}, bf16[256,2048]{1,0:T(8,128)(2,1)S(1)}, u32[]{:S(2)}, u32[]{:S(2)}) collective-permute-start(bf16[256,2048]{1,0:T(8,128)(2,1)} %get-tuple-element.311), channel_id=1, source_target_pairs={{0,18},{2,16},{16,2},{18,0},{1,19},{3,17},{17,3},{19,1},{4,22},{6,... | collective-permute-start | bytes 3145736 | tf_op jit(solution)/shard_map/ppermute | solution.py:75
  420.5 47.4 %collective-permute-start.51 = (bf16[512,768]{1,0:T(8,128)(2,1)S(1)}, bf16[512,768]{1,0:T(8,128)(2,1)S(1)}, u32[]{:S(2)}, u32[]{:S(2)}) collective-permute-start(bf16[512,768]{1,0:T(8,128)(2,1)S(1)} %add_convert_fusion.2), channel_id=1, source_target_pairs={{0,4},{4,12},{12,8},{8,0},{1,5},{5,13},{13,9},{9,1},{2,6},{6,14},{... | collective-permute-start | bytes 2359304 | tf_op jit(solution)/shard_map/ppermute | solution.py:110
  421.7 54.8 %collective-permute-start.52 = (bf16[512,640]{1,0:T(8,128)(2,1)S(1)}, bf16[512,640]{1,0:T(8,128)(2,1)S(1)}, u32[]{:S(2)}, u32[]{:S(2)}) collective-permute-start(bf16[512,640]{1,0:T(8,128)(2,1)S(1)} %copy-done.65), channel_id=1, source_target_pairs={{0,4},{4,12},{12,8},{8,0},{1,5},{5,13},{13,9},{9,1},{2,6},{6,14},{... | collective-permute-start | bytes 1966088 | tf_op jit(solution)/shard_map/ppermute | solution.py:110
  480.9 44.7 %collective-permute-start.61 = (bf16[4,2048,256]{2,1,0:T(8,128)(2,1)S(1)}, bf16[4,2048,256]{2,1,0:T(8,128)(2,1)}, u32[]{:S(2)}, u32[]{:S(2)}) collective-permute-start(bf16[4,2048,256]{2,1,0:T(8,128)(2,1)S(1)} %copy-done.46), channel_id=1, source_target_pairs={{0,1},{1,0},{2,3},{3,2},{4,5},{5,4},{6,7},{7,6},{8,9},{9,8},{10,11... | collective-permute-start | bytes 12582920 | tf_op jit(solution)/shard_map/ppermute | solution.py:75
  483.7 38.9 %collective-permute-start.60 = (bf16[512,640]{1,0:T(8,128)(2,1)S(1)}, bf16[512,640]{1,0:T(8,128)(2,1)S(1)}, u32[]{:S(2)}, u32[]{:S(2)}) collective-permute-start(bf16[512,640]{1,0:T(8,128)(2,1)S(1)} %add_convert_fusion.9), channel_id=1, source_target_pairs={{0,4},{4,12},{12,8},{8,0},{1,5},{5,13},{13,9},{9,1},{2,6},{6,14},{... | collective-permute-start | bytes 1966088 | tf_op jit(solution)/shard_map/ppermute | solution.py:110
  542.8 35.9 %collective-permute-start.65 = (bf16[1024,2048]{1,0:T(8,128)(2,1)S(1)}, bf16[1024,2048]{1,0:T(8,128)(2,1)}, u32[]{:S(2)}, u32[]{:S(2)}) collective-permute-start(bf16[1024,2048]{1,0:T(8,128)(2,1)S(1)} %copy-done.45), channel_id=1, source_target_pairs={{0,1},{1,0},{2,3},{3,2},{4,5},{5,4},{6,7},{7,6},{8,9},{9,8},{10,11... | collective-permute-start | bytes 12582920 | tf_op jit(solution)/shard_map/ppermute | solution.py:75
  544.3 32.6 %collective-permute-start.64 = (bf16[176,2048]{1,0:T(8,128)(2,1)S(1)}, bf16[176,2048]{1,0:T(8,128)(2,1)S(1)}, u32[]{:S(2)}, u32[]{:S(2)}) collective-permute-start(bf16[176,2048]{1,0:T(8,128)(2,1)S(1)} %add_convert_fusion.6), channel_id=1, source_target_pairs={{0,4},{4,12},{12,8},{8,0},{1,5},{5,13},{13,9},{9,1},{2,6},{6,14},{... | collective-permute-start | bytes 2162696 | tf_op jit(solution)/shard_map/ppermute | solution.py:110
  611.2 101.3 %collective-permute-start.79 = (bf16[1024,2048]{1,0:T(8,128)(2,1)}, bf16[1024,2048]{1,0:T(8,128)(2,1)}, u32[]{:S(2)}, u32[]{:S(2)}) collective-permute-start(bf16[1024,2048]{1,0:T(8,128)(2,1)} %back_product.2), channel_id=1, source_target_pairs={{0,1},{1,0},{2,3},{3,2},{4,5},{5,4},{6,7},{7,6},{8,9},{9,8},{10,11... | collective-permute-start | bytes 12582920 | tf_op jit(solution)/shard_map/ppermute | solution.py:75
  612.3 48.2 %collective-permute-start.68 = (bf16[2048,256]{1,0:T(8,128)(2,1)S(1)}, bf16[2048,256]{1,0:T(8,128)(2,1)}, u32[]{:S(2)}, u32[]{:S(2)}) collective-permute-start(bf16[2048,256]{1,0:T(8,128)(2,1)S(1)} %copy-done.50), channel_id=1, source_target_pairs={{0,18},{2,16},{16,2},{18,0},{1,19},{3,17},{17,3},{19,1},{4,22},{6,... | collective-permute-start | bytes 3145736 | tf_op jit(solution)/shard_map/ppermute | solution.py:75
  615.5 63.0 %collective-permute-start.78 = (bf16[512,384]{1,0:T(8,128)(2,1)}, bf16[512,384]{1,0:T(8,128)(2,1)S(1)}, u32[]{:S(2)}, u32[]{:S(2)}) collective-permute-start(bf16[512,384]{1,0:T(8,128)(2,1)} %get-tuple-element.385), channel_id=1, source_target_pairs={{0,4},{4,12},{12,8},{8,0},{1,5},{5,13},{13,9},{9,1},{2,6},{6,14},{... | collective-permute-start | bytes 1179656 | tf_op jit(solution)/shard_map/ppermute | solution.py:110
  660.5 48.8 %collective-permute-start.69 = (bf16[256,2048]{1,0:T(8,128)(2,1)}, bf16[256,2048]{1,0:T(8,128)(2,1)S(1)}, u32[]{:S(2)}, u32[]{:S(2)}) collective-permute-start(bf16[256,2048]{1,0:T(8,128)(2,1)} %get-tuple-element.365), channel_id=1, source_target_pairs={{0,16},{16,0},{1,17},{17,1},{2,18},{18,2},{3,19},{19,3},{4,20},{20... | collective-permute-start | bytes 3145736 | tf_op jit(solution)/shard_map/ppermute | solution.py:75
  661.0 48.8 %collective-permute-start.70 = (bf16[256,2048]{1,0:T(8,128)(2,1)}, bf16[256,2048]{1,0:T(8,128)(2,1)S(1)}, u32[]{:S(2)}, u32[]{:S(2)}) collective-permute-start(bf16[256,2048]{1,0:T(8,128)(2,1)} %get-tuple-element.366), channel_id=1, source_target_pairs={{0,2},{2,0},{1,3},{3,1},{4,6},{6,4},{5,7},{7,5},{8,10},{10,8},{9,1... | collective-permute-start | bytes 3145736 | tf_op jit(solution)/shard_map/ppermute | solution.py:75
  661.7 49.6 %collective-permute-start.71 = (bf16[256,2048]{1,0:T(8,128)(2,1)}, bf16[256,2048]{1,0:T(8,128)(2,1)S(1)}, u32[]{:S(2)}, u32[]{:S(2)}) collective-permute-start(bf16[256,2048]{1,0:T(8,128)(2,1)} %get-tuple-element.367), channel_id=1, source_target_pairs={{0,18},{2,16},{16,2},{18,0},{1,19},{3,17},{17,3},{19,1},{4,22},{6,... | collective-permute-start | bytes 3145736 | tf_op jit(solution)/shard_map/ppermute | solution.py:75
  678.4 49.3 %collective-permute-start.85 = (bf16[512,768]{1,0:T(8,128)(2,1)}, bf16[512,768]{1,0:T(8,128)(2,1)}, u32[]{:S(2)}, u32[]{:S(2)}) collective-permute-start(bf16[512,768]{1,0:T(8,128)(2,1)} %join.15.refs_0_), channel_id=1, source_target_pairs={{0,16},{16,0},{1,17},{17,1},{2,18},{18,2},{3,19},{19,3},{4,20},{20... | collective-permute-start | bytes 2359304 | tf_op jit(solution)/shard_map/ppermute | solution.py:75
  709.8 45.1 %collective-permute-start.103 = (bf16[172,2048]{1,0:T(8,128)(2,1)S(1)}, bf16[172,2048]{1,0:T(8,128)(2,1)S(1)}, u32[]{:S(2)}, u32[]{:S(2)}) collective-permute-start(bf16[172,2048]{1,0:T(8,128)(2,1)S(1)} %get-tuple-element.432), channel_id=1, source_target_pairs={{0,16},{16,0},{1,17},{17,1},{2,18},{18,2},{3,19},{19,3},{4,20},{20... | collective-permute-start | bytes 2113544 | tf_op jit(solution)/shard_map/ppermute | solution.py:75
  778.9 75.6 %collective-permute-start.80 = (bf16[256,2048]{1,0:T(8,128)(2,1)}, bf16[256,2048]{1,0:T(8,128)(2,1)S(1)}, u32[]{:S(2)}, u32[]{:S(2)}) collective-permute-start(bf16[256,2048]{1,0:T(8,128)(2,1)} %get-tuple-element.390), channel_id=1, source_target_pairs={{0,16},{16,0},{1,17},{17,1},{2,18},{18,2},{3,19},{19,3},{4,20},{20... | collective-permute-start | bytes 3145736 | tf_op jit(solution)/shard_map/ppermute | solution.py:75
  780.5 74.0 %collective-permute-start.81 = (bf16[256,2048]{1,0:T(8,128)(2,1)}, bf16[256,2048]{1,0:T(8,128)(2,1)}, u32[]{:S(2)}, u32[]{:S(2)}) collective-permute-start(bf16[256,2048]{1,0:T(8,128)(2,1)} %get-tuple-element.391), channel_id=1, source_target_pairs={{0,2},{2,0},{1,3},{3,1},{4,6},{6,4},{5,7},{7,5},{8,10},{10,8},{9,1... | collective-permute-start | bytes 3145736 | tf_op jit(solution)/shard_map/ppermute | solution.py:75
  781.7 72.8 %collective-permute-start.82 = (bf16[256,2048]{1,0:T(8,128)(2,1)}, bf16[256,2048]{1,0:T(8,128)(2,1)}, u32[]{:S(2)}, u32[]{:S(2)}) collective-permute-start(bf16[256,2048]{1,0:T(8,128)(2,1)} %get-tuple-element.392), channel_id=1, source_target_pairs={{0,18},{2,16},{16,2},{18,0},{1,19},{3,17},{17,3},{19,1},{4,22},{6,... | collective-permute-start | bytes 3145736 | tf_op jit(solution)/shard_map/ppermute | solution.py:75
  783.1 56.3 %collective-permute-start.101 = (bf16[512,384]{1,0:T(8,128)(2,1)}, bf16[512,384]{1,0:T(8,128)(2,1)}, u32[]{:S(2)}, u32[]{:S(2)}) collective-permute-start(bf16[512,384]{1,0:T(8,128)(2,1)} %join.17.refs_0_), channel_id=1, source_target_pairs={{0,16},{16,0},{1,17},{17,1},{2,18},{18,2},{3,19},{19,3},{4,20},{20... | collective-permute-start | bytes 1179656 | tf_op jit(solution)/shard_map/ppermute | solution.py:75
  787.1 60.3 %collective-permute-start.102 = (bf16[512,384]{1,0:T(8,128)(2,1)}, bf16[512,384]{1,0:T(8,128)(2,1)}, u32[]{:S(2)}, u32[]{:S(2)}) collective-permute-start(bf16[512,384]{1,0:T(8,128)(2,1)} %join.19.refs_2_), channel_id=1, source_target_pairs={{0,16},{16,0},{1,17},{17,1},{2,18},{18,2},{3,19},{19,3},{4,20},{20... | collective-permute-start | bytes 1179656 | tf_op jit(solution)/shard_map/ppermute | solution.py:75
  (172 other events, 2213.2 us)

commit v3 on v2

--- a/solution.py
+++ b/solution.py
@@ -1059,14 +1059,14 @@
 
     need(down_got[1], *pieces[1:])
     qkv_plane, out_plane = do(join_two, info, 3 * (width // 8), *pieces)
-    out_got = lane_a.gather(out_plane)
+    out_got = lane_b.gather(out_plane)
     qkv_got = lane_b.gather(qkv_plane)
-    need(out_got[1], *pair_pieces[1:])
+    need(*out_got)
+    out_cols = do(join, info, *out_got)
+    need(qkv_got[1], *pair_pieces[1:])
     pair_first, pair_second = do(join_two, info, 2 * planes * pads[0], *pair_pieces)
-    need(*out_got, qkv_got[1])
-    out_cols = do(join, info, *out_got)
     out_parts = near_parts(out_cols, token_parts[1:2], pair_pieces, token_parts)
-    need(*token_parts)
+    need(*token_parts, qkv_got[2])
     tokens_near = do(join, info, *token_parts)
     tokens_far = hop(tokens_near, 4)
     lane_a.last = (qkv_got[-1],)
@@ -1077,29 +1077,28 @@
     qkv, full_qkv, act_near, act_far = do(
         project, info, tokens_near, tokens_far, qkv_got, cosine, sine
     )
-    need(*out_parts)
+    need(*out_parts, down_got[2], pair_first_got[1])
     out_near = do(join, info, *out_parts)
     out_far = hop(out_near, 4)
     top_parts = near_parts(after(cotangent[0], *out_parts))
     attn_near, attn_far, lse = do(attend, info, qkv)
     moved = hop(attn_far, 4)
-    need(out_far, down_got[2], pair_first_got[1])
+    need(out_far)
     full_out = do(spread, info, out_near, out_far, planes)
-    need(moved)
+    need(moved, pair_first_got[2])
     attn_moved = near_moves(do(meet, info, attn_near, moved))
     need(*attn_moved)
     attn, middle, scale, act_own = do(branch, info, attn_moved, full_out, tokens[0])
     act_parts = near_parts(act_own)
-    need(*top_parts, pair_first_got[2])
+    need(*top_parts, *down_got)
     top_near = do(join, info, *top_parts)
     top_far = hop(top_near, 4)
-    need(*down_got)
+    need(*pair_first_got)
     down_a, down_b = do(stack_planes, info, pads[0], *down_got)
     need(top_far)
     slope_near, slope_far = do(slopes, info, top_near, top_far, down_a, down_b)
-    need(*pair_first_got, pair_second_got[1])
     full_first = do(assemble, info, *pair_first_got)
-    need(*act_parts)
+    need(*act_parts, pair_second_got[1])
     ffn_near = do(join, info, *act_parts)
     ffn_far = hop(ffn_near, 4)
 
@@ -1167,15 +1166,14 @@
         do(grad_rows, info, act_near, act_far, grads_first, grads_first, planes, "grad_qkv", True),
     )
     block_moved = hop(after(block_far, qkv_first.total), 4)
+    grads_second = do(attend_back, info, qkv, attn_grads, lse, cosine, sine, 1)
     pair_b.move()
-    grads_second = do(attend_back, info, qkv, attn_grads, lse, cosine, sine, 1)
-    second_pieces = owners(pair_b.total)
+    second_pieces = owners(after(pair_b.total, *out_parts))
     down_sum.move()
     need(block_moved)
     block_terms = do(combine, info, block_near, block_moved)
     qkv_first.move()
-    need(*second_pieces)
-    sums_second = rows_of(pair_b.total, second_pieces)
+    need(*out_parts)
     qkv_second = Sum(
         order,
         lane_b,
@@ -1193,14 +1191,14 @@
     down_mine = down_sum.total[:half_down]
     down_theirs = hop(down_mine, 1)
     in_near = do(back_product, info, grads_first, grads_second, full_qkv, False)
-    need(*out_parts)
     out_sum = Sum(order, lane_c, do(order_out, info, out_own, out_parts, planes))
+    sums_second = rows_of(pair_b.total, second_pieces)
     qkv_second.move()
-    need(in_moved, *block_parts)
+    need(in_moved)
     in_own, in_parts = scatter_moves(*do(combine, info, in_near, in_moved))
     qkv_first.move()
     out_sum.move()
-    need(*sums_first, *sums_second)
+    need(*sums_first, *sums_second, *block_parts)
     sum_gate, sum_up, gain_sum_ffn = do(
         finish_pair, info, sums_first, sums_second, weight_gate, weight_up, wide_ffn,
         planes, reals, pads,
@@ -1208,6 +1206,7 @@
     first_pieces = owners(qkv_first.total)
     qkv_second.move()
     out_sum.finish()
+    need(*in_parts)
     first_rows = rows_of(qkv_first.total, first_pieces)
     out_pieces = owners(out_sum.total)
     qkv_second.finish()

time: 871 us -> 840 us (0.964)
  waiting for transfers between devices: 314 us -> 288 us
    ppermute x71, waiting for transfers between devices: 186 us -> 157 us  [hop(): return lax.ppermute(block, axes, [(i, last - i) for i in range(last + 1)])]
    unnamed x205 -> x219, local copies, waits for them, and re-layouts: 25.4 us -> 20.1 us
  transfers between devices with their start and end apart: 104 -> 104, of which waited for: 33 -> 38; matrix products, arithmetic and copies ran while one was open for 4% -> 5% of each run, Pallas kernels for 35% -> 36%
where the time goes in v3:
time: 840 us; the launch traced here: 829 us
  Pallas kernels  368 us (44%)
  waiting for transfers between devices  288 us (34%)
  starting transfers between devices  109 us (13%)
  local copies, waits for them, and re-layouts  31.5 us (4%)
  other arithmetic  31.2 us (4%)
    pallas_call x48, Pallas kernels, call(): pl.pallas_call(kernel, grid_spec=pltpu.PrefetchScalarGridSpec(num_scalar_...  368 us
    ppermute x71, waiting for transfers between devices, hop(): return lax.ppermute(block, axes, [(i, last - i) for i in range(last + 1)])  157 us
    ppermute x33, waiting for transfers between devices, hop(): moved = lax.ppermute(block, 'z', self.route)  130 us
    ppermute x71, starting transfers between devices, hop(): return lax.ppermute(block, axes, [(i, last - i) for i in range(last + 1)])  64.6 us
    ppermute x33, starting transfers between devices, hop(): moved = lax.ppermute(block, 'z', self.route)  44 us
    unnamed x219, local copies, waits for them, and re-layouts  20.1 us
  transfers between devices with their start and end apart: 104, of which 38 were waited for; matrix products, arithmetic and copies ran while one was open for 5% of the time, Pallas kernels for 36%

profile of v3, /device:TPU:0, one launch (start us, length us, event | category | flops | bytes accessed | tf_op | source)
XLA Modules:
  0.0 829.1 jit_solution(15053218652080153266)
XLA Ops:
  57.0 17.7 %collective-permute-done.7.refs_1_ = bf16[512,768]{1,0:T(8,128)(2,1)} collective-permute-done((bf16[512,768]{1,0:T(8,128)(2,1)}, bf16[512,768]{1,0:T(8,128)(2,1)}, u32[]{:S(2)}, u32[]{:S(2)}) %collective-permute-start.7) | collective-permute-done | bytes 786464 | tf_op jit(solution)/shard_map/ppermute | solution.py:110
  117.5 14.6 %collective-permute-done.17.refs_3_ = bf16[512,768]{1,0:T(8,128)(2,1)S(1)} collective-permute-done((bf16[512,768]{1,0:T(8,128)(2,1)}, bf16[512,768]{1,0:T(8,128)(2,1)S(1)}, u32[]{:S(2)}, u32[]{:S(2)}) %collective-permute-start.17) | collective-permute-done | bytes 786464 | tf_op jit(solution)/shard_map/ppermute | solution.py:110
  140.1 15.7 %project.1 = (bf16[2048,768]{1,0:T(8,128)(2,1)}, bf16[2,1024,768]{2,1,0:T(8,128)(2,1)}, bf16[1024,2048]{1,0:T(8,128)(2,1)}, bf16[1024,2048]{1,0:T(8,128)(2,1)}) custom-call(s32[7]{0:T(128)} %pad_add_fusion.info, bf16[1024,2048]{1,0:T(8,128)(2,1)} %join.11.near, bf16[1024,2048]{1,0:T(8,128)(2,1)} %collective-permute-done.16.far, ...), custom_call_target="tpu_custom_call" | custom-call | flops 8194001920 | bytes 1 | tf_op jit(solution)/shard_map/project/pallas_call | solution.py:37
  155.8 11.2 %collective-permute-done.22.refs_2_ = bf16[176,2048]{1,0:T(8,128)(2,1)S(1)} collective-permute-done((bf16[176,2048]{1,0:T(8,128)(2,1)S(1)}, bf16[176,2048]{1,0:T(8,128)(2,1)S(1)}, u32[]{:S(2)}, u32[]{:S(2)}) %collective-permute-start.22) | collective-permute-done | bytes 720928 | tf_op jit(solution)/shard_map/ppermute | solution.py:110
  174.1 13.7 %attend.1 = (bf16[1024,256]{1,0:T(8,128)(2,1)}, bf16[1024,256]{1,0:T(8,128)(2,1)}, f32[2,2048,1]{2,1,0:T(8,128)}) custom-call(s32[7]{0:T(128)} %pad_add_fusion.info, bf16[2048,768]{1,0:T(8,128)(2,1)} %bitcast.74), custom_call_target="tpu_custom_call" | custom-call | flops 2168458240 | bytes 1 | tf_op jit(solution)/shard_map/attend/pallas_call | solution.py:37
  220.7 9.2 %branch.1 = (bf16[256,2048]{1,0:T(8,128)(2,1)}, f32[256,2048]{1,0:T(8,128)}, f32[256,1]{1,0:T(8,128)}, bf16[256,2048]{1,0:T(8,128)(2,1)}) custom-call(s32[7]{0:T(128)} %pad_add_fusion.info, bf16[512,256]{1,0:T(8,128)(2,1)} %get-tuple-element.252.refs_0_, bf16[512,256]{1,0:T(8,128)(2,1)} %copy-done.85, bf16[512,256]{1,0:T(8,128)(2,1)} %copy-done.86, ...), custom_call_target="tpu_custom_call" | custom-call | flops 4576650240 | bytes 1 | tf_op jit(solution)/shard_map/branch/pallas_call | solution.py:37
  242.1 18.6 %collective-permute-done.35.refs_3_ = bf16[512,768]{1,0:T(8,128)(2,1)} collective-permute-done((bf16[512,768]{1,0:T(8,128)(2,1)S(1)}, bf16[512,768]{1,0:T(8,128)(2,1)}, u32[]{:S(2)}, u32[]{:S(2)}) %collective-permute-start.35) | collective-permute-done | bytes 786464 | tf_op jit(solution)/shard_map/ppermute | solution.py:110
  268.6 13.5 %slopes.1 = (f32[1024,768]{1,0:T(8,128)}, f32[1024,768]{1,0:T(8,128)}) custom-call(s32[7]{0:T(128)} %pad_add_fusion.info, bf16[1024,2048]{1,0:T(8,128)(2,1)} %join.13.near.refs_0_, bf16[1024,2048]{1,0:T(8,128)(2,1)} %copy-done.40, bf16[384,2048]{1,0:T(8,128)(2,1)} %get-tuple-element.266.first.b, bf16[384,2048]{1,0:T(8,128)(2,1)} %get-tuple-element.268.second.d), custom_call_target="tpu_custom_call" | custom-call | flops 5299932160 | bytes 1 | tf_op jit(solution)/shard_map/slopes/pallas_call | solution.py:37
  291.5 18.2 %collective-permute-done.43.refs_2_ = bf16[512,640]{1,0:T(8,128)(2,1)S(1)} collective-permute-done((bf16[512,640]{1,0:T(8,128)(2,1)}, bf16[512,640]{1,0:T(8,128)(2,1)S(1)}, u32[]{:S(2)}, u32[]{:S(2)}) %collective-permute-start.43) | collective-permute-done | bytes 655392 | tf_op jit(solution)/shard_map/ppermute | solution.py:110
  329.0 12.7 %grad_pair.2 = (bf16[512,768]{1,0:T(8,128)(2,1)}, bf16[512,768]{1,0:T(8,128)(2,1)}, bf16[512,768]{1,0:T(8,128)(2,1)}, bf16[512,768]{1,0:T(8,128)(2,1)}) custom-call(s32[7]{0:T(128)} %pad_add_fusion.info, bf16[1024,2048]{1,0:T(8,128)(2,1)} %join.14.refs_0_.act_near, bf16[1024,2048]{1,0:T(8,128)(2,1)} %copy-done.42, ...), custom_call_target="tpu_custom_call" | custom-call | flops 4576414720 | bytes 1 | tf_op jit(solution)/shard_map/grad_pair/pallas_call | solution.py:37
  346.7 15.8 %ffn.6 = (bf16[1024,384]{1,0:T(8,128)(2,1)}, bf16[1024,640]{1,0:T(8,128)(2,1)}, bf16[1024,2048]{1,0:T(8,128)(2,1)}) custom-call(s32[7]{0:T(128)} %pad_add_fusion.info, bf16[1024,2048]{1,0:T(8,128)(2,1)} %copy-done.42, f32[1024,768]{1,0:T(8,128)} %get-tuple-element.281.refs_1_, bf16[2048,640]{1,0:T(8,128)(2,1)} %assemble.3.refs_2_, ...), custom_call_target="tpu_custom_call" | custom-call | flops 6023449600 | bytes 1 | tf_op jit(solution)/shard_map/ffn/pallas_call | solution.py:37
  365.2 15.8 %ffn.7 = (bf16[1024,384]{1,0:T(8,128)(2,1)}, bf16[1024,640]{1,0:T(8,128)(2,1)}, bf16[1024,2048]{1,0:T(8,128)(2,1)}) custom-call(s32[7]{0:T(128)} %pad_add_fusion.info, bf16[1024,2048]{1,0:T(8,128)(2,1)} %join.14.refs_0_.act_near, f32[1024,768]{1,0:T(8,128)} %get-tuple-element.269.refs_1_, bf16[2048,640]{1,0:T(8,128)(2,1)} %assemble.3.refs_2_, ...), custom_call_target="tpu_custom_call" | custom-call | flops 6023449600 | bytes 1 | tf_op jit(solution)/shard_map/ffn/pallas_call | solution.py:37
  397.7 12.4 %grad_pair.3 = (bf16[512,640]{1,0:T(8,128)(2,1)}, bf16[512,640]{1,0:T(8,128)(2,1)}, bf16[512,640]{1,0:T(8,128)(2,1)}, bf16[512,640]{1,0:T(8,128)(2,1)}) custom-call(s32[7]{0:T(128)} %pad_add_fusion.info, bf16[1024,2048]{1,0:T(8,128)(2,1)} %join.14.refs_0_.act_near, bf16[1024,2048]{1,0:T(8,128)(2,1)} %copy-done.42, ...), custom_call_target="tpu_custom_call" | custom-call | flops 4335242240 | bytes 1 | tf_op jit(solution)/shard_map/grad_pair/pallas_call | solution.py:37
  412.7 11.6 %grad_down.1 = (bf16[176,2048]{1,0:T(8,128)(2,1)}, bf16[176,2048]{1,0:T(8,128)(2,1)}, bf16[176,2048]{1,0:T(8,128)(2,1)}, bf16[176,2048]{1,0:T(8,128)(2,1)}) custom-call(s32[7]{0:T(128)} %pad_add_fusion.info, bf16[1024,384]{1,0:T(8,128)(2,1)} %get-tuple-element.278.first_near.a, bf16[1024,384]{1,0:T(8,128)(2,1)} %get-tuple-element.282.first_far.a, ...), custom_call_target="tpu_custom_call" | custom-call | flops 4516121600 | bytes 1 | tf_op jit(solution)/shard_map/grad_down/pallas_call | solution.py:37
  424.3 9.0 %down_product.2 = bf16[1024,2048]{1,0:T(8,128)(2,1)} custom-call(s32[7]{0:T(128)} %pad_add_fusion.info, bf16[1024,384]{1,0:T(8,128)(2,1)} %get-tuple-element.278.first_near.a, bf16[384,2048]{1,0:T(8,128)(2,1)} %get-tuple-element.266.first.b, bf16[1024,384]{1,0:T(8,128)(2,1)} %get-tuple-element.292.second_near.c, bf16[384,2048]{1,0:T(8,128)(2,1)} %get-tuple-element.268.second.d), custom_call_target="tpu_custom_call" | custom-call | flops 3249966080 | bytes 1 | tf_op jit(solution)/shard_map/down_product/pallas_call | solution.py:37
  433.2 9.3 %collective-permute-done.50.refs_3_ = bf16[256,2048]{1,0:T(8,128)(2,1)S(1)} collective-permute-done((bf16[256,2048]{1,0:T(8,128)(2,1)}, bf16[256,2048]{1,0:T(8,128)(2,1)S(1)}, u32[]{:S(2)}, u32[]{:S(2)}) %collective-permute-start.50) | collective-permute-done | bytes 1048608 | tf_op jit(solution)/shard_map/ppermute | solution.py:75
  443.5 14.2 %grad_attn.1 = (f32[256,2048]{1,0:T(8,128)}, bf16[256,2048]{1,0:T(8,128)(2,1)}, bf16[1024,256]{1,0:T(8,128)(2,1)}, bf16[1024,256]{1,0:T(8,128)(2,1)}) custom-call(s32[7]{0:T(128)} %pad_add_fusion.info, f32[256,2048]{1,0:T(8,128)} %get-tuple-element.299.refs_0_, bf16[256,2048]{1,0:T(8,128)(2,1)} %copy-done.50, bf16[256,2048]{1,0:T(8,128)(2,1)} %copy-done.51, ...), custom_call_target="tpu_custom_call" | custom-call | flops 6023685120 | bytes 1 | tf_op jit(solution)/shard_map/grad_attn/pallas_call | solution.py:37
  485.0 9.0 %down_product.3 = bf16[1024,2048]{1,0:T(8,128)(2,1)} custom-call(s32[7]{0:T(128)} %pad_add_fusion.info, bf16[1024,384]{1,0:T(8,128)(2,1)} %get-tuple-element.282.first_far.a, bf16[384,2048]{1,0:T(8,128)(2,1)} %get-tuple-element.266.first.b, bf16[1024,384]{1,0:T(8,128)(2,1)} %get-tuple-element.290.second_far.c, bf16[384,2048]{1,0:T(8,128)(2,1)} %get-tuple-element.268.second.d), custom_call_target="tpu_custom_call" | custom-call | flops 3249966080 | bytes 1 | tf_op jit(solution)/shard_map/down_product/pallas_call | solution.py:37
  498.5 14.0 %attend_back.2.near.far.first = bf16[2048,384]{1,0:T(8,128)(2,1)} custom-call(s32[7]{0:T(128)} %pad_add_fusion.info, bf16[2048,768]{1,0:T(8,128)(2,1)} %bitcast.75, bf16[512,256]{1,0:T(8,128)(2,1)} %get-tuple-element.328.refs_0_, bf16[512,256]{1,0:T(8,128)(2,1)} %copy-done.81, bf16[512,256]{1,0:T(8,128)(2,1)} %copy-done.82, bf16[512,256]{1,0:T(8,128)(2,1)} %copy-done.83, ...), custom_call_target="tpu_custom_call" | custom-call | flops 3012561920 | bytes 1 | tf_op jit(solution)/shard_map/attend_back/pallas_call | solution.py:37
  522.6 9.6 %grad_qkv.2 = (bf16[512,384]{1,0:T(8,128)(2,1)}, bf16[512,384]{1,0:T(8,128)(2,1)}, bf16[512,384]{1,0:T(8,128)(2,1)}, bf16[512,384]{1,0:T(8,128)(2,1)}) custom-call(s32[7]{0:T(128)} %pad_add_fusion.info, bf16[1024,2048]{1,0:T(8,128)(2,1)} %get-tuple-element.347.act_near, bf16[1024,2048]{1,0:T(8,128)(2,1)} %get-tuple-element.348.act_far, ...), custom_call_target="tpu_custom_call" | custom-call | flops 4214656000 | bytes 1 | tf_op jit(solution)/shard_map/grad_qkv/pallas_call | solution.py:37
  534.8 13.9 %attend_back.3.near.far.second = bf16[2048,384]{1,0:T(8,128)(2,1)} custom-call(s32[7]{0:T(128)} %pad_add_fusion.info, bf16[2048,768]{1,0:T(8,128)(2,1)} %bitcast.76, bf16[512,256]{1,0:T(8,128)(2,1)} %get-tuple-element.328.refs_0_, bf16[512,256]{1,0:T(8,128)(2,1)} %copy-done.81, bf16[512,256]{1,0:T(8,128)(2,1)} %copy-done.82, bf16[512,256]{1,0:T(8,128)(2,1)} %copy-done.83, ...), custom_call_target="tpu_custom_call" | custom-call | flops 3012561920 | bytes 1 | tf_op jit(solution)/shard_map/attend_back/pallas_call | solution.py:37
  554.2 12.1 %collective-permute-done.64 = bf16[176,2048]{1,0:T(8,128)(2,1)S(1)} collective-permute-done((bf16[176,2048]{1,0:T(8,128)(2,1)S(1)}, bf16[176,2048]{1,0:T(8,128)(2,1)S(1)}, u32[]{:S(2)}, u32[]{:S(2)}) %collective-permute-start.64) | collective-permute-done | bytes 720928 | tf_op jit(solution)/shard_map/ppermute | solution.py:110
  578.8 20.3 %collective-permute-done.68.third = bf16[2048,256]{1,0:T(8,128)(2,1)S(1)} collective-permute-done((bf16[2048,256]{1,0:T(8,128)(2,1)}, bf16[2048,256]{1,0:T(8,128)(2,1)S(1)}, u32[]{:S(2)}, u32[]{:S(2)}) %collective-permute-start.68) | collective-permute-done | bytes 1048608 | tf_op jit(solution)/shard_map/ppermute | solution.py:75
  599.1 9.6 %grad_qkv.3 = (bf16[512,384]{1,0:T(8,128)(2,1)}, bf16[512,384]{1,0:T(8,128)(2,1)}, bf16[512,384]{1,0:T(8,128)(2,1)}, bf16[512,384]{1,0:T(8,128)(2,1)}) custom-call(s32[7]{0:T(128)} %pad_add_fusion.info, bf16[1024,2048]{1,0:T(8,128)(2,1)} %get-tuple-element.347.act_near, bf16[1024,2048]{1,0:T(8,128)(2,1)} %get-tuple-element.348.act_far, ...), custom_call_target="tpu_custom_call" | custom-call | flops 4214656000 | bytes 1 | tf_op jit(solution)/shard_map/grad_qkv/pallas_call | solution.py:37
  609.0 9.3 %back_product.2 = bf16[1024,2048]{1,0:T(8,128)(2,1)} custom-call(s32[7]{0:T(128)} %pad_add_fusion.info, bf16[2048,384]{1,0:T(8,128)(2,1)} %attend_back.2.near.far.first, bf16[2048,384]{1,0:T(8,128)(2,1)} %attend_back.3.near.far.second, bf16[2048,768]{1,0:T(8,128)(2,1)} %get-tuple-element.378.weight), custom_call_target="tpu_custom_call" | custom-call | flops 3611724800 | bytes 1 | tf_op jit(solution)/shard_map/back_product/pallas_call | solution.py:37
  623.2 10.2 %collective-permute-done.74 = bf16[512,384]{1,0:T(8,128)(2,1)S(1)} collective-permute-done((bf16[512,384]{1,0:T(8,128)(2,1)S(1)}, bf16[512,384]{1,0:T(8,128)(2,1)S(1)}, u32[]{:S(2)}, u32[]{:S(2)}) %collective-permute-start.74) | collective-permute-done | bytes 393248 | tf_op jit(solution)/shard_map/ppermute | solution.py:110
  634.7 9.2 %back_product.3 = bf16[1024,2048]{1,0:T(8,128)(2,1)} custom-call(s32[7]{0:T(128)} %pad_add_fusion.info, bf16[2048,384]{1,0:T(8,128)(2,1)} %attend_back.2.near.far.first, bf16[2048,384]{1,0:T(8,128)(2,1)} %attend_back.3.near.far.second, bf16[2048,768]{1,0:T(8,128)(2,1)} %get-tuple-element.378.weight), custom_call_target="tpu_custom_call" | custom-call | flops 3611724800 | bytes 1 | tf_op jit(solution)/shard_map/back_product/pallas_call | solution.py:37
  661.7 10.7 %collective-permute-done.84 = bf16[512,256]{1,0:T(8,128)(2,1)S(1)} collective-permute-done((bf16[512,256]{1,0:T(8,128)(2,1)S(1)}, bf16[512,256]{1,0:T(8,128)(2,1)S(1)}, u32[]{:S(2)}, u32[]{:S(2)}) %collective-permute-start.84) | collective-permute-done | bytes 262176 | tf_op jit(solution)/shard_map/ppermute | solution.py:110
  682.3 33.1 %collective-permute-done.85.refs_1_ = bf16[512,768]{1,0:T(8,128)(2,1)} collective-permute-done((bf16[512,768]{1,0:T(8,128)(2,1)S(1)}, bf16[512,768]{1,0:T(8,128)(2,1)}, u32[]{:S(2)}, u32[]{:S(2)}) %collective-permute-start.85) | collective-permute-done | bytes 786464 | tf_op jit(solution)/shard_map/ppermute | solution.py:75
  717.0 10.3 %collective-permute-done.86.refs_3_ = bf16[512,640]{1,0:T(8,128)(2,1)S(1)} collective-permute-done((bf16[512,640]{1,0:T(8,128)(2,1)S(1)}, bf16[512,640]{1,0:T(8,128)(2,1)S(1)}, u32[]{:S(2)}, u32[]{:S(2)}) %collective-permute-start.86) | collective-permute-done | bytes 655392 | tf_op jit(solution)/shard_map/ppermute | solution.py:75
  729.1 11.0 %finish_pair.1 = (f32[128,5504]{1,0:T(8,128)}, f32[128,5504]{1,0:T(8,128)}, f32[128,1]{1,0:T(8,128)}) custom-call(s32[7]{0:T(128)} %pad_add_fusion.info, bf16[512,768]{1,0:T(8,128)(2,1)} %join.15.refs_0_, bf16[512,768]{1,0:T(8,128)(2,1)} %collective-permute-done.85.refs_1_, bf16[512,640]{1,0:T(8,128)(2,1)} %join.16.refs_2_, bf16[512,640]{1,0:T(8,128)(2,1)} %copy-done.68, ...), custom_call_target="tpu_custom_call" | custom-call | flops 3807912960 | bytes 1 | tf_op jit(solution)/shard_map/finish_pair/pallas_call | solution.py:37
  759.9 29.5 %collective-permute-done.92.refs_3_ = bf16[128,384]{1,0:T(8,128)(2,1)S(1)} collective-permute-done((bf16[128,384]{1,0:T(8,128)(2,1)}, bf16[128,384]{1,0:T(8,128)(2,1)S(1)}, u32[]{:S(2)}, u32[]{:S(2)}) %collective-permute-start.92) | collective-permute-done | bytes 98336 | tf_op jit(solution)/shard_map/ppermute | solution.py:75
  (520 shorter events, 381.7 us)
Async XLA Ops:
  32.7 42.4 %collective-permute-start.11 = (bf16[256,2048]{1,0:T(8,128)(2,1)}, bf16[256,2048]{1,0:T(8,128)(2,1)}, u32[]{:S(2)}, u32[]{:S(2)}) collective-permute-start(bf16[256,2048]{1,0:T(8,128)(2,1)} %bitcast.16.refs_0_.refs_5_), channel_id=1, source_target_pairs={{0,16},{16,0},{1,17},{17,1},{2,18},{18,2},{3,19},{19,3},{4,20},{20... | collective-permute-start | bytes 3145736 | tf_op jit(solution)/shard_map/ppermute | solution.py:75
  107.8 32.2 %collective-permute-start.16 = (bf16[1024,2048]{1,0:T(8,128)(2,1)}, bf16[1024,2048]{1,0:T(8,128)(2,1)}, u32[]{:S(2)}, u32[]{:S(2)}) collective-permute-start(bf16[1024,2048]{1,0:T(8,128)(2,1)} %join.11.near), channel_id=1, source_target_pairs={{0,1},{1,0},{2,3},{3,2},{4,5},{5,4},{6,7},{7,6},{8,9},{9,8},{10,11... | collective-permute-start | bytes 12582920 | tf_op jit(solution)/shard_map/ppermute | solution.py:75
  132.2 34.9 %collective-permute-start.23 = (bf16[512,768]{1,0:T(8,128)(2,1)S(1)}, bf16[512,768]{1,0:T(8,128)(2,1)S(1)}, u32[]{:S(2)}, u32[]{:S(2)}) collective-permute-start(bf16[512,768]{1,0:T(8,128)(2,1)S(1)} %copy-done.54), channel_id=1, source_target_pairs={{0,4},{4,12},{12,8},{8,0},{1,5},{5,13},{13,9},{9,1},{2,6},{6,14},{... | collective-permute-start | bytes 2359304 | tf_op jit(solution)/shard_map/ppermute | solution.py:110
  137.6 29.4 %collective-permute-start.22 = (bf16[176,2048]{1,0:T(8,128)(2,1)S(1)}, bf16[176,2048]{1,0:T(8,128)(2,1)S(1)}, u32[]{:S(2)}, u32[]{:S(2)}) collective-permute-start(bf16[176,2048]{1,0:T(8,128)(2,1)S(1)} %copy-done.61), channel_id=1, source_target_pairs={{0,4},{4,12},{12,8},{8,0},{1,5},{5,13},{13,9},{9,1},{2,6},{6,14},{... | collective-permute-start | bytes 2162696 | tf_op jit(solution)/shard_map/ppermute | solution.py:110
  172.8 33.7 %collective-permute-start.30 = (bf16[256,2048]{1,0:T(8,128)(2,1)}, bf16[256,2048]{1,0:T(8,128)(2,1)S(1)}, u32[]{:S(2)}, u32[]{:S(2)}) collective-permute-start(bf16[256,2048]{1,0:T(8,128)(2,1)} %bitcast.19.refs_0_.refs_4_), channel_id=1, source_target_pairs={{0,16},{16,0},{1,17},{17,1},{2,18},{18,2},{3,19},{19,3},{4,20},{20... | collective-permute-start | bytes 3145736 | tf_op jit(solution)/shard_map/ppermute | solution.py:75
  173.6 33.5 %collective-permute-start.31 = (bf16[256,2048]{1,0:T(8,128)(2,1)}, bf16[256,2048]{1,0:T(8,128)(2,1)S(1)}, u32[]{:S(2)}, u32[]{:S(2)}) collective-permute-start(bf16[256,2048]{1,0:T(8,128)(2,1)} %bitcast.19.refs_0_.refs_4_), channel_id=1, source_target_pairs={{0,2},{2,0},{1,3},{3,1},{4,6},{6,4},{5,7},{7,5},{8,10},{10,8},{9,1... | collective-permute-start | bytes 3145736 | tf_op jit(solution)/shard_map/ppermute | solution.py:75
  236.5 30.1 %collective-permute-start.36 = (bf16[1024,2048]{1,0:T(8,128)(2,1)}, bf16[1024,2048]{1,0:T(8,128)(2,1)S(1)}, u32[]{:S(2)}, u32[]{:S(2)}) collective-permute-start(bf16[1024,2048]{1,0:T(8,128)(2,1)} %join.13.near.refs_0_), channel_id=1, source_target_pairs={{0,1},{1,0},{2,3},{3,2},{4,5},{5,4},{6,7},{7,6},{8,9},{9,8},{10,11... | collective-permute-start | bytes 12582920 | tf_op jit(solution)/shard_map/ppermute | solution.py:75
  239.6 46.9 %collective-permute-start.41 = (bf16[512,640]{1,0:T(8,128)(2,1)S(1)}, bf16[512,640]{1,0:T(8,128)(2,1)}, u32[]{:S(2)}, u32[]{:S(2)}) collective-permute-start(bf16[512,640]{1,0:T(8,128)(2,1)S(1)} %copy-done.65), channel_id=1, source_target_pairs={{0,4},{4,12},{12,8},{8,0},{1,5},{5,13},{13,9},{9,1},{2,6},{6,14},{... | collective-permute-start | bytes 1966088 | tf_op jit(solution)/shard_map/ppermute | solution.py:110
  309.7 32.1 %collective-permute-start.44 = (bf16[512,640]{1,0:T(8,128)(2,1)S(1)}, bf16[512,640]{1,0:T(8,128)(2,1)S(1)}, u32[]{:S(2)}, u32[]{:S(2)}) collective-permute-start(bf16[512,640]{1,0:T(8,128)(2,1)S(1)} %collective-permute-done.43.refs_2_), channel_id=1, source_target_pairs={{0,4},{4,12},{12,8},{8,0},{1,5},{5,13},{13,9},{9,1},{2,6},{6,14},{... | collective-permute-start | bytes 1966088 | tf_op jit(solution)/shard_map/ppermute | solution.py:110
  394.2 39.0 %collective-permute-start.48 = (bf16[256,2048]{1,0:T(8,128)(2,1)}, bf16[256,2048]{1,0:T(8,128)(2,1)S(1)}, u32[]{:S(2)}, u32[]{:S(2)}) collective-permute-start(bf16[256,2048]{1,0:T(8,128)(2,1)} %get-tuple-element.310), channel_id=1, source_target_pairs={{0,16},{16,0},{1,17},{17,1},{2,18},{18,2},{3,19},{19,3},{4,20},{20... | collective-permute-start | bytes 3145736 | tf_op jit(solution)/shard_map/ppermute | solution.py:75
  395.4 37.8 %collective-permute-start.49 = (bf16[256,2048]{1,0:T(8,128)(2,1)}, bf16[256,2048]{1,0:T(8,128)(2,1)S(1)}, u32[]{:S(2)}, u32[]{:S(2)}) collective-permute-start(bf16[256,2048]{1,0:T(8,128)(2,1)} %get-tuple-element.311), channel_id=1, source_target_pairs={{0,2},{2,0},{1,3},{3,1},{4,6},{6,4},{5,7},{7,5},{8,10},{10,8},{9,1... | collective-permute-start | bytes 3145736 | tf_op jit(solution)/shard_map/ppermute | solution.py:75
  396.9 45.6 %collective-permute-start.50 = (bf16[256,2048]{1,0:T(8,128)(2,1)}, bf16[256,2048]{1,0:T(8,128)(2,1)S(1)}, u32[]{:S(2)}, u32[]{:S(2)}) collective-permute-start(bf16[256,2048]{1,0:T(8,128)(2,1)} %get-tuple-element.312), channel_id=1, source_target_pairs={{0,18},{2,16},{16,2},{18,0},{1,19},{3,17},{17,3},{19,1},{4,22},{6,... | collective-permute-start | bytes 3145736 | tf_op jit(solution)/shard_map/ppermute | solution.py:75
  410.3 47.4 %collective-permute-start.51 = (bf16[512,768]{1,0:T(8,128)(2,1)S(1)}, bf16[512,768]{1,0:T(8,128)(2,1)S(1)}, u32[]{:S(2)}, u32[]{:S(2)}) collective-permute-start(bf16[512,768]{1,0:T(8,128)(2,1)S(1)} %add_convert_fusion.2), channel_id=1, source_target_pairs={{0,4},{4,12},{12,8},{8,0},{1,5},{5,13},{13,9},{9,1},{2,6},{6,14},{... | collective-permute-start | bytes 2359304 | tf_op jit(solution)/shard_map/ppermute | solution.py:110
  411.6 54.8 %collective-permute-start.52 = (bf16[512,640]{1,0:T(8,128)(2,1)S(1)}, bf16[512,640]{1,0:T(8,128)(2,1)S(1)}, u32[]{:S(2)}, u32[]{:S(2)}) collective-permute-start(bf16[512,640]{1,0:T(8,128)(2,1)S(1)} %copy-done.67), channel_id=1, source_target_pairs={{0,4},{4,12},{12,8},{8,0},{1,5},{5,13},{13,9},{9,1},{2,6},{6,14},{... | collective-permute-start | bytes 1966088 | tf_op jit(solution)/shard_map/ppermute | solution.py:110
  470.8 44.7 %collective-permute-start.61 = (bf16[4,2048,256]{2,1,0:T(8,128)(2,1)S(1)}, bf16[4,2048,256]{2,1,0:T(8,128)(2,1)}, u32[]{:S(2)}, u32[]{:S(2)}) collective-permute-start(bf16[4,2048,256]{2,1,0:T(8,128)(2,1)S(1)} %copy-done.41), channel_id=1, source_target_pairs={{0,1},{1,0},{2,3},{3,2},{4,5},{5,4},{6,7},{7,6},{8,9},{9,8},{10,11... | collective-permute-start | bytes 12582920 | tf_op jit(solution)/shard_map/ppermute | solution.py:75
  473.5 38.9 %collective-permute-start.60 = (bf16[512,640]{1,0:T(8,128)(2,1)S(1)}, bf16[512,640]{1,0:T(8,128)(2,1)S(1)}, u32[]{:S(2)}, u32[]{:S(2)}) collective-permute-start(bf16[512,640]{1,0:T(8,128)(2,1)S(1)} %add_convert_fusion.9), channel_id=1, source_target_pairs={{0,4},{4,12},{12,8},{8,0},{1,5},{5,13},{13,9},{9,1},{2,6},{6,14},{... | collective-permute-start | bytes 1966088 | tf_op jit(solution)/shard_map/ppermute | solution.py:110
  532.2 36.4 %collective-permute-start.65 = (bf16[1024,2048]{1,0:T(8,128)(2,1)}, bf16[1024,2048]{1,0:T(8,128)(2,1)}, u32[]{:S(2)}, u32[]{:S(2)}) collective-permute-start(bf16[1024,2048]{1,0:T(8,128)(2,1)} %down_product.3), channel_id=1, source_target_pairs={{0,1},{1,0},{2,3},{3,2},{4,5},{5,4},{6,7},{7,6},{8,9},{9,8},{10,11... | collective-permute-start | bytes 12582920 | tf_op jit(solution)/shard_map/ppermute | solution.py:75
  533.7 32.5 %collective-permute-start.64 = (bf16[176,2048]{1,0:T(8,128)(2,1)S(1)}, bf16[176,2048]{1,0:T(8,128)(2,1)S(1)}, u32[]{:S(2)}, u32[]{:S(2)}) collective-permute-start(bf16[176,2048]{1,0:T(8,128)(2,1)S(1)} %add_convert_fusion.6), channel_id=1, source_target_pairs={{0,4},{4,12},{12,8},{8,0},{1,5},{5,13},{13,9},{9,1},{2,6},{6,14},{... | collective-permute-start | bytes 2162696 | tf_op jit(solution)/shard_map/ppermute | solution.py:110
  566.2 32.9 %collective-permute-start.68 = (bf16[2048,256]{1,0:T(8,128)(2,1)}, bf16[2048,256]{1,0:T(8,128)(2,1)S(1)}, u32[]{:S(2)}, u32[]{:S(2)}) collective-permute-start(bf16[2048,256]{1,0:T(8,128)(2,1)} %get-tuple-element.365), channel_id=1, source_target_pairs={{0,18},{2,16},{16,2},{18,0},{1,19},{3,17},{17,3},{19,1},{4,22},{6,... | collective-permute-start | bytes 3145736 | tf_op jit(solution)/shard_map/ppermute | solution.py:75
  568.6 40.1 %collective-permute-start.73 = (bf16[176,2048]{1,0:T(8,128)(2,1)S(1)}, bf16[176,2048]{1,0:T(8,128)(2,1)S(1)}, u32[]{:S(2)}, u32[]{:S(2)}) collective-permute-start(bf16[176,2048]{1,0:T(8,128)(2,1)S(1)} %add_convert_fusion.5), channel_id=1, source_target_pairs={{0,4},{4,12},{12,8},{8,0},{1,5},{5,13},{13,9},{9,1},{2,6},{6,14},{... | collective-permute-start | bytes 2162696 | tf_op jit(solution)/shard_map/ppermute | solution.py:110
  618.2 40.2 %collective-permute-start.79 = (bf16[1024,2048]{1,0:T(8,128)(2,1)}, bf16[1024,2048]{1,0:T(8,128)(2,1)}, u32[]{:S(2)}, u32[]{:S(2)}) collective-permute-start(bf16[1024,2048]{1,0:T(8,128)(2,1)} %back_product.2), channel_id=1, source_target_pairs={{0,1},{1,0},{2,3},{3,2},{4,5},{5,4},{6,7},{7,6},{8,9},{9,8},{10,11... | collective-permute-start | bytes 12582920 | tf_op jit(solution)/shard_map/ppermute | solution.py:75
  620.8 29.9 %collective-permute-start.77 = (bf16[128,640]{1,0:T(8,128)(2,1)S(1)}, bf16[128,640]{1,0:T(8,128)(2,1)S(1)}, u32[]{:S(2)}, u32[]{:S(2)}) collective-permute-start(bf16[128,640]{1,0:T(8,128)(2,1)S(1)} %get-tuple-element.436), channel_id=1, source_target_pairs={{0,3},{1,2},{2,1},{3,0},{4,7},{5,6},{6,5},{7,4},{8,11},{9,10},{10,... | collective-permute-start | bytes 491528 | tf_op jit(solution)/shard_map/ppermute | solution.py:75
  649.8 77.5 %collective-permute-start.69 = (bf16[256,2048]{1,0:T(8,128)(2,1)}, bf16[256,2048]{1,0:T(8,128)(2,1)S(1)}, u32[]{:S(2)}, u32[]{:S(2)}) collective-permute-start(bf16[256,2048]{1,0:T(8,128)(2,1)} %get-tuple-element.366), channel_id=1, source_target_pairs={{0,16},{16,0},{1,17},{17,1},{2,18},{18,2},{3,19},{19,3},{4,20},{20... | collective-permute-start | bytes 3145736 | tf_op jit(solution)/shard_map/ppermute | solution.py:75
  650.7 76.7 %collective-permute-start.70 = (bf16[256,2048]{1,0:T(8,128)(2,1)}, bf16[256,2048]{1,0:T(8,128)(2,1)S(1)}, u32[]{:S(2)}, u32[]{:S(2)}) collective-permute-start(bf16[256,2048]{1,0:T(8,128)(2,1)} %get-tuple-element.367), channel_id=1, source_target_pairs={{0,2},{2,0},{1,3},{3,1},{4,6},{6,4},{5,7},{7,5},{8,10},{10,8},{9,1... | collective-permute-start | bytes 3145736 | tf_op jit(solution)/shard_map/ppermute | solution.py:75
  655.1 72.3 %collective-permute-start.71 = (bf16[256,2048]{1,0:T(8,128)(2,1)S(1)}, bf16[256,2048]{1,0:T(8,128)(2,1)}, u32[]{:S(2)}, u32[]{:S(2)}) collective-permute-start(bf16[256,2048]{1,0:T(8,128)(2,1)S(1)} %copy-done.45), channel_id=1, source_target_pairs={{0,18},{2,16},{16,2},{18,0},{1,19},{3,17},{17,3},{19,1},{4,22},{6,... | collective-permute-start | bytes 3145736 | tf_op jit(solution)/shard_map/ppermute | solution.py:75
  672.4 42.9 %collective-permute-start.85 = (bf16[512,768]{1,0:T(8,128)(2,1)S(1)}, bf16[512,768]{1,0:T(8,128)(2,1)}, u32[]{:S(2)}, u32[]{:S(2)}) collective-permute-start(bf16[512,768]{1,0:T(8,128)(2,1)S(1)} %copy-done.53), channel_id=1, source_target_pairs={{0,16},{16,0},{1,17},{17,1},{2,18},{18,2},{3,19},{19,3},{4,20},{20... | collective-permute-start | bytes 2359304 | tf_op jit(solution)/shard_map/ppermute | solution.py:75
  673.6 53.7 %collective-permute-start.86 = (bf16[512,640]{1,0:T(8,128)(2,1)S(1)}, bf16[512,640]{1,0:T(8,128)(2,1)S(1)}, u32[]{:S(2)}, u32[]{:S(2)}) collective-permute-start(bf16[512,640]{1,0:T(8,128)(2,1)S(1)} %copy-done.66), channel_id=1, source_target_pairs={{0,16},{16,0},{1,17},{17,1},{2,18},{18,2},{3,19},{19,3},{4,20},{20... | collective-permute-start | bytes 1966088 | tf_op jit(solution)/shard_map/ppermute | solution.py:75
  742.3 48.4 %collective-permute-start.80 = (bf16[256,2048]{1,0:T(8,128)(2,1)}, bf16[256,2048]{1,0:T(8,128)(2,1)S(1)}, u32[]{:S(2)}, u32[]{:S(2)}) collective-permute-start(bf16[256,2048]{1,0:T(8,128)(2,1)} %get-tuple-element.392), channel_id=1, source_target_pairs={{0,16},{16,0},{1,17},{17,1},{2,18},{18,2},{3,19},{19,3},{4,20},{20... | collective-permute-start | bytes 3145736 | tf_op jit(solution)/shard_map/ppermute | solution.py:75
  743.1 48.3 %collective-permute-start.81 = (bf16[256,2048]{1,0:T(8,128)(2,1)}, bf16[256,2048]{1,0:T(8,128)(2,1)S(1)}, u32[]{:S(2)}, u32[]{:S(2)}) collective-permute-start(bf16[256,2048]{1,0:T(8,128)(2,1)} %get-tuple-element.393), channel_id=1, source_target_pairs={{0,2},{2,0},{1,3},{3,1},{4,6},{6,4},{5,7},{7,5},{8,10},{10,8},{9,1... | collective-permute-start | bytes 3145736 | tf_op jit(solution)/shard_map/ppermute | solution.py:75
  743.6 48.7 %collective-permute-start.82 = (bf16[256,2048]{1,0:T(8,128)(2,1)}, bf16[256,2048]{1,0:T(8,128)(2,1)S(1)}, u32[]{:S(2)}, u32[]{:S(2)}) collective-permute-start(bf16[256,2048]{1,0:T(8,128)(2,1)} %get-tuple-element.394), channel_id=1, source_target_pairs={{0,18},{2,16},{16,2},{18,0},{1,19},{3,17},{17,3},{19,1},{4,22},{6,... | collective-permute-start | bytes 3145736 | tf_op jit(solution)/shard_map/ppermute | solution.py:75
  757.2 38.9 %collective-permute-start.93 = (bf16[512,384]{1,0:T(8,128)(2,1)S(1)}, bf16[512,384]{1,0:T(8,128)(2,1)S(1)}, u32[]{:S(2)}, u32[]{:S(2)}) collective-permute-start(bf16[512,384]{1,0:T(8,128)(2,1)S(1)} %add_convert_fusion.11), channel_id=1, source_target_pairs={{0,4},{4,12},{12,8},{8,0},{1,5},{5,13},{13,9},{9,1},{2,6},{6,14},{... | collective-permute-start | bytes 1179656 | tf_op jit(solution)/shard_map/ppermute | solution.py:110
  759.9 29.6 %collective-permute-start.92 = (bf16[128,384]{1,0:T(8,128)(2,1)}, bf16[128,384]{1,0:T(8,128)(2,1)S(1)}, u32[]{:S(2)}, u32[]{:S(2)}) collective-permute-start(bf16[128,384]{1,0:T(8,128)(2,1)} %get-tuple-element.442), channel_id=1, source_target_pairs={{0,3},{1,2},{2,1},{3,0},{4,7},{5,6},{6,5},{7,4},{8,11},{9,10},{10,... | collective-permute-start | bytes 294920 | tf_op jit(solution)/shard_map/ppermute | solution.py:75
  (179 other events, 2323.6 us)

commit v4 on v3

--- a/solution.py
+++ b/solution.py
@@ -1169,7 +1169,6 @@
     grads_second = do(attend_back, info, qkv, attn_grads, lse, cosine, sine, 1)
     pair_b.move()
     second_pieces = owners(after(pair_b.total, *out_parts))
-    down_sum.move()
     need(block_moved)
     block_terms = do(combine, info, block_near, block_moved)
     qkv_first.move()
@@ -1188,16 +1187,17 @@
     in_far = do(back_product, info, grads_first, grads_second, full_qkv, True)
     in_moved = hop(in_far, 4)
     qkv_first.move()
-    down_mine = down_sum.total[:half_down]
-    down_theirs = hop(down_mine, 1)
     in_near = do(back_product, info, grads_first, grads_second, full_qkv, False)
     out_sum = Sum(order, lane_c, do(order_out, info, out_own, out_parts, planes))
     sums_second = rows_of(pair_b.total, second_pieces)
+    down_sum.move()
     qkv_second.move()
     need(in_moved)
     in_own, in_parts = scatter_moves(*do(combine, info, in_near, in_moved))
     qkv_first.move()
     out_sum.move()
+    down_mine = down_sum.total[:half_down]
+    down_theirs = hop(down_mine, 1)
     need(*sums_first, *sums_second, *block_parts)
     sum_gate, sum_up, gain_sum_ffn = do(
         finish_pair, info, sums_first, sums_second, weight_gate, weight_up, wide_ffn,

time: 840 us -> 836 us (level)
    unnamed x219 -> x215, local copies, waits for them, and re-layouts: 20.1 us -> 20 us
  transfers between devices with their start and end apart: 104 -> 104, of which waited for: 38 -> 36; matrix products, arithmetic and copies ran while one was open for 5% -> 5% of each run, Pallas kernels for 36% -> 36%
where the time goes in v4:
time: 836 us; the launch traced here: 825 us
  Pallas kernels  367 us (44%)
  waiting for transfers between devices  290 us (35%)
  starting transfers between devices  107 us (13%)
  local copies, waits for them, and re-layouts  31.4 us (4%)
  other arithmetic  27.2 us (3%)
    pallas_call x48, Pallas kernels, call(): pl.pallas_call(kernel, grid_spec=pltpu.PrefetchScalarGridSpec(num_scalar_...  367 us
    ppermute x71, waiting for transfers between devices, hop(): return lax.ppermute(block, axes, [(i, last - i) for i in range(last + 1)])  158 us
    ppermute x33, waiting for transfers between devices, hop(): moved = lax.ppermute(block, 'z', self.route)  132 us
    ppermute x71, starting transfers between devices, hop(): return lax.ppermute(block, axes, [(i, last - i) for i in range(last + 1)])  63.4 us
    ppermute x33, starting transfers between devices, hop(): moved = lax.ppermute(block, 'z', self.route)  43.8 us
    unnamed x215, local copies, waits for them, and re-layouts  20 us
  transfers between devices with their start and end apart: 104, of which 36 were waited for; matrix products, arithmetic and copies ran while one was open for 5% of the time, Pallas kernels for 36%

profile of v4, /device:TPU:0, one launch (start us, length us, event | category | flops | bytes accessed | tf_op | source)
XLA Modules:
  0.0 825.4 jit_solution(6244453087425244066)
XLA Ops:
  57.0 17.7 %collective-permute-done.7.refs_1_ = bf16[512,768]{1,0:T(8,128)(2,1)} collective-permute-done((bf16[512,768]{1,0:T(8,128)(2,1)}, bf16[512,768]{1,0:T(8,128)(2,1)}, u32[]{:S(2)}, u32[]{:S(2)}) %collective-permute-start.7) | collective-permute-done | bytes 786464 | tf_op jit(solution)/shard_map/ppermute | solution.py:110
  117.5 14.6 %collective-permute-done.17.refs_3_ = bf16[512,768]{1,0:T(8,128)(2,1)S(1)} collective-permute-done((bf16[512,768]{1,0:T(8,128)(2,1)}, bf16[512,768]{1,0:T(8,128)(2,1)S(1)}, u32[]{:S(2)}, u32[]{:S(2)}) %collective-permute-start.17) | collective-permute-done | bytes 786464 | tf_op jit(solution)/shard_map/ppermute | solution.py:110
  140.1 15.7 %project.1 = (bf16[2048,768]{1,0:T(8,128)(2,1)}, bf16[2,1024,768]{2,1,0:T(8,128)(2,1)}, bf16[1024,2048]{1,0:T(8,128)(2,1)}, bf16[1024,2048]{1,0:T(8,128)(2,1)}) custom-call(s32[7]{0:T(128)} %pad_add_fusion.info, bf16[1024,2048]{1,0:T(8,128)(2,1)} %join.11.near, bf16[1024,2048]{1,0:T(8,128)(2,1)} %collective-permute-done.16.far, ...), custom_call_target="tpu_custom_call" | custom-call | flops 8194001920 | bytes 1 | tf_op jit(solution)/shard_map/project/pallas_call | solution.py:37
  155.8 11.2 %collective-permute-done.22.refs_2_ = bf16[176,2048]{1,0:T(8,128)(2,1)S(1)} collective-permute-done((bf16[176,2048]{1,0:T(8,128)(2,1)S(1)}, bf16[176,2048]{1,0:T(8,128)(2,1)S(1)}, u32[]{:S(2)}, u32[]{:S(2)}) %collective-permute-start.22) | collective-permute-done | bytes 720928 | tf_op jit(solution)/shard_map/ppermute | solution.py:110
  174.1 13.7 %attend.1 = (bf16[1024,256]{1,0:T(8,128)(2,1)}, bf16[1024,256]{1,0:T(8,128)(2,1)}, f32[2,2048,1]{2,1,0:T(8,128)}) custom-call(s32[7]{0:T(128)} %pad_add_fusion.info, bf16[2048,768]{1,0:T(8,128)(2,1)} %bitcast.74), custom_call_target="tpu_custom_call" | custom-call | flops 2168458240 | bytes 1 | tf_op jit(solution)/shard_map/attend/pallas_call | solution.py:37
  189.8 8.6 %spread.1.refs_4_.refs_7_ = bf16[2048,2048]{1,0:T(8,128)(2,1)} custom-call(s32[7]{0:T(128)} %pad_add_fusion.info, bf16[8192,256]{1,0:T(8,128)(2,1)} %join.12.refs_0_, bf16[8192,256]{1,0:T(8,128)(2,1)} %copy-done.45), custom_call_target="tpu_custom_call" | custom-call | flops 5058759680 | bytes 1 | tf_op jit(solution)/shard_map/spread/pallas_call | solution.py:37
  220.7 9.2 %branch.1 = (bf16[256,2048]{1,0:T(8,128)(2,1)}, f32[256,2048]{1,0:T(8,128)}, f32[256,1]{1,0:T(8,128)}, bf16[256,2048]{1,0:T(8,128)(2,1)}) custom-call(s32[7]{0:T(128)} %pad_add_fusion.info, bf16[512,256]{1,0:T(8,128)(2,1)} %get-tuple-element.252.refs_0_, bf16[512,256]{1,0:T(8,128)(2,1)} %copy-done.84, bf16[512,256]{1,0:T(8,128)(2,1)} %copy-done.85, ...), custom_call_target="tpu_custom_call" | custom-call | flops 4576650240 | bytes 1 | tf_op jit(solution)/shard_map/branch/pallas_call | solution.py:37
  242.1 18.6 %collective-permute-done.35.refs_3_ = bf16[512,768]{1,0:T(8,128)(2,1)} collective-permute-done((bf16[512,768]{1,0:T(8,128)(2,1)S(1)}, bf16[512,768]{1,0:T(8,128)(2,1)}, u32[]{:S(2)}, u32[]{:S(2)}) %collective-permute-start.35) | collective-permute-done | bytes 786464 | tf_op jit(solution)/shard_map/ppermute | solution.py:110
  268.5 13.5 %slopes.1 = (f32[1024,768]{1,0:T(8,128)}, f32[1024,768]{1,0:T(8,128)}) custom-call(s32[7]{0:T(128)} %pad_add_fusion.info, bf16[1024,2048]{1,0:T(8,128)(2,1)} %join.13.near.refs_0_, bf16[1024,2048]{1,0:T(8,128)(2,1)} %copy-done.41, bf16[384,2048]{1,0:T(8,128)(2,1)} %get-tuple-element.266.first.b, bf16[384,2048]{1,0:T(8,128)(2,1)} %get-tuple-element.268.second.d), custom_call_target="tpu_custom_call" | custom-call | flops 5299932160 | bytes 1 | tf_op jit(solution)/shard_map/slopes/pallas_call | solution.py:37
  291.4 18.2 %collective-permute-done.43.refs_2_ = bf16[512,640]{1,0:T(8,128)(2,1)S(1)} collective-permute-done((bf16[512,640]{1,0:T(8,128)(2,1)}, bf16[512,640]{1,0:T(8,128)(2,1)S(1)}, u32[]{:S(2)}, u32[]{:S(2)}) %collective-permute-start.43) | collective-permute-done | bytes 655392 | tf_op jit(solution)/shard_map/ppermute | solution.py:110
  309.6 8.7 %ffn.4 = (bf16[1024,384]{1,0:T(8,128)(2,1)}, bf16[1024,768]{1,0:T(8,128)(2,1)}) custom-call(s32[7]{0:T(128)} %pad_add_fusion.info, bf16[1024,2048]{1,0:T(8,128)(2,1)} %join.14.refs_0_.act_near, f32[1024,768]{1,0:T(8,128)} %get-tuple-element.269.refs_1_, bf16[2048,768]{1,0:T(8,128)(2,1)} %assemble.2.refs_2_.refs_4_), custom_call_target="tpu_custom_call" | custom-call | flops 4154362880 | bytes 1 | tf_op jit(solution)/shard_map/ffn/pallas_call | solution.py:37
  320.3 8.7 %ffn.5 = (bf16[1024,384]{1,0:T(8,128)(2,1)}, bf16[1024,768]{1,0:T(8,128)(2,1)}) custom-call(s32[7]{0:T(128)} %pad_add_fusion.info, bf16[1024,2048]{1,0:T(8,128)(2,1)} %copy-done.43, f32[1024,768]{1,0:T(8,128)} %get-tuple-element.281.refs_1_, bf16[2048,768]{1,0:T(8,128)(2,1)} %assemble.2.refs_2_.refs_4_), custom_call_target="tpu_custom_call" | custom-call | flops 4154362880 | bytes 1 | tf_op jit(solution)/shard_map/ffn/pallas_call | solution.py:37
  328.9 12.7 %grad_pair.2 = (bf16[512,768]{1,0:T(8,128)(2,1)}, bf16[512,768]{1,0:T(8,128)(2,1)}, bf16[512,768]{1,0:T(8,128)(2,1)}, bf16[512,768]{1,0:T(8,128)(2,1)}) custom-call(s32[7]{0:T(128)} %pad_add_fusion.info, bf16[1024,2048]{1,0:T(8,128)(2,1)} %join.14.refs_0_.act_near, bf16[1024,2048]{1,0:T(8,128)(2,1)} %copy-done.43, ...), custom_call_target="tpu_custom_call" | custom-call | flops 4576414720 | bytes 1 | tf_op jit(solution)/shard_map/grad_pair/pallas_call | solution.py:37
  346.5 15.8 %ffn.6 = (bf16[1024,384]{1,0:T(8,128)(2,1)}, bf16[1024,640]{1,0:T(8,128)(2,1)}, bf16[1024,2048]{1,0:T(8,128)(2,1)}) custom-call(s32[7]{0:T(128)} %pad_add_fusion.info, bf16[1024,2048]{1,0:T(8,128)(2,1)} %copy-done.43, f32[1024,768]{1,0:T(8,128)} %get-tuple-element.281.refs_1_, bf16[2048,640]{1,0:T(8,128)(2,1)} %assemble.3.refs_2_, ...), custom_call_target="tpu_custom_call" | custom-call | flops 6023449600 | bytes 1 | tf_op jit(solution)/shard_map/ffn/pallas_call | solution.py:37
  365.0 15.8 %ffn.7 = (bf16[1024,384]{1,0:T(8,128)(2,1)}, bf16[1024,640]{1,0:T(8,128)(2,1)}, bf16[1024,2048]{1,0:T(8,128)(2,1)}) custom-call(s32[7]{0:T(128)} %pad_add_fusion.info, bf16[1024,2048]{1,0:T(8,128)(2,1)} %join.14.refs_0_.act_near, f32[1024,768]{1,0:T(8,128)} %get-tuple-element.269.refs_1_, bf16[2048,640]{1,0:T(8,128)(2,1)} %assemble.3.refs_2_, ...), custom_call_target="tpu_custom_call" | custom-call | flops 6023449600 | bytes 1 | tf_op jit(solution)/shard_map/ffn/pallas_call | solution.py:37
  397.5 12.5 %grad_pair.3 = (bf16[512,640]{1,0:T(8,128)(2,1)}, bf16[512,640]{1,0:T(8,128)(2,1)}, bf16[512,640]{1,0:T(8,128)(2,1)}, bf16[512,640]{1,0:T(8,128)(2,1)}) custom-call(s32[7]{0:T(128)} %pad_add_fusion.info, bf16[1024,2048]{1,0:T(8,128)(2,1)} %join.14.refs_0_.act_near, bf16[1024,2048]{1,0:T(8,128)(2,1)} %copy-done.43, ...), custom_call_target="tpu_custom_call" | custom-call | flops 4335242240 | bytes 1 | tf_op jit(solution)/shard_map/grad_pair/pallas_call | solution.py:37
  412.5 11.6 %grad_down.1 = (bf16[176,2048]{1,0:T(8,128)(2,1)}, bf16[176,2048]{1,0:T(8,128)(2,1)}, bf16[176,2048]{1,0:T(8,128)(2,1)}, bf16[176,2048]{1,0:T(8,128)(2,1)}) custom-call(s32[7]{0:T(128)} %pad_add_fusion.info, bf16[1024,384]{1,0:T(8,128)(2,1)} %get-tuple-element.278.first_near.a, bf16[1024,384]{1,0:T(8,128)(2,1)} %get-tuple-element.282.first_far.a, ...), custom_call_target="tpu_custom_call" | custom-call | flops 4516121600 | bytes 1 | tf_op jit(solution)/shard_map/grad_down/pallas_call | solution.py:37
  424.1 8.9 %down_product.2 = bf16[1024,2048]{1,0:T(8,128)(2,1)} custom-call(s32[7]{0:T(128)} %pad_add_fusion.info, bf16[1024,384]{1,0:T(8,128)(2,1)} %get-tuple-element.278.first_near.a, bf16[384,2048]{1,0:T(8,128)(2,1)} %get-tuple-element.266.first.b, bf16[1024,384]{1,0:T(8,128)(2,1)} %get-tuple-element.292.second_near.c, bf16[384,2048]{1,0:T(8,128)(2,1)} %get-tuple-element.268.second.d), custom_call_target="tpu_custom_call" | custom-call | flops 3249966080 | bytes 1 | tf_op jit(solution)/shard_map/down_product/pallas_call | solution.py:37
  433.0 9.3 %collective-permute-done.50.refs_3_ = bf16[256,2048]{1,0:T(8,128)(2,1)S(1)} collective-permute-done((bf16[256,2048]{1,0:T(8,128)(2,1)}, bf16[256,2048]{1,0:T(8,128)(2,1)S(1)}, u32[]{:S(2)}, u32[]{:S(2)}) %collective-permute-start.50) | collective-permute-done | bytes 1048608 | tf_op jit(solution)/shard_map/ppermute | solution.py:75
  443.3 14.2 %grad_attn.1 = (f32[256,2048]{1,0:T(8,128)}, bf16[256,2048]{1,0:T(8,128)(2,1)}, bf16[1024,256]{1,0:T(8,128)(2,1)}, bf16[1024,256]{1,0:T(8,128)(2,1)}) custom-call(s32[7]{0:T(128)} %pad_add_fusion.info, f32[256,2048]{1,0:T(8,128)} %get-tuple-element.299.refs_0_, bf16[256,2048]{1,0:T(8,128)(2,1)} %copy-done.51, bf16[256,2048]{1,0:T(8,128)(2,1)} %copy-done.52, ...), custom_call_target="tpu_custom_call" | custom-call | flops 6023685120 | bytes 1 | tf_op jit(solution)/shard_map/grad_attn/pallas_call | solution.py:37
  484.7 8.9 %down_product.3 = bf16[1024,2048]{1,0:T(8,128)(2,1)} custom-call(s32[7]{0:T(128)} %pad_add_fusion.info, bf16[1024,384]{1,0:T(8,128)(2,1)} %get-tuple-element.282.first_far.a, bf16[384,2048]{1,0:T(8,128)(2,1)} %get-tuple-element.266.first.b, bf16[1024,384]{1,0:T(8,128)(2,1)} %get-tuple-element.290.second_far.c, bf16[384,2048]{1,0:T(8,128)(2,1)} %get-tuple-element.268.second.d), custom_call_target="tpu_custom_call" | custom-call | flops 3249966080 | bytes 1 | tf_op jit(solution)/shard_map/down_product/pallas_call | solution.py:37
  498.2 14.0 %attend_back.2.near.far.first = bf16[2048,384]{1,0:T(8,128)(2,1)} custom-call(s32[7]{0:T(128)} %pad_add_fusion.info, bf16[2048,768]{1,0:T(8,128)(2,1)} %bitcast.75, bf16[512,256]{1,0:T(8,128)(2,1)} %get-tuple-element.328.refs_0_, bf16[512,256]{1,0:T(8,128)(2,1)} %copy-done.81, bf16[512,256]{1,0:T(8,128)(2,1)} %copy-done.82, bf16[512,256]{1,0:T(8,128)(2,1)} %copy-done.83, ...), custom_call_target="tpu_custom_call" | custom-call | flops 3012561920 | bytes 1 | tf_op jit(solution)/shard_map/attend_back/pallas_call | solution.py:37
  522.3 9.5 %grad_qkv.2 = (bf16[512,384]{1,0:T(8,128)(2,1)}, bf16[512,384]{1,0:T(8,128)(2,1)}, bf16[512,384]{1,0:T(8,128)(2,1)}, bf16[512,384]{1,0:T(8,128)(2,1)}) custom-call(s32[7]{0:T(128)} %pad_add_fusion.info, bf16[1024,2048]{1,0:T(8,128)(2,1)} %get-tuple-element.347.act_near, bf16[1024,2048]{1,0:T(8,128)(2,1)} %get-tuple-element.348.act_far, ...), custom_call_target="tpu_custom_call" | custom-call | flops 4214656000 | bytes 1 | tf_op jit(solution)/shard_map/grad_qkv/pallas_call | solution.py:37
  537.0 13.9 %attend_back.3.near.far.second = bf16[2048,384]{1,0:T(8,128)(2,1)} custom-call(s32[7]{0:T(128)} %pad_add_fusion.info, bf16[2048,768]{1,0:T(8,128)(2,1)} %bitcast.76, bf16[512,256]{1,0:T(8,128)(2,1)} %get-tuple-element.328.refs_0_, bf16[512,256]{1,0:T(8,128)(2,1)} %copy-done.81, bf16[512,256]{1,0:T(8,128)(2,1)} %copy-done.82, bf16[512,256]{1,0:T(8,128)(2,1)} %copy-done.83, ...), custom_call_target="tpu_custom_call" | custom-call | flops 3012561920 | bytes 1 | tf_op jit(solution)/shard_map/attend_back/pallas_call | solution.py:37
  560.6 17.1 %collective-permute-done.71 = bf16[512,384]{1,0:T(8,128)(2,1)S(1)} collective-permute-done((bf16[512,384]{1,0:T(8,128)(2,1)S(1)}, bf16[512,384]{1,0:T(8,128)(2,1)S(1)}, u32[]{:S(2)}, u32[]{:S(2)}) %collective-permute-start.71) | collective-permute-done | bytes 393248 | tf_op jit(solution)/shard_map/ppermute | solution.py:110
  582.7 9.5 %grad_qkv.3 = (bf16[512,384]{1,0:T(8,128)(2,1)}, bf16[512,384]{1,0:T(8,128)(2,1)}, bf16[512,384]{1,0:T(8,128)(2,1)}, bf16[512,384]{1,0:T(8,128)(2,1)}) custom-call(s32[7]{0:T(128)} %pad_add_fusion.info, bf16[1024,2048]{1,0:T(8,128)(2,1)} %get-tuple-element.347.act_near, bf16[1024,2048]{1,0:T(8,128)(2,1)} %get-tuple-element.348.act_far, ...), custom_call_target="tpu_custom_call" | custom-call | flops 4214656000 | bytes 1 | tf_op jit(solution)/shard_map/grad_qkv/pallas_call | solution.py:37
  592.5 9.2 %back_product.2 = bf16[1024,2048]{1,0:T(8,128)(2,1)} custom-call(s32[7]{0:T(128)} %pad_add_fusion.info, bf16[2048,384]{1,0:T(8,128)(2,1)} %attend_back.2.near.far.first, bf16[2048,384]{1,0:T(8,128)(2,1)} %attend_back.3.near.far.second, bf16[2048,768]{1,0:T(8,128)(2,1)} %get-tuple-element.375.weight), custom_call_target="tpu_custom_call" | custom-call | flops 3611724800 | bytes 1 | tf_op jit(solution)/shard_map/back_product/pallas_call | solution.py:37
  614.3 9.1 %back_product.3 = bf16[1024,2048]{1,0:T(8,128)(2,1)} custom-call(s32[7]{0:T(128)} %pad_add_fusion.info, bf16[2048,384]{1,0:T(8,128)(2,1)} %attend_back.2.near.far.first, bf16[2048,384]{1,0:T(8,128)(2,1)} %attend_back.3.near.far.second, bf16[2048,768]{1,0:T(8,128)(2,1)} %get-tuple-element.375.weight), custom_call_target="tpu_custom_call" | custom-call | flops 3611724800 | bytes 1 | tf_op jit(solution)/shard_map/back_product/pallas_call | solution.py:37
  636.6 40.6 %collective-permute-done.68 = bf16[256,2048]{1,0:T(8,128)(2,1)S(1)} collective-permute-done((bf16[256,2048]{1,0:T(8,128)(2,1)}, bf16[256,2048]{1,0:T(8,128)(2,1)S(1)}, u32[]{:S(2)}, u32[]{:S(2)}) %collective-permute-start.68) | collective-permute-done | bytes 1048608 | tf_op jit(solution)/shard_map/ppermute | solution.py:75
  691.7 17.8 %collective-permute-done.103 = bf16[172,2048]{1,0:T(8,128)(2,1)S(1)} collective-permute-done((bf16[172,2048]{1,0:T(8,128)(2,1)S(1)}, bf16[172,2048]{1,0:T(8,128)(2,1)S(1)}, u32[]{:S(2)}, u32[]{:S(2)}) %collective-permute-start.103) | collective-permute-done | bytes 704544 | tf_op jit(solution)/shard_map/ppermute | solution.py:75
  724.5 10.8 %finish_pair.1 = (f32[128,5504]{1,0:T(8,128)}, f32[128,5504]{1,0:T(8,128)}, f32[128,1]{1,0:T(8,128)}) custom-call(s32[7]{0:T(128)} %pad_add_fusion.info, bf16[512,768]{1,0:T(8,128)(2,1)} %join.15.refs_0_, bf16[512,768]{1,0:T(8,128)(2,1)} %copy-done.58, bf16[512,640]{1,0:T(8,128)(2,1)} %join.16.refs_2_, bf16[512,640]{1,0:T(8,128)(2,1)} %copy-done.69, ...), custom_call_target="tpu_custom_call" | custom-call | flops 3807912960 | bytes 1 | tf_op jit(solution)/shard_map/finish_pair/pallas_call | solution.py:37
  752.9 32.6 %collective-permute-done.92.refs_3_ = bf16[128,384]{1,0:T(8,128)(2,1)S(1)} collective-permute-done((bf16[128,384]{1,0:T(8,128)(2,1)}, bf16[128,384]{1,0:T(8,128)(2,1)S(1)}, u32[]{:S(2)}, u32[]{:S(2)}) %collective-permute-start.92) | collective-permute-done | bytes 98336 | tf_op jit(solution)/shard_map/ppermute | solution.py:75
  (516 shorter events, 370.7 us)
Async XLA Ops:
  32.7 42.4 %collective-permute-start.11 = (bf16[256,2048]{1,0:T(8,128)(2,1)}, bf16[256,2048]{1,0:T(8,128)(2,1)}, u32[]{:S(2)}, u32[]{:S(2)}) collective-permute-start(bf16[256,2048]{1,0:T(8,128)(2,1)} %bitcast.16.refs_0_.refs_5_), channel_id=1, source_target_pairs={{0,16},{16,0},{1,17},{17,1},{2,18},{18,2},{3,19},{19,3},{4,20},{20... | collective-permute-start | bytes 3145736 | tf_op jit(solution)/shard_map/ppermute | solution.py:75
  107.8 32.2 %collective-permute-start.16 = (bf16[1024,2048]{1,0:T(8,128)(2,1)}, bf16[1024,2048]{1,0:T(8,128)(2,1)}, u32[]{:S(2)}, u32[]{:S(2)}) collective-permute-start(bf16[1024,2048]{1,0:T(8,128)(2,1)} %join.11.near), channel_id=1, source_target_pairs={{0,1},{1,0},{2,3},{3,2},{4,5},{5,4},{6,7},{7,6},{8,9},{9,8},{10,11... | collective-permute-start | bytes 12582920 | tf_op jit(solution)/shard_map/ppermute | solution.py:75
  132.2 34.9 %collective-permute-start.23 = (bf16[512,768]{1,0:T(8,128)(2,1)S(1)}, bf16[512,768]{1,0:T(8,128)(2,1)S(1)}, u32[]{:S(2)}, u32[]{:S(2)}) collective-permute-start(bf16[512,768]{1,0:T(8,128)(2,1)S(1)} %copy-done.54), channel_id=1, source_target_pairs={{0,4},{4,12},{12,8},{8,0},{1,5},{5,13},{13,9},{9,1},{2,6},{6,14},{... | collective-permute-start | bytes 2359304 | tf_op jit(solution)/shard_map/ppermute | solution.py:110
  172.8 33.8 %collective-permute-start.30 = (bf16[256,2048]{1,0:T(8,128)(2,1)}, bf16[256,2048]{1,0:T(8,128)(2,1)S(1)}, u32[]{:S(2)}, u32[]{:S(2)}) collective-permute-start(bf16[256,2048]{1,0:T(8,128)(2,1)} %bitcast.19.refs_0_.refs_4_), channel_id=1, source_target_pairs={{0,16},{16,0},{1,17},{17,1},{2,18},{18,2},{3,19},{19,3},{4,20},{20... | collective-permute-start | bytes 3145736 | tf_op jit(solution)/shard_map/ppermute | solution.py:75
  173.6 33.5 %collective-permute-start.31 = (bf16[256,2048]{1,0:T(8,128)(2,1)}, bf16[256,2048]{1,0:T(8,128)(2,1)S(1)}, u32[]{:S(2)}, u32[]{:S(2)}) collective-permute-start(bf16[256,2048]{1,0:T(8,128)(2,1)} %bitcast.19.refs_0_.refs_4_), channel_id=1, source_target_pairs={{0,2},{2,0},{1,3},{3,1},{4,6},{6,4},{5,7},{7,5},{8,10},{10,8},{9,1... | collective-permute-start | bytes 3145736 | tf_op jit(solution)/shard_map/ppermute | solution.py:75
  236.4 30.1 %collective-permute-start.36 = (bf16[1024,2048]{1,0:T(8,128)(2,1)}, bf16[1024,2048]{1,0:T(8,128)(2,1)S(1)}, u32[]{:S(2)}, u32[]{:S(2)}) collective-permute-start(bf16[1024,2048]{1,0:T(8,128)(2,1)} %join.13.near.refs_0_), channel_id=1, source_target_pairs={{0,1},{1,0},{2,3},{3,2},{4,5},{5,4},{6,7},{7,6},{8,9},{9,8},{10,11... | collective-permute-start | bytes 12582920 | tf_op jit(solution)/shard_map/ppermute | solution.py:75
  239.6 46.8 %collective-permute-start.41 = (bf16[512,640]{1,0:T(8,128)(2,1)S(1)}, bf16[512,640]{1,0:T(8,128)(2,1)}, u32[]{:S(2)}, u32[]{:S(2)}) collective-permute-start(bf16[512,640]{1,0:T(8,128)(2,1)S(1)} %copy-done.66), channel_id=1, source_target_pairs={{0,4},{4,12},{12,8},{8,0},{1,5},{5,13},{13,9},{9,1},{2,6},{6,14},{... | collective-permute-start | bytes 1966088 | tf_op jit(solution)/shard_map/ppermute | solution.py:110
  309.6 32.0 %collective-permute-start.44 = (bf16[512,640]{1,0:T(8,128)(2,1)S(1)}, bf16[512,640]{1,0:T(8,128)(2,1)S(1)}, u32[]{:S(2)}, u32[]{:S(2)}) collective-permute-start(bf16[512,640]{1,0:T(8,128)(2,1)S(1)} %collective-permute-done.43.refs_2_), channel_id=1, source_target_pairs={{0,4},{4,12},{12,8},{8,0},{1,5},{5,13},{13,9},{9,1},{2,6},{6,14},{... | collective-permute-start | bytes 1966088 | tf_op jit(solution)/shard_map/ppermute | solution.py:110
  394.0 39.0 %collective-permute-start.48 = (bf16[256,2048]{1,0:T(8,128)(2,1)}, bf16[256,2048]{1,0:T(8,128)(2,1)S(1)}, u32[]{:S(2)}, u32[]{:S(2)}) collective-permute-start(bf16[256,2048]{1,0:T(8,128)(2,1)} %get-tuple-element.310), channel_id=1, source_target_pairs={{0,16},{16,0},{1,17},{17,1},{2,18},{18,2},{3,19},{19,3},{4,20},{20... | collective-permute-start | bytes 3145736 | tf_op jit(solution)/shard_map/ppermute | solution.py:75
  395.2 37.8 %collective-permute-start.49 = (bf16[256,2048]{1,0:T(8,128)(2,1)}, bf16[256,2048]{1,0:T(8,128)(2,1)S(1)}, u32[]{:S(2)}, u32[]{:S(2)}) collective-permute-start(bf16[256,2048]{1,0:T(8,128)(2,1)} %get-tuple-element.311), channel_id=1, source_target_pairs={{0,2},{2,0},{1,3},{3,1},{4,6},{6,4},{5,7},{7,5},{8,10},{10,8},{9,1... | collective-permute-start | bytes 3145736 | tf_op jit(solution)/shard_map/ppermute | solution.py:75
  396.7 45.6 %collective-permute-start.50 = (bf16[256,2048]{1,0:T(8,128)(2,1)}, bf16[256,2048]{1,0:T(8,128)(2,1)S(1)}, u32[]{:S(2)}, u32[]{:S(2)}) collective-permute-start(bf16[256,2048]{1,0:T(8,128)(2,1)} %get-tuple-element.312), channel_id=1, source_target_pairs={{0,18},{2,16},{16,2},{18,0},{1,19},{3,17},{17,3},{19,1},{4,22},{6,... | collective-permute-start | bytes 3145736 | tf_op jit(solution)/shard_map/ppermute | solution.py:75
  410.2 47.3 %collective-permute-start.51 = (bf16[512,768]{1,0:T(8,128)(2,1)S(1)}, bf16[512,768]{1,0:T(8,128)(2,1)S(1)}, u32[]{:S(2)}, u32[]{:S(2)}) collective-permute-start(bf16[512,768]{1,0:T(8,128)(2,1)S(1)} %add_convert_fusion.2), channel_id=1, source_target_pairs={{0,4},{4,12},{12,8},{8,0},{1,5},{5,13},{13,9},{9,1},{2,6},{6,14},{... | collective-permute-start | bytes 2359304 | tf_op jit(solution)/shard_map/ppermute | solution.py:110
  411.4 54.8 %collective-permute-start.52 = (bf16[512,640]{1,0:T(8,128)(2,1)S(1)}, bf16[512,640]{1,0:T(8,128)(2,1)S(1)}, u32[]{:S(2)}, u32[]{:S(2)}) collective-permute-start(bf16[512,640]{1,0:T(8,128)(2,1)S(1)} %copy-done.68), channel_id=1, source_target_pairs={{0,4},{4,12},{12,8},{8,0},{1,5},{5,13},{13,9},{9,1},{2,6},{6,14},{... | collective-permute-start | bytes 1966088 | tf_op jit(solution)/shard_map/ppermute | solution.py:110
  470.5 44.7 %collective-permute-start.61 = (bf16[4,2048,256]{2,1,0:T(8,128)(2,1)S(1)}, bf16[4,2048,256]{2,1,0:T(8,128)(2,1)}, u32[]{:S(2)}, u32[]{:S(2)}) collective-permute-start(bf16[4,2048,256]{2,1,0:T(8,128)(2,1)S(1)} %copy-done.42), channel_id=1, source_target_pairs={{0,1},{1,0},{2,3},{3,2},{4,5},{5,4},{6,7},{7,6},{8,9},{9,8},{10,11... | collective-permute-start | bytes 12582920 | tf_op jit(solution)/shard_map/ppermute | solution.py:75
  473.3 38.9 %collective-permute-start.60 = (bf16[512,640]{1,0:T(8,128)(2,1)S(1)}, bf16[512,640]{1,0:T(8,128)(2,1)S(1)}, u32[]{:S(2)}, u32[]{:S(2)}) collective-permute-start(bf16[512,640]{1,0:T(8,128)(2,1)S(1)} %add_convert_fusion.9), channel_id=1, source_target_pairs={{0,4},{4,12},{12,8},{8,0},{1,5},{5,13},{13,9},{9,1},{2,6},{6,14},{... | collective-permute-start | bytes 1966088 | tf_op jit(solution)/shard_map/ppermute | solution.py:110
  533.5 44.3 %collective-permute-start.65 = (bf16[2048,256]{1,0:T(8,128)(2,1)}, bf16[2048,256]{1,0:T(8,128)(2,1)S(1)}, u32[]{:S(2)}, u32[]{:S(2)}) collective-permute-start(bf16[2048,256]{1,0:T(8,128)(2,1)} %get-tuple-element.360), channel_id=1, source_target_pairs={{0,16},{16,0},{1,17},{17,1},{2,18},{18,2},{3,19},{19,3},{4,20},{20... | collective-permute-start | bytes 3145736 | tf_op jit(solution)/shard_map/ppermute | solution.py:75
  534.7 43.1 %collective-permute-start.66 = (bf16[2048,256]{1,0:T(8,128)(2,1)}, bf16[2048,256]{1,0:T(8,128)(2,1)S(1)}, u32[]{:S(2)}, u32[]{:S(2)}) collective-permute-start(bf16[2048,256]{1,0:T(8,128)(2,1)} %get-tuple-element.361), channel_id=1, source_target_pairs={{0,2},{2,0},{1,3},{3,1},{4,6},{6,4},{5,7},{7,5},{8,10},{10,8},{9,1... | collective-permute-start | bytes 3145736 | tf_op jit(solution)/shard_map/ppermute | solution.py:75
  536.2 46.5 %collective-permute-start.67 = (bf16[2048,256]{1,0:T(8,128)(2,1)}, bf16[2048,256]{1,0:T(8,128)(2,1)}, u32[]{:S(2)}, u32[]{:S(2)}) collective-permute-start(bf16[2048,256]{1,0:T(8,128)(2,1)} %get-tuple-element.362), channel_id=1, source_target_pairs={{0,18},{2,16},{16,2},{18,0},{1,19},{3,17},{17,3},{19,1},{4,22},{6,... | collective-permute-start | bytes 3145736 | tf_op jit(solution)/shard_map/ppermute | solution.py:75
  550.9 41.3 %collective-permute-start.72 = (bf16[176,2048]{1,0:T(8,128)(2,1)S(1)}, bf16[176,2048]{1,0:T(8,128)(2,1)S(1)}, u32[]{:S(2)}, u32[]{:S(2)}) collective-permute-start(bf16[176,2048]{1,0:T(8,128)(2,1)S(1)} %add_convert_fusion.6), channel_id=1, source_target_pairs={{0,4},{4,12},{12,8},{8,0},{1,5},{5,13},{13,9},{9,1},{2,6},{6,14},{... | collective-permute-start | bytes 2162696 | tf_op jit(solution)/shard_map/ppermute | solution.py:110
  601.7 110.6 %collective-permute-start.79 = (bf16[1024,2048]{1,0:T(8,128)(2,1)}, bf16[1024,2048]{1,0:T(8,128)(2,1)}, u32[]{:S(2)}, u32[]{:S(2)}) collective-permute-start(bf16[1024,2048]{1,0:T(8,128)(2,1)} %back_product.2), channel_id=1, source_target_pairs={{0,1},{1,0},{2,3},{3,2},{4,5},{5,4},{6,7},{7,6},{8,9},{9,8},{10,11... | collective-permute-start | bytes 12582920 | tf_op jit(solution)/shard_map/ppermute | solution.py:75
  628.4 48.8 %collective-permute-start.68 = (bf16[256,2048]{1,0:T(8,128)(2,1)}, bf16[256,2048]{1,0:T(8,128)(2,1)S(1)}, u32[]{:S(2)}, u32[]{:S(2)}) collective-permute-start(bf16[256,2048]{1,0:T(8,128)(2,1)} %get-tuple-element.363), channel_id=1, source_target_pairs={{0,16},{16,0},{1,17},{17,1},{2,18},{18,2},{3,19},{19,3},{4,20},{20... | collective-permute-start | bytes 3145736 | tf_op jit(solution)/shard_map/ppermute | solution.py:75
  629.7 49.8 %collective-permute-start.69 = (bf16[256,2048]{1,0:T(8,128)(2,1)S(1)}, bf16[256,2048]{1,0:T(8,128)(2,1)S(1)}, u32[]{:S(2)}, u32[]{:S(2)}) collective-permute-start(bf16[256,2048]{1,0:T(8,128)(2,1)S(1)} %copy-done.47), channel_id=1, source_target_pairs={{0,2},{2,0},{1,3},{3,1},{4,6},{6,4},{5,7},{7,5},{8,10},{10,8},{9,1... | collective-permute-start | bytes 3145736 | tf_op jit(solution)/shard_map/ppermute | solution.py:75
  631.2 49.5 %collective-permute-start.70 = (bf16[256,2048]{1,0:T(8,128)(2,1)S(1)}, bf16[256,2048]{1,0:T(8,128)(2,1)S(1)}, u32[]{:S(2)}, u32[]{:S(2)}) collective-permute-start(bf16[256,2048]{1,0:T(8,128)(2,1)S(1)} %copy-done.46), channel_id=1, source_target_pairs={{0,18},{2,16},{16,2},{18,0},{1,19},{3,17},{17,3},{19,1},{4,22},{6,... | collective-permute-start | bytes 3145736 | tf_op jit(solution)/shard_map/ppermute | solution.py:75
  634.9 87.8 %collective-permute-start.85 = (bf16[512,768]{1,0:T(8,128)(2,1)}, bf16[512,768]{1,0:T(8,128)(2,1)S(1)}, u32[]{:S(2)}, u32[]{:S(2)}) collective-permute-start(bf16[512,768]{1,0:T(8,128)(2,1)} %join.15.refs_0_), channel_id=1, source_target_pairs={{0,16},{16,0},{1,17},{17,1},{2,18},{18,2},{3,19},{19,3},{4,20},{20... | collective-permute-start | bytes 2359304 | tf_op jit(solution)/shard_map/ppermute | solution.py:75
  677.2 45.4 %collective-permute-start.84 = (bf16[512,256]{1,0:T(8,128)(2,1)}, bf16[512,256]{1,0:T(8,128)(2,1)S(1)}, u32[]{:S(2)}, u32[]{:S(2)}) collective-permute-start(bf16[512,256]{1,0:T(8,128)(2,1)} %get-tuple-element.381), channel_id=1, source_target_pairs={{0,4},{4,12},{12,8},{8,0},{1,5},{5,13},{13,9},{9,1},{2,6},{6,14},{... | collective-permute-start | bytes 786440 | tf_op jit(solution)/shard_map/ppermute | solution.py:110
  679.5 30.0 %collective-permute-start.103 = (bf16[172,2048]{1,0:T(8,128)(2,1)S(1)}, bf16[172,2048]{1,0:T(8,128)(2,1)S(1)}, u32[]{:S(2)}, u32[]{:S(2)}) collective-permute-start(bf16[172,2048]{1,0:T(8,128)(2,1)S(1)} %get-tuple-element.434), channel_id=1, source_target_pairs={{0,16},{16,0},{1,17},{17,1},{2,18},{18,2},{3,19},{19,3},{4,20},{20... | collective-permute-start | bytes 2113544 | tf_op jit(solution)/shard_map/ppermute | solution.py:75
  690.4 32.3 %collective-permute-start.86 = (bf16[512,640]{1,0:T(8,128)(2,1)S(1)}, bf16[512,640]{1,0:T(8,128)(2,1)S(1)}, u32[]{:S(2)}, u32[]{:S(2)}) collective-permute-start(bf16[512,640]{1,0:T(8,128)(2,1)S(1)} %copy-done.67), channel_id=1, source_target_pairs={{0,16},{16,0},{1,17},{17,1},{2,18},{18,2},{3,19},{19,3},{4,20},{20... | collective-permute-start | bytes 1966088 | tf_op jit(solution)/shard_map/ppermute | solution.py:75
  737.6 49.5 %collective-permute-start.80 = (bf16[256,2048]{1,0:T(8,128)(2,1)}, bf16[256,2048]{1,0:T(8,128)(2,1)S(1)}, u32[]{:S(2)}, u32[]{:S(2)}) collective-permute-start(bf16[256,2048]{1,0:T(8,128)(2,1)} %get-tuple-element.392), channel_id=1, source_target_pairs={{0,16},{16,0},{1,17},{17,1},{2,18},{18,2},{3,19},{19,3},{4,20},{20... | collective-permute-start | bytes 3145736 | tf_op jit(solution)/shard_map/ppermute | solution.py:75
  738.8 48.7 %collective-permute-start.81 = (bf16[256,2048]{1,0:T(8,128)(2,1)}, bf16[256,2048]{1,0:T(8,128)(2,1)S(1)}, u32[]{:S(2)}, u32[]{:S(2)}) collective-permute-start(bf16[256,2048]{1,0:T(8,128)(2,1)} %get-tuple-element.393), channel_id=1, source_target_pairs={{0,2},{2,0},{1,3},{3,1},{4,6},{6,4},{5,7},{7,5},{8,10},{10,8},{9,1... | collective-permute-start | bytes 3145736 | tf_op jit(solution)/shard_map/ppermute | solution.py:75
  739.3 49.3 %collective-permute-start.82 = (bf16[256,2048]{1,0:T(8,128)(2,1)}, bf16[256,2048]{1,0:T(8,128)(2,1)S(1)}, u32[]{:S(2)}, u32[]{:S(2)}) collective-permute-start(bf16[256,2048]{1,0:T(8,128)(2,1)} %get-tuple-element.394), channel_id=1, source_target_pairs={{0,18},{2,16},{16,2},{18,0},{1,19},{3,17},{17,3},{19,1},{4,22},{6,... | collective-permute-start | bytes 3145736 | tf_op jit(solution)/shard_map/ppermute | solution.py:75
  749.9 42.1 %collective-permute-start.93 = (bf16[512,384]{1,0:T(8,128)(2,1)S(1)}, bf16[512,384]{1,0:T(8,128)(2,1)S(1)}, u32[]{:S(2)}, u32[]{:S(2)}) collective-permute-start(bf16[512,384]{1,0:T(8,128)(2,1)S(1)} %add_convert_fusion.11), channel_id=1, source_target_pairs={{0,4},{4,12},{12,8},{8,0},{1,5},{5,13},{13,9},{9,1},{2,6},{6,14},{... | collective-permute-start | bytes 1179656 | tf_op jit(solution)/shard_map/ppermute | solution.py:110
  752.7 32.9 %collective-permute-start.92 = (bf16[128,384]{1,0:T(8,128)(2,1)}, bf16[128,384]{1,0:T(8,128)(2,1)S(1)}, u32[]{:S(2)}, u32[]{:S(2)}) collective-permute-start(bf16[128,384]{1,0:T(8,128)(2,1)} %get-tuple-element.442), channel_id=1, source_target_pairs={{0,3},{1,2},{2,1},{3,0},{4,7},{5,6},{6,5},{7,4},{8,11},{9,10},{10,... | collective-permute-start | bytes 294920 | tf_op jit(solution)/shard_map/ppermute | solution.py:75
  (177 other events, 2229.7 us)
